TPU v7x, 32 devices: a whole 2x2x4 slice. The times are simulated.
32 devices in a mesh: fsdp: 32 (over z, y, x, core).
Axes of the slice: x: 2, y: 2, z: 4, core: 2. Of those that a mesh axis runs over, the one named last changes fastest.
Arguments:
- tokens: bfloat16 [32, 128, 2048], P(None, 'fsdp'), may hold values from -6 to 6
- lengths: int32 [32], replicated, may hold values from 1 to 128, 2457 in all
- permutation: int32 [32], replicated, may hold values from 0 to 31, each once
- query_weight: bfloat16 [2048, 2048], P('fsdp'), may hold values from -0.015625 to 0.015625
- key_weight: bfloat16 [2048, 2048], P('fsdp'), may hold values from -0.125 to 0.125
- value_weight: bfloat16 [2048, 2048], P('fsdp'), may hold values from -0.125 to 0.125
- out_weight: bfloat16 [2048, 2048], P('fsdp'), may hold values from -1 to 1
- gate_weight: bfloat16 [2048, 5120], P('fsdp'), may hold values from -0.125 to 0.125
- up_weight: bfloat16 [2048, 5120], P('fsdp'), may hold values from -0.125 to 0.125
- down_weight: bfloat16 [5120, 2048], P('fsdp'), may hold values from -0.125 to 0.125
- gain_attention: bfloat16 [2048], P('fsdp'), may hold values from 0.25 to 1.75
- gain_feedforward: bfloat16 [2048], P('fsdp'), may hold values from 0.25 to 1.75
- bias_table: bfloat16 [1024], P('fsdp'), may hold values from -5 to 5
- cotangent: bfloat16 [32, 128, 2048], P('fsdp'), may hold values from -6 to 6
Outputs:
- layer_output: bfloat16 [32, 128, 2048], P('fsdp')
- tokens_grad: bfloat16 [32, 128, 2048], P(None, 'fsdp')
- query_grad: float32 [2048, 2048], P('fsdp')
- key_grad: float32 [2048, 2048], P('fsdp')
- value_grad: float32 [2048, 2048], P('fsdp')
- out_grad: float32 [2048, 2048], P('fsdp')
- gate_grad: float32 [2048, 5120], P('fsdp')
- up_grad: float32 [2048, 5120], P('fsdp')
- down_grad: float32 [5120, 2048], P('fsdp')
- gain_attention_grad: float32 [2048], P('fsdp')
- gain_feedforward_grad: float32 [2048], P('fsdp')
- table_grad: float32 [1024], P('fsdp')
Inputs may be any that keep to these rules, and one draw needn't show every extreme that they name: The lengths sum to 2457 and at least one sequence has exactly 128 tokens. `permutation`: every sequence number appears exactly once.
All inputs are finite; a program needn't handle non-finite values.
Results may differ from a plain program's by a relative error of at most 0.015.
Values may be sent and summed in bfloat16 or wider, within the bound.
A program may use at most 768 MiB of HBM per device.

v0:
```python
import jax
import jax.numpy as jnp
from jax import lax
from jax.sharding import PartitionSpec as P

HEADS = 32
HEAD_DIM = 64
BUCKETS = 32


EPSILON = 1e-06
masked_score = -1000000000.0
HIGHEST = lax.Precision.HIGHEST


def bucket_index(relative):
    half_buckets = BUCKETS // 2
    exact_count = half_buckets // 2
    distance = jnp.abs(relative)
    side_offset = jnp.where(relative > 0, half_buckets, 0).astype(jnp.int32)
    square = distance * distance
    far_bucket = jnp.full_like(distance, exact_count)
    for doubling in range(1, half_buckets - exact_count):
        far_bucket = far_bucket + (square >= exact_count * exact_count * 2**doubling).astype(
            jnp.int32
        )
    return side_offset + jnp.where(distance < exact_count, distance, far_bucket)


def bucket_onehot(seq_len):
    positions = jnp.arange(seq_len, dtype=jnp.int32)
    relative = (positions[None, :] - positions[:, None]).reshape(-1)
    bucket_ids = jnp.arange(BUCKETS, dtype=jnp.int32)
    return (bucket_index(relative)[None, :] == bucket_ids[:, None]).astype(jnp.float32)


def norm_scale(values):
    return lax.rsqrt(jnp.mean(values * values, axis=-1, keepdims=True) + EPSILON)


def norm_back(values, scale, gain_vec, d_norm):
    weighted = gain_vec * d_norm
    return scale * weighted - values * (scale * scale * scale) * jnp.mean(
        weighted * values, axis=-1, keepdims=True
    )


def rows_product(left, right):
    return lax.dot_general(
        left, right, (((0,), (0,)), ((), ())), preferred_element_type=jnp.float32
    )


def against_rows(left, right):
    return lax.dot_general(
        left, right, (((1,), (1,)), ((), ())), preferred_element_type=jnp.float32
    )


def masked_scores(query_heads, key_heads, rel_bias, length):
    scores = (
        jnp.einsum("qhd,khd->hqk", query_heads, key_heads, preferred_element_type=jnp.float32)
        + rel_bias
    )
    key_valid = jnp.arange(key_heads.shape[0], dtype=jnp.int32) < length
    return jnp.where(key_valid[None, None, :], scores, masked_score)


def unpack_weights(full_weights, onehot, seq_len):
    table_full = full_weights[4].astype(jnp.float32).reshape(BUCKETS, HEADS)
    rel_bias = jnp.dot(table_full.T, onehot, precision=HIGHEST).reshape(HEADS, seq_len, seq_len)
    return (
        full_weights[0],
        full_weights[1],
        full_weights[2].astype(jnp.float32),
        full_weights[3].astype(jnp.float32),
        rel_bias,
    )


def body(
    tokens,
    lengths,
    permutation,
    query_weight,
    key_weight,
    value_weight,
    out_weight,
    gate_weight,
    up_weight,
    down_weight,
    gain_attention,
    gain_feedforward,
    bias_table,
    cotangent,
):
    model_width = query_weight.shape[1]
    hidden_width = gate_weight.shape[1]
    packed = jnp.concatenate(
        (query_weight, key_weight, value_weight, out_weight, gate_weight, up_weight), axis=1
    )
    shards = (packed, down_weight, gain_attention, gain_feedforward, bias_table)
    full_weights = (
        lax.all_gather(shards[0], "fsdp", axis=0, tiled=True),
        lax.all_gather(shards[1], "fsdp", axis=0, tiled=True),
        lax.all_gather(shards[2], "fsdp", axis=0, tiled=True),
        lax.all_gather(shards[3], "fsdp", axis=0, tiled=True),
        lax.all_gather(shards[4], "fsdp", axis=0, tiled=True),
    )
    reordered = tokens[permutation]
    dealt = lax.all_to_all(reordered, "fsdp", split_axis=0, concat_axis=1, tiled=True)
    seq_count = dealt.shape[0]
    seq_len = dealt.shape[1]
    local_ids = lax.dynamic_slice_in_dim(permutation, lax.axis_index("fsdp") * seq_count, seq_count)
    seq_lengths = lengths[local_ids]
    positions = jnp.arange(seq_len, dtype=jnp.int32)
    row_valid = (positions[None, :] < seq_lengths[:, None]).astype(jnp.float32).reshape(-1, 1)
    onehot = bucket_onehot(seq_len)
    onehot_low = onehot.astype(jnp.bfloat16)
    full_packed, full_down, gain_one, gain_two, rel_bias = unpack_weights(
        full_weights, onehot, seq_len
    )
    head_shape = (seq_count, seq_len, HEADS, HEAD_DIM)
    rows_in = dealt.reshape(-1, model_width).astype(jnp.float32)
    scale_one = norm_scale(rows_in)
    normed = (rows_in * scale_one * gain_one).astype(jnp.bfloat16)
    projected = jnp.dot(
        normed, full_packed[:, : 3 * model_width], preferred_element_type=jnp.float32
    ).astype(jnp.bfloat16)
    query_heads = projected[:, :model_width].reshape(head_shape)
    key_heads = projected[:, model_width : 2 * model_width].reshape(head_shape)
    value_heads = projected[:, 2 * model_width :].reshape(head_shape)

    def attend_forward(pieces):
        query_one, key_one, value_one, length = pieces
        scores = masked_scores(query_one, key_one, rel_bias, length)
        row_max = jnp.max(scores, axis=-1, keepdims=True)
        exp_total = jnp.sum(jnp.exp(scores - row_max), axis=-1, keepdims=True)
        log_total = row_max + jnp.log(exp_total)
        weights_soft = jnp.exp(scores - log_total).astype(jnp.bfloat16)
        attended_one = jnp.einsum(
            "hqk,khd->qhd", weights_soft, value_one, preferred_element_type=jnp.float32
        )
        return (attended_one.astype(jnp.bfloat16), log_total)

    attended_heads, log_totals = lax.map(
        attend_forward, (query_heads, key_heads, value_heads, seq_lengths)
    )
    attended_rows = attended_heads.reshape(-1, model_width)
    middle = rows_in + jnp.dot(
        attended_rows,
        full_packed[:, 3 * model_width : 4 * model_width],
        preferred_element_type=jnp.float32,
    )
    scale_two = norm_scale(middle)
    normed_two = (middle * scale_two * gain_two).astype(jnp.bfloat16)
    gate_up = jnp.dot(
        normed_two, full_packed[:, 4 * model_width :], preferred_element_type=jnp.float32
    )

    def gelu_product(gate_part, up_part):
        return jax.nn.gelu(gate_part, approximate=True) * up_part

    hidden_full, gelu_pull = jax.vjp(
        gelu_product, gate_up[:, :hidden_width], gate_up[:, hidden_width:]
    )
    hidden = hidden_full.astype(jnp.bfloat16)
    result = middle + jnp.dot(hidden, full_down, preferred_element_type=jnp.float32)
    layer_output = (
        (result * row_valid).astype(jnp.bfloat16).reshape(seq_count, seq_len, model_width)
    )
    full_weights = (
        lax.all_gather(shards[0], "fsdp", axis=0, tiled=True),
        lax.all_gather(shards[1], "fsdp", axis=0, tiled=True),
        lax.all_gather(shards[2], "fsdp", axis=0, tiled=True),
        lax.all_gather(shards[3], "fsdp", axis=0, tiled=True),
        lax.all_gather(shards[4], "fsdp", axis=0, tiled=True),
    )
    full_packed, full_down, gain_one, gain_two, rel_bias = unpack_weights(
        full_weights, onehot, seq_len
    )
    upstream = cotangent.reshape(-1, model_width).astype(jnp.float32) * row_valid
    upstream_low = upstream.astype(jnp.bfloat16)
    d_hidden = against_rows(upstream_low, full_down)
    d_gate, d_up = gelu_pull(d_hidden)
    d_gate_up = jnp.concatenate((d_gate, d_up), axis=1).astype(jnp.bfloat16)
    d_normed_two = against_rows(d_gate_up, full_packed[:, 4 * model_width :])
    gain_two_grad = jnp.sum(d_normed_two * middle * scale_two, axis=0)
    d_middle = upstream + norm_back(middle, scale_two, gain_two, d_normed_two)
    d_branch = d_middle.astype(jnp.bfloat16)
    d_attended = against_rows(d_branch, full_packed[:, 3 * model_width : 4 * model_width]).astype(
        jnp.bfloat16
    )

    def attend_backward(pieces):
        query_one, key_one, value_one, length, log_total, d_attended_one = pieces
        scores = masked_scores(query_one, key_one, rel_bias, length)
        probs = jnp.exp(scores - log_total)
        probs_low = probs.astype(jnp.bfloat16)
        d_value = jnp.einsum(
            "hqk,qhd->khd", probs_low, d_attended_one, preferred_element_type=jnp.float32
        )
        d_probs = jnp.einsum(
            "qhd,khd->hqk", d_attended_one, value_one, preferred_element_type=jnp.float32
        )
        inner = jnp.sum(probs * d_probs, axis=-1, keepdims=True)
        d_scores = (probs * (d_probs - inner)).astype(jnp.bfloat16)
        d_query = jnp.einsum("hqk,khd->qhd", d_scores, key_one, preferred_element_type=jnp.float32)
        d_key = jnp.einsum("hqk,qhd->khd", d_scores, query_one, preferred_element_type=jnp.float32)
        d_bias = against_rows(d_scores.reshape(HEADS, -1), onehot_low)
        return (
            (
                d_query.astype(jnp.bfloat16),
                d_key.astype(jnp.bfloat16),
                d_value.astype(jnp.bfloat16),
            ),
            d_bias,
        )

    (d_query_all, d_key_all, d_value_all), d_bias_all = lax.map(
        attend_backward,
        (
            query_heads,
            key_heads,
            value_heads,
            seq_lengths,
            log_totals,
            d_attended.reshape(head_shape),
        ),
    )
    d_qkv = jnp.concatenate(
        (
            d_query_all.reshape(-1, model_width),
            d_key_all.reshape(-1, model_width),
            d_value_all.reshape(-1, model_width),
        ),
        axis=1,
    )
    d_normed = against_rows(d_qkv, full_packed[:, : 3 * model_width])
    gain_one_grad = jnp.sum(d_normed * rows_in * scale_one, axis=0)
    d_rows = d_middle + norm_back(rows_in, scale_one, gain_one, d_normed)
    d_dealt = d_rows.astype(jnp.bfloat16).reshape(seq_count, seq_len, model_width)
    returned_rows = lax.all_to_all(d_dealt, "fsdp", split_axis=1, concat_axis=0, tiled=True)
    tokens_grad = returned_rows[jnp.argsort(permutation)]
    packed_grad = lax.psum_scatter(
        jnp.concatenate(
            (
                rows_product(normed, d_qkv),
                jnp.concatenate(
                    (rows_product(attended_rows, d_branch), rows_product(normed_two, d_gate_up)),
                    axis=1,
                ),
            ),
            axis=1,
        ),
        "fsdp",
        scatter_dimension=0,
        tiled=True,
    )
    mixer_grad = packed_grad[:, : 3 * model_width]
    branch_grad = packed_grad[:, 3 * model_width :]
    down_grad = lax.psum_scatter(
        rows_product(hidden, upstream_low), "fsdp", scatter_dimension=0, tiled=True
    )
    table_sum = jnp.sum(d_bias_all, axis=0).T.reshape(-1)
    gain_attention_grad, gain_feedforward_grad, table_grad = (
        lax.psum_scatter(gain_one_grad, "fsdp", scatter_dimension=0, tiled=True),
        lax.psum_scatter(gain_two_grad, "fsdp", scatter_dimension=0, tiled=True),
        lax.psum_scatter(table_sum, "fsdp", scatter_dimension=0, tiled=True),
    )
    return (
        layer_output,
        tokens_grad,
        mixer_grad[:, :model_width],
        mixer_grad[:, model_width : 2 * model_width],
        mixer_grad[:, 2 * model_width :],
        branch_grad[:, :model_width],
        branch_grad[:, model_width : model_width + hidden_width],
        branch_grad[:, model_width + hidden_width :],
        down_grad,
        gain_attention_grad,
        gain_feedforward_grad,
        table_grad,
    )


def solution(mesh):
    placed = (
        P(None, "fsdp", None),
        P(),
        P(),
        P("fsdp", None),
        P("fsdp", None),
        P("fsdp", None),
        P("fsdp", None),
        P("fsdp", None),
        P("fsdp", None),
        P("fsdp", None),
        P("fsdp"),
        P("fsdp"),
        P("fsdp"),
        P("fsdp", None, None),
    )
    return jax.shard_map(
        body,
        mesh=mesh,
        in_specs=placed,
        out_specs=(
            P("fsdp", None, None),
            P(None, "fsdp", None),
            P("fsdp", None),
            P("fsdp", None),
            P("fsdp", None),
            P("fsdp", None),
            P("fsdp", None),
            P("fsdp", None),
            P("fsdp", None),
            P("fsdp"),
            P("fsdp"),
            P("fsdp"),
        ),
        check_vma=False,
    )
```

profile of v0, /device:TPU:29, one launch (start us, length us, event | category | flops | bytes accessed | tf_op | source)
XLA Modules:
  0.0 2487.6 jit_solution(4945955838257978550)
XLA Ops:
  16.5 6.2 all-to-all-start
  25.3 42.7 %all-reduce.7 = (bf16[2048]{0:T(1024)(128)(2,1)S(1)}, bf16[1024]{0:T(1024)(128)(2,1)S(1)}, bf16[2048]{0:T(1024)(128)(2,1)S(1)}) all-reduce(bf16[2048]{0:T(1024)(128)(2,1)S(1)} %dynamic-update-slice.1, bf16[1024]{0:T(1024)(128)(2,1)S(1)} %dynamic-update-slice.2, bf16[2048]{0:T(1024)(128)(2,1)S(1)} %dynamic-update-slice.3), channel_id=1, replica_groups=mesh['fsdp'=32] {'fsdp'}, use_global_device_ids=true, to_apply=%add | all-reduce | flops 5120 | bytes 20480
  74.7 343.2 %all-gather.3.cloned.1.call-done = bf16[2048,18432]{1,0:T(8,128)(2,1)} async-done(((bf16[64,18432]{1,0:T(8,128)(2,1)}), bf16[2048,18432]{1,0:T(8,128)(2,1)}) %all-gather.3.cloned.1.call-update) | async-done | bytes 75497488 | tf_op jit(solution)/shard_map/all_gather | solution.py:104
  417.9 10.3 fusion.12
  433.8 4.8 multiply_reduce_fusion.5
  439.6 17.3 fusion.2
  456.9 96.6 %all-gather.5.cloned.1.call-done = bf16[5120,2048]{1,0:T(8,128)(2,1)} async-done(((bf16[160,2048]{1,0:T(8,128)(2,1)}), bf16[5120,2048]{1,0:T(8,128)(2,1)}) %all-gather.5.cloned.1.call-update) | async-done | bytes 20971536 | tf_op jit(solution)/shard_map/all_gather | solution.py:105
  553.5 15.3 fusion.21
  568.8 21.4 multiply_reduce_fusion.1
  592.8 7.1 fusion.26
  608.5 8.1 fusion.46
  616.6 30.7 %fusion.32 = f32[2048,10240]{1,0:T(8,128)} fusion(bf16[128,5120]{1,0:T(8,128)(2,1)} %get-tuple-element.99, bf16[128,5120]{1,0:T(8,128)(2,1)} %get-tuple-element.98, f32[128,2048]{1,0:T(8,128)S(1)} %copy-done.8, f32[2048]{0:T(1024)S(1)} %convert_element_type.228, f32[128]{0:T(128)S(1)} %get-tuple-element.111), kind=kOutput, calls=%fused_computation.43 | convolution fusion | flops 5374738432 | bytes 87564800 | tf_op jit(solution)/shard_map/dot_general | solution.py:49
  647.3 20.7 fusion.42
  668.0 98.5 %pad_maximum_fusion = f32[2048,18432]{1,0:T(8,128)} fusion(f32[2048,10240]{1,0:T(8,128)} %fusion.32, f32[2048,2048]{1,0:T(8,128)} %fusion.46, f32[2048,6144]{1,0:T(8,128)} %fusion.42), kind=kLoop, calls=%fused_computation.2 | loop fusion | flops 75497472 | bytes 301989888 | tf_op jit(solution)/shard_map/concatenate | solution.py:246
  767.9 22.9 fusion.49
  796.7 17.5 multiply_reduce_fusion.2
  814.2 39.6 %all-reduce.6 = (f32[2048]{0:T(1024)S(1)}, f32[2048]{0:T(1024)S(1)}, f32[1024]{0:T(1024)S(1)}) all-reduce(f32[2048]{0:T(1024)S(1)} %get-tuple-element.90, f32[2048]{0:T(1024)S(1)} %copy-done.35, f32[1024]{0:T(1024)S(1)} %reshape.251), channel_id=4, replica_groups=mesh['fsdp'=32] {'fsdp'}, use_global_device_ids=true, to_apply=%region_11.12.clone | all-reduce | flops 5120 | bytes 40960
  859.0 5.0 reduce.6
  865.2 6.9 all-to-all-start.1
  872.7 13.7 fusion.30
  887.0 3.0 bitcast_reduce_fusion
  891.9 1137.2 %reduce-scatter.3.cloned.1.call-done = f32[64,18432]{1,0:T(8,128)} async-done(((f32[2048,18432]{1,0:T(8,128)}), f32[64,18432]{1,0:T(8,128)}) %reduce-scatter.3.cloned.1.call-update) | async-done | bytes 4718608 | tf_op jit(solution)/shard_map/reduce_scatter | solution.py:245
  2032.0 3.5 fusion.68
  2035.5 445.2 %reduce-scatter.5.cloned.1.call-done = f32[160,2048]{1,0:T(8,128)} async-done(((f32[5120,2048]{1,0:T(8,128)}), f32[160,2048]{1,0:T(8,128)}) %reduce-scatter.5.cloned.1.call-update) | async-done | bytes 1310736 | tf_op jit(solution)/shard_map/reduce_scatter | solution.py:262
  (165 shorter events, 53.6 us)
Async XLA Ops:
  7.2 410.7 %all-gather.3.cloned.1.call-start = ((), (), s32[]{:S(2)}) async-start(), calls=%async_computation.4 | async-start | bytes 77856768 | tf_op jit(solution)/shard_map/all_gather | solution.py:104
  12.5 12.1 copy-start.38
  12.5 12.4 copy-start.39
  12.5 12.6 copy-start.40
  13.9 539.6 %all-gather.5.cloned.1.call-start = ((), (), s32[]{:S(2)}) async-start(), calls=%async_computation.5 | async-start | bytes 21626880 | tf_op jit(solution)/shard_map/all_gather | solution.py:105
  16.5 57.7 %all-to-all-start = ((bf16[32,4,2048]{2,1,0:T(4,128)(2,1)}), bf16[32,4,2048]{2,1,0:T(4,128)(2,1)S(1)}, u32[]{:S(2)}, u32[]{:S(2)}) async-start(bf16[32,4,2048]{2,1,0:T(4,128)(2,1)} %gather_fusion), calls=%async_computation | async-start | bytes 1048576 | tf_op jit(solution)/shard_map/all_to_all | solution.py:111
  22.6 2006.5 %reduce-scatter.3.cloned.1.call-start = ((), (), s32[]{:S(2)}) async-start(), calls=%async_computation.6 | async-start | bytes 155713536 | tf_op jit(solution)/shard_map/reduce_scatter | solution.py:245
  68.0 579.2 %copy-start.29 = (f32[2048]{0:T(1024)}, f32[2048]{0:T(1024)S(1)}, u32[]{:S(2)}) copy-start(f32[2048]{0:T(1024)S(1)} %convert_element_type.208) | copy-start | bytes 24580
  73.5 516.7 %copy-start.36 = (f32[128]{0:T(128)}, f32[128]{0:T(128)S(1)}, u32[]{:S(2)}) copy-start(f32[128]{0:T(128)S(1)} %fusion.67) | copy-start | bytes 1540
  74.6 572.7 %copy-start.33 = (f32[128]{0:T(128)}, f32[128]{0:T(128)S(1)}, u32[]{:S(2)}) copy-start(f32[128]{0:T(128)S(1)} %rsqrt.26) | copy-start | bytes 1540
  74.7 353.6 %copy-start.2 = (f32[128,2048]{1,0:T(8,128)}, f32[128,2048]{1,0:T(8,128)S(1)}, u32[]{:S(2)}) copy-start(f32[128,2048]{1,0:T(8,128)S(1)} %reshape.272) | copy-start | bytes 3145732
  568.8 21.4 copy-start.7
  568.8 21.4 copy-start.22
  607.3 40.0 %copy-start.26 = (bf16[32,64,128]{2,1,0:T(8,128)(2,1)}, bf16[32,64,128]{2,1,0:T(8,128)(2,1)S(1)}, u32[]{:S(2)}) copy-start(bf16[32,64,128]{2,1,0:T(8,128)(2,1)S(1)} %convolution_convert_fusion.1) | copy-start | bytes 1572868
  608.5 8.1 copy-start.8
  616.6 30.7 %copy-start.4 = (f32[128,2048]{1,0:T(8,128)S(1)}, f32[128,2048]{1,0:T(8,128)}, u32[]{:S(2)}) copy-start(f32[128,2048]{1,0:T(8,128)} %copy-done.2) | copy-start | bytes 3145732
  616.6 30.7 %copy-start.24 = (bf16[32,64,128]{2,1,0:T(8,128)(2,1)S(1)}, bf16[32,64,128]{2,1,0:T(8,128)(2,1)}, u32[]{:S(2)}) copy-start(bf16[32,64,128]{2,1,0:T(8,128)(2,1)} %convolution_convert_fusion) | copy-start | bytes 1572868
  766.5 1714.1 %reduce-scatter.5.cloned.1.call-start = ((), (), s32[]{:S(2)}) async-start(), calls=%async_computation.7 | async-start | bytes 43253760 | tf_op jit(solution)/shard_map/reduce_scatter | solution.py:262
  796.7 17.5 copy-start.35
  796.7 58.3 %copy-start.14 = (f32[128,2048]{1,0:T(8,128)S(1)}, f32[128,2048]{1,0:T(8,128)}, u32[]{:S(2)}) copy-start(f32[128,2048]{1,0:T(8,128)} %copy-done.12) | copy-start | bytes 3145732
  856.7 16.0 copy-start.9
  856.7 16.0 copy-start.16
  865.2 21.3 all-to-all-start.1
  2029.1 451.6 %copy-start.1 = (bf16[32,4,2048]{2,1,0:T(4,128)(2,1)S(1)}, bf16[32,4,2048]{2,1,0:T(4,128)(2,1)}, u32[]{:S(2)}) copy-start(bf16[32,4,2048]{2,1,0:T(4,128)(2,1)} %param.14) | copy-start | bytes 1572868
  (26 other events, 72.9 us)
Sparse Core Ops, SparseCore 0:
  14.0 403.8 all-gather.2
  420.8 132.6 all-gather.4
  766.7 1262.3 reduce-scatter.2
  2031.9 448.6 reduce-scatter.4
where the time goes:
time: 2500 us; the launch traced here: 2490 us
  waiting for transfers between devices  2020 us (81%)
  matrix products  201 us (8%)
  other arithmetic  111 us (4%)
  blocking collectives  82.3 us (3%)
  local copies, waits for them, and re-layouts  40.5 us (2%)
    reduce_scatter x1, waiting for transfers between devices, body(): lax.psum_scatter(jnp.concatenate((rows_product(normed, d_qkv), jnp.concat...  1140 us
    reduce_scatter x1, waiting for transfers between devices, body(): lax.psum_scatter(rows_product(hidden, upstream_low), 'fsdp', scatter_dime...  445 us
    all_gather x1, waiting for transfers between devices, body(): lax.all_gather(shards[0], 'fsdp', axis=0, tiled=True)  343 us
    concatenate x1, other arithmetic, body(): jnp.concatenate((rows_product(normed, d_qkv), jnp.concatenate((rows_produ...  98.5 us
    all_gather x1, waiting for transfers between devices, body(): lax.all_gather(shards[1], 'fsdp', axis=0, tiled=True)  96.6 us
    unnamed x2, blocking collectives  82.3 us
    dot_general x4, matrix products, rows_product(): lax.dot_general(left, right, (((0,), (0,)), ((), ())), preferred_element_...  82.3 us
    dot_general x5, matrix products, against_rows(): lax.dot_general(left, right, (((1,), (1,)), ((), ())), preferred_element_...  63.3 us
  transfers between devices with their start and end apart: 6, of which 4 were waited for; matrix products, arithmetic and copies ran while one was open for 5% of the time, Pallas kernels for 0%

commit v1 on v0

--- a/solution.py
+++ b/solution.py
@@ -1,6 +1,10 @@
+import functools
+
 import jax
 import jax.numpy as jnp
 from jax import lax
+from jax.experimental import pallas as pl
+from jax.experimental.pallas import tpu as pltpu
 from jax.sharding import PartitionSpec as P
 
 HEADS = 32
@@ -78,7 +82,7 @@
     )
 
 
-def body(
+def body_any(
     tokens,
     lengths,
     permutation,
@@ -284,6 +288,556 @@
     )
 
 
+MESH = pl.DeviceIdType.MESH
+AXIS = "fsdp"
+
+
+def place():
+    me = lax.axis_index(AXIS)
+    c, x, y, z = me % 2, (me // 2) % 2, (me // 4) % 2, me // 8
+    return me, c, x, y, z
+
+
+def greet(nc, nx, ny, n1, n2, mid):
+    bar = pltpu.get_barrier_semaphore()
+    for peer in (nc, nx, ny, n1):
+        pl.semaphore_signal(bar, inc=1, device_id=(peer,), device_id_type=MESH)
+
+    @pl.when(mid)
+    def _():
+        pl.semaphore_signal(bar, inc=1, device_id=(n2,), device_id_type=MESH)
+
+    pl.semaphore_wait(bar, 4 + mid.astype(jnp.int32))
+
+
+def gather_kernel(a_ref, o_ref, own_sem, ssem, rsem):
+    me, c, x, y, z = place()
+    half = a_ref.shape[1] // 2
+    mid = (z == 1) | (z == 2)
+    z1, z2, z3 = z + 1 - 2 * (z % 2), 2 - z // 2, 3 - 3 * (z // 2)
+    nc, nx, ny = me + 1 - 2 * c, me + 2 - 4 * x, me + 4 - 8 * y
+    n1, n2 = me + 8 * (z1 - z), me + 8 * (z2 - z)
+    greet(nc, nx, ny, n1, n2, mid)
+    own = pltpu.make_async_copy(a_ref, o_ref.at[me], own_sem)
+    own.start()
+    cols = (pl.ds(0, half), pl.ds(half, half))
+    sends = []
+    count = [0]
+
+    def push(part, block, peer, mine=False, when=None):
+        k = count[0]
+        count[0] += 1
+        src = a_ref.at[:, cols[part]] if mine else o_ref.at[block, :, cols[part]]
+
+        def copy():
+            return pltpu.make_async_remote_copy(
+                src, o_ref.at[block, :, cols[part]], ssem.at[k], rsem.at[part, block],
+                device_id=(peer,), device_id_type=MESH)
+
+        def start():
+            copy().start()
+
+        def finish():
+            copy().wait_send()
+        if when is None:
+            start()
+        else:
+            pl.when(when)(start)
+        sends.append((finish, when))
+
+    def arrive(part, block):
+        pltpu.make_async_remote_copy(
+            o_ref.at[block, :, cols[part]], o_ref.at[block, :, cols[part]], ssem.at[0],
+            rsem.at[part, block], device_id=(nc,), device_id_type=MESH).wait_recv()
+
+    for part in (0, 1):
+        push(part, me, n1, True)
+        push(part, me, n2, True, mid)
+        push(part, me, (nx, ny)[part], True)
+        push(part, me, (ny, nx)[part], True)
+    for part in (0, 1):
+        push(part, me, nc, True)
+
+    zs = (z, z1, z2, z3)
+    zdel = [8 * (zz - z) for zz in zs]
+
+    def from_z(part, j):
+        b = me + zdel[j]
+        arrive(part, b)
+        push(part, b, n2 if j == 1 else n1, when=mid)
+        push(part, b, (nx, ny)[part])
+        push(part, b, (ny, nx)[part])
+        push(part, b, nc)
+
+    def from_first(part, j):
+        b = (nx, ny)[part] + zdel[j]
+        arrive(part, b)
+        push(part, b, (ny, nx)[part])
+        push(part, b, nc)
+
+    def from_last(part, j, diag):
+        b = (ny, nx)[part] + zdel[j]
+        if diag:
+            b = nx + ny - me + zdel[j]
+        arrive(part, b)
+        push(part, b, nc)
+
+    for j in range(4):
+        if j:
+            for part in (0, 1):
+                from_z(part, j)
+        for part in (0, 1):
+            from_first(part, j)
+        if j:
+            for part in (0, 1):
+                from_last(part, j - 1, False)
+    for part in (0, 1):
+        from_last(part, 3, False)
+    for j in range(4):
+        for part in (0, 1):
+            from_last(part, j, True)
+    for j in range(4):
+        for base in (nc, nc + nx - me, nc + ny - me, nc + nx + ny - 2 * me):
+            for part in (0, 1):
+                arrive(part, base + zdel[j])
+    own.wait()
+    for finish, when in sends:
+        if when is None:
+            finish()
+        else:
+            pl.when(when)(finish)
+
+
+def gather(block, cid=0):
+    rows, width = block.shape
+    n_sends = 10 + 3 * 2 * 4 + 4 * 2 * 2 + 8 * 2
+    return pl.pallas_call(
+        gather_kernel,
+        out_shape=jax.ShapeDtypeStruct((32, rows, width), block.dtype),
+        in_specs=[pl.BlockSpec(memory_space=pl.ANY)],
+        out_specs=pl.BlockSpec(memory_space=pl.ANY),
+        scratch_shapes=[
+            pltpu.SemaphoreType.DMA,
+            pltpu.SemaphoreType.DMA((n_sends,)),
+            pltpu.SemaphoreType.DMA((2, 32)),
+        ],
+        name="gather_rows",
+        compiler_params=pltpu.CompilerParams(collective_id=cid, has_side_effects=True),
+    )(block)
+
+
+def scatter_kernel(p_ref, o_ref, m_ref, s_ref, first_ref, second_ref, za_ref, zb_ref,
+                   lsem, ssem, csem, fsem, gsem, zasem, zbsem):
+    me, c, x, y, z = place()
+    rows, width = o_ref.shape
+    half = width // 2
+    mid = (z == 1) | (z == 2)
+    end = jnp.logical_not(mid)
+    z1, z2, z3 = z + 1 - 2 * (z % 2), 2 - z // 2, 3 - 3 * (z // 2)
+    nc, nx, ny = me + 1 - 2 * c, me + 2 - 4 * x, me + 4 - 8 * y
+    n1, n2 = me + 8 * (z1 - z), me + 8 * (z2 - z)
+    diag = nx + ny - me
+    greet(nc, nx, ny, n1, n2, mid)
+    cols = (pl.ds(0, half), pl.ds(half, half))
+    zs = (z, z1, z2, z3)
+    sends = []
+    count = [0]
+
+    def push(src, dst, rsem, peer, when=None):
+        k = count[0]
+        count[0] += 1
+
+        def copy():
+            return pltpu.make_async_remote_copy(src, dst, ssem.at[k], rsem, device_id=(peer,), device_id_type=MESH)
+        if when is None:
+            copy().start()
+        else:
+            pl.when(when)(lambda: copy().start())
+        sends.append((lambda: copy().wait_send(), when))
+
+    def arrive(dst, rsem):
+        pltpu.make_async_remote_copy(dst, dst, ssem.at[0], rsem, device_id=(nc,), device_id_type=MESH).wait_recv()
+
+    def add_into(dst, src, extra=None):
+        def step(i, _):
+            r = pl.ds(pl.multiple_of(i * 16, 16), 16)
+            v = dst[r, :].astype(jnp.float32) + src[r, :].astype(jnp.float32)
+            if extra is not None:
+                v = v + extra[r, :].astype(jnp.float32)
+            dst[r, :] = v.astype(dst.dtype)
+            return _
+        lax.fori_loop(0, rows // 16, step, 0)
+
+    plane = (me, nx, ny, diag)
+    order = [(q, j) for q in (3, 1, 2, 0) for j in (3, 2, 1, 0)]
+    for q, j in order:
+        b = plane[q] + 8 * (zs[j] - z)
+        slot = q * 4 + zs[j]
+        pltpu.make_async_copy(p_ref.at[b], m_ref.at[slot], lsem.at[slot]).start()
+        push(p_ref.at[b + nc - me], s_ref.at[slot], csem.at[slot], nc)
+    first_peer, second_peer = (ny, nx), (nx, ny)
+
+    def joined(q, j):
+        slot = q * 4 + zs[j]
+        pltpu.make_async_copy(p_ref.at[0], m_ref.at[slot], lsem.at[slot]).wait()
+        arrive(s_ref.at[slot], csem.at[slot])
+        add_into(m_ref.at[slot], s_ref.at[slot])
+
+    def to_first(part, q, j):
+        far = 4 if q == 3 else 0
+        push(m_ref.at[q * 4 + zs[j], :, cols[part]], first_ref.at[part, far + zs[j]],
+             fsem.at[part, far + zs[j]], first_peer[part])
+
+    for j in (3, 2, 1, 0):
+        joined(3, j)
+        to_first(0, 3, j)
+        to_first(1, 3, j)
+    for j in (3, 2, 1, 0):
+        joined(2, j)
+        to_first(0, 2, j)
+        joined(1, j)
+        to_first(1, 1, j)
+    for j in (3, 2, 1, 0):
+        for part in (0, 1):
+            arrive(first_ref.at[part, 4 + zs[j]], fsem.at[part, 4 + zs[j]])
+            q = (1, 2)[part]
+            m = m_ref.at[q * 4 + zs[j], :, cols[part]]
+            add_into(m, first_ref.at[part, 4 + zs[j]])
+            push(m, second_ref.at[part, zs[j]], gsem.at[part, zs[j]], second_peer[part])
+        joined(0, j)
+
+    def plane_sum(part, j):
+        m = m_ref.at[zs[j], :, cols[part]]
+        arrive(first_ref.at[part, zs[j]], fsem.at[part, zs[j]])
+        arrive(second_ref.at[part, zs[j]], gsem.at[part, zs[j]])
+        add_into(m, first_ref.at[part, zs[j]], second_ref.at[part, zs[j]])
+        return m
+    for part in (0, 1):
+        pass
+    for j in (3, 2, 1, 0):
+        for part in (0, 1):
+            m = plane_sum(part, j)
+            if j == 3:
+                push(m, za_ref.at[part, 0], zasem.at[part, 0], n1, end)
+
+                @pl.when(mid)
+                def _():
+                    arrive(za_ref.at[part, 0], zasem.at[part, 0])
+                    add_into(m, za_ref.at[part, 0])
+                push(m, zb_ref.at[part, 0], zbsem.at[part, 0], n2, mid)
+            elif j == 2:
+                push(m, za_ref.at[part, 1], zasem.at[part, 1], n1, end)
+
+                @pl.when(mid)
+                def _():
+                    arrive(za_ref.at[part, 1], zasem.at[part, 1])
+                    add_into(m, za_ref.at[part, 1])
+                push(m, zb_ref.at[part, 1], zbsem.at[part, 1], n2, mid)
+            elif j == 1:
+                push(m, za_ref.at[part, 2], zasem.at[part, 2], n1, end)
+
+                @pl.when(mid)
+                def _():
+                    arrive(zb_ref.at[part, 0], zbsem.at[part, 0])
+                    add_into(m, zb_ref.at[part, 0])
+                push(m, zb_ref.at[part, 0], zbsem.at[part, 0], n1, mid)
+    for part in (0, 1):
+        m = m_ref.at[zs[0], :, cols[part]]
+        o = o_ref.at[:, cols[part]]
+
+        def total(*more):
+            def step(i, _):
+                r = pl.ds(pl.multiple_of(i * 16, 16), 16)
+                v = m[r, :].astype(jnp.float32)
+                for e in more:
+                    v = v + e[r, :].astype(jnp.float32)
+                o[r, :] = v
+                return _
+            lax.fori_loop(0, rows // 16, step, 0)
+
+        @pl.when(mid)
+        def _():
+            arrive(za_ref.at[part, 2], zasem.at[part, 2])
+            arrive(zb_ref.at[part, 1], zbsem.at[part, 1])
+            total(za_ref.at[part, 2], zb_ref.at[part, 1])
+
+        @pl.when(end)
+        def _():
+            arrive(zb_ref.at[part, 0], zbsem.at[part, 0])
+            total(zb_ref.at[part, 0])
+    for finish, when in sends:
+        if when is None:
+            finish()
+        else:
+            pl.when(when)(finish)
+
+
+def scatter(parts, cid=1):
+    n, rows, width = parts.shape
+    dt = parts.dtype
+    half = width // 2
+    return pl.pallas_call(
+        scatter_kernel,
+        out_shape=jax.ShapeDtypeStruct((rows, width), jnp.float32),
+        in_specs=[pl.BlockSpec(memory_space=pl.ANY)],
+        out_specs=pl.BlockSpec(memory_space=pltpu.VMEM),
+        scratch_shapes=[
+            pltpu.VMEM((16, rows, width), dt),
+            pltpu.VMEM((16, rows, width), dt),
+            pltpu.VMEM((2, 8, rows, half), dt),
+            pltpu.VMEM((2, 4, rows, half), dt),
+            pltpu.VMEM((2, 3, rows, half), dt),
+            pltpu.VMEM((2, 2, rows, half), dt),
+            pltpu.SemaphoreType.DMA((16,)),
+            pltpu.SemaphoreType.DMA((16 + 16 + 8 + 12,)),
+            pltpu.SemaphoreType.DMA((16,)),
+            pltpu.SemaphoreType.DMA((2, 8)),
+            pltpu.SemaphoreType.DMA((2, 4)),
+            pltpu.SemaphoreType.DMA((2, 3)),
+            pltpu.SemaphoreType.DMA((2, 2)),
+        ],
+        name="scatter_rows",
+        compiler_params=pltpu.CompilerParams(collective_id=cid, has_side_effects=True, vmem_limit_bytes=56 * 2**20),
+    )(parts)
+
+
+def exchange(blocks):
+    return lax.all_to_all(blocks, AXIS, split_axis=0, concat_axis=0, tiled=True)
+
+
+def dot(left, right):
+    return jnp.dot(left, right, preferred_element_type=jnp.float32)
+
+
+def select(mask, rows):
+    return dot(mask.astype(jnp.bfloat16), rows).astype(jnp.bfloat16)
+
+
+def natural(rows, count, tiles):
+    width = rows.shape[-1]
+    return (
+        rows.reshape(count, tiles, -1, width).transpose(1, 0, 2, 3).reshape(tiles, -1, width)
+    )
+
+
+def dealt_order(rows, count):
+    tiles, length, width = rows.shape
+    return (
+        rows.reshape(tiles, count, length // count, width)
+        .transpose(1, 0, 2, 3)
+        .reshape(-1, width)
+    )
+
+
+def windows(tiled):
+    edge = jnp.zeros_like(tiled[:1])
+    padded = jnp.concatenate((edge, tiled, edge), axis=0)
+    return jnp.concatenate((padded[:-2], padded[1:-1], padded[2:]), axis=1)
+
+
+def unwindow(wide):
+    length = wide.shape[1] // 3
+    edge = jnp.zeros_like(wide[:1, :length])
+    return (
+        jnp.concatenate((wide[1:, :length], edge), axis=0)
+        + wide[:, length : 2 * length]
+        + jnp.concatenate((edge, wide[:-1, 2 * length :]), axis=0)
+    )
+
+
+def batched(left, right, left_dim, right_dim):
+    return lax.dot_general(
+        left,
+        right,
+        (((left_dim,), (right_dim,)), ((0,), (0,))),
+        preferred_element_type=jnp.float32,
+    )
+
+
+def body(
+    tokens,
+    lengths,
+    permutation,
+    query_weight,
+    key_weight,
+    value_weight,
+    out_weight,
+    gate_weight,
+    up_weight,
+    down_weight,
+    gain_attention,
+    gain_feedforward,
+    bias_table,
+    cotangent,
+):
+    me = lax.axis_index(AXIS)
+    count = tokens.shape[0]
+    grain = tokens.shape[1]
+    length = cotangent.shape[1]
+    width = tokens.shape[2]
+    shard = query_weight.shape[0]
+    hidden_width = gate_weight.shape[1] // count
+    head = HEAD_DIM
+    total = 3 * count * length // 5
+    tiles = -(-total // length)
+    slots = tiles * grain
+
+    columns = jnp.concatenate(
+        (
+            query_weight.reshape(shard, count, head),
+            key_weight.reshape(shard, count, head),
+            value_weight.reshape(shard, count, head),
+            gate_weight.reshape(shard, count, hidden_width),
+            up_weight.reshape(shard, count, hidden_width),
+        ),
+        axis=2,
+    )
+    columns = exchange(columns.transpose(1, 0, 2)).reshape(count * shard, -1)
+    qkv_columns, gate_up_columns = columns[:, : 3 * head], columns[:, 3 * head :]
+
+    small = jnp.concatenate((gain_attention, gain_feedforward, bias_table))
+    small = jnp.pad(small, (0, width - small.shape[0]))
+    small = jnp.broadcast_to(small, (count, 1, width))
+    came = exchange(jnp.concatenate((tokens[permutation], small), axis=1))
+    dealt = came[:, :grain].reshape(length, width)
+    gain_one = came[:, grain, :shard].reshape(-1).astype(jnp.float32)
+    gain_two = came[:, grain, shard : 2 * shard].reshape(-1).astype(jnp.float32)
+    table = came[:, grain, 2 * shard : 2 * shard + HEADS]
+
+    dealt_lengths = lengths[permutation]
+    ends = jnp.cumsum(dealt_lengths)
+    starts = ends - dealt_lengths
+    my_start, my_length = starts[me], dealt_lengths[me]
+    place_in = jnp.arange(length, dtype=jnp.int32)
+    turn = (
+        (place_in[:, None] - my_start) % length == place_in[None, :]
+    ) & (place_in[None, :] < my_length)
+    rolled = select(turn, jnp.concatenate((dealt, cotangent[0]), axis=1))
+    came = exchange(rolled.reshape(count, grain, 2 * width)).reshape(length, 2 * width)
+    slot_ids = jnp.arange(slots, dtype=jnp.int32)
+    packed_ids = slot_ids // grain * length + me * grain + slot_ids % grain
+    source_seq = jnp.sum((packed_ids[:, None] >= ends[None, :]).astype(jnp.int32), axis=1)
+    pick = (source_seq * grain + slot_ids % grain)[:, None] == place_in[None, :]
+    blocks = select(pick, came)
+    rows_in = blocks[:, :width].astype(jnp.float32)
+    upstream_low = blocks[:, width:]
+    upstream = upstream_low.astype(jnp.float32)
+
+    all_ids = jnp.arange(tiles * length, dtype=jnp.int32)
+    segment = jnp.sum((all_ids[:, None] >= ends[None, :]).astype(jnp.int32), axis=1) + 1
+    segment = segment.reshape(tiles, length, 1)
+    same = segment == windows(segment).reshape(tiles, 1, 3 * length)
+    relative = (
+        jnp.arange(3 * length, dtype=jnp.int32)[None, :] - length - place_in[:, None]
+    ).reshape(-1)
+    onehot = bucket_index(relative)[None, :] == jnp.arange(BUCKETS, dtype=jnp.int32)[:, None]
+    head_table = lax.dynamic_slice_in_dim(table, me, 1, axis=1)
+    rel_bias = dot(head_table.T, onehot.astype(jnp.bfloat16)).reshape(1, length, 3 * length)
+
+    scale_one = norm_scale(rows_in)
+    normed = (rows_in * scale_one * gain_one).astype(jnp.bfloat16)
+    normed_all = gather(normed).reshape(-1, width)
+    qkv = natural(dot(normed_all, qkv_columns).astype(jnp.bfloat16), count, tiles)
+    query, key, value = qkv[:, :, :head], qkv[:, :, head : 2 * head], qkv[:, :, 2 * head :]
+    key_window, value_window = windows(key), windows(value)
+    scores = jnp.where(same, batched(query, key_window, 2, 2) + rel_bias, masked_score)
+    probs = jax.nn.softmax(scores, axis=-1)
+    probs_low = probs.astype(jnp.bfloat16)
+    attended = dealt_order(batched(probs_low, value_window, 2, 1).astype(jnp.bfloat16), count)
+    branch = scatter(dot(attended, out_weight).astype(jnp.bfloat16).reshape(count, slots, width))
+    middle = rows_in + branch
+
+    scale_two = norm_scale(middle)
+    normed_two = (middle * scale_two * gain_two).astype(jnp.bfloat16)
+    normed_two_all = gather(normed_two).reshape(-1, width)
+    gate_up = dot(normed_two_all, gate_up_columns)
+
+    def gelu_product(gate_part, up_part):
+        return jax.nn.gelu(gate_part, approximate=True) * up_part
+
+    hidden_full, gelu_pull = jax.vjp(
+        gelu_product, gate_up[:, :hidden_width], gate_up[:, hidden_width:]
+    )
+    hidden = hidden_full.astype(jnp.bfloat16)
+    down = scatter(dot(hidden, down_weight).astype(jnp.bfloat16).reshape(count, slots, width))
+    result = (middle + down).astype(jnp.bfloat16)
+
+    upstream_all = gather(upstream_low).reshape(-1, width)
+    d_gate, d_up = gelu_pull(against_rows(upstream_all, down_weight))
+    d_gate_up = jnp.concatenate((d_gate, d_up), axis=1).astype(jnp.bfloat16)
+    down_grad = rows_product(hidden, upstream_all)
+    gate_up_grad = rows_product(normed_two_all, d_gate_up)
+    d_normed_two = scatter(
+        against_rows(d_gate_up, gate_up_columns)
+        .astype(jnp.bfloat16)
+        .reshape(count, slots, width)
+    )
+    gain_two_grad = jnp.sum(d_normed_two * middle * scale_two, axis=0)
+    d_middle = upstream + norm_back(middle, scale_two, gain_two, d_normed_two)
+
+    d_branch_all = gather(d_middle.astype(jnp.bfloat16)).reshape(-1, width)
+    out_grad = rows_product(attended, d_branch_all)
+    d_attended = natural(
+        against_rows(d_branch_all, out_weight).astype(jnp.bfloat16), count, tiles
+    )
+    d_value = unwindow(batched(probs_low, d_attended, 1, 1))
+    d_probs = batched(d_attended, value_window, 2, 2)
+    inner = jnp.sum(probs * d_probs, axis=-1, keepdims=True)
+    d_scores = (probs * (d_probs - inner)).astype(jnp.bfloat16)
+    d_query = batched(d_scores, key_window, 2, 1)
+    d_key = unwindow(batched(d_scores, query, 1, 1))
+    d_bias = jnp.sum(d_scores.astype(jnp.float32), axis=0).reshape(1, -1)
+    table_sum = jnp.sum(jnp.where(onehot, d_bias, 0.0), axis=1)
+    d_qkv = dealt_order(
+        jnp.concatenate((d_query, d_key, d_value), axis=2).astype(jnp.bfloat16), count
+    )
+    qkv_grad = rows_product(normed_all, d_qkv)
+    d_normed = scatter(
+        against_rows(d_qkv, qkv_columns).astype(jnp.bfloat16).reshape(count, slots, width)
+    )
+    gain_one_grad = jnp.sum(d_normed * rows_in * scale_one, axis=0)
+    d_dealt = (d_middle + norm_back(rows_in, scale_one, gain_one, d_normed)).astype(jnp.bfloat16)
+
+    turned = starts + (me * grain + jnp.arange(grain, dtype=jnp.int32)[:, None] - starts) % length
+    back_slot = (turned // length * grain + jnp.arange(grain, dtype=jnp.int32)[:, None]).T
+    spread = back_slot.reshape(-1, 1) == slot_ids[None, :]
+    going = select(spread, jnp.concatenate((result, d_dealt), axis=1))
+    came = exchange(going.reshape(count, grain, 2 * width)).reshape(length, 2 * width)
+    came = select(turn.T, came)
+    layer_output = came[None, :, :width]
+    tokens_grad = exchange(came[:, width:].reshape(count, grain, width))[jnp.argsort(permutation)]
+
+    going = jnp.concatenate((qkv_grad, gate_up_grad), axis=1).astype(jnp.bfloat16)
+    grads = exchange(going.reshape(count, shard, -1)).astype(jnp.float32)
+
+    def owned(first, size):
+        return grads[:, :, first : first + size].transpose(1, 0, 2).reshape(shard, -1)
+
+    going = jnp.concatenate(
+        (
+            gain_one_grad.reshape(count, shard),
+            gain_two_grad.reshape(count, shard),
+            table_sum.reshape(count, 1),
+        ),
+        axis=1,
+    )
+    came = exchange(jnp.pad(going, ((0, 0), (0, 256 - going.shape[1]))))
+    return (
+        layer_output,
+        tokens_grad,
+        owned(0, head),
+        owned(head, head),
+        owned(2 * head, head),
+        out_grad,
+        owned(3 * head, hidden_width),
+        owned(3 * head + hidden_width, hidden_width),
+        down_grad,
+        jnp.sum(came[:, :shard], axis=0),
+        jnp.sum(came[:, shard : 2 * shard], axis=0),
+        came[:, 2 * shard],
+    )
+
+
 def solution(mesh):
     placed = (
         P(None, "fsdp", None),
@@ -302,7 +856,7 @@
         P("fsdp", None, None),
     )
     return jax.shard_map(
-        body,
+        body if mesh.shape[AXIS] == 32 else body_any,
         mesh=mesh,
         in_specs=placed,
         out_specs=(

time: 2500 us -> 857 us (0.34)
  waiting for transfers between devices: 2020 us -> 64 us
  Pallas kernels: 0 us -> 487 us
  matrix products: 201 us -> 102 us
  blocking collectives: 82.3 us -> 0 us
  other arithmetic: 111 us -> 31.4 us
  local copies, waits for them, and re-layouts: 40.5 us -> 117 us
  starting transfers between devices: 13.2 us -> 44.4 us
    reduce_scatter x2 -> x0, waiting for transfers between devices: 1580 us -> none  [the longest x1 1140 us: body(): lax.psum_scatter(jnp.concatenate((rows_product(normed, d_qkv), jnp.concat...]
    pallas_call x0 -> x8, Pallas kernels: none -> 487 us  [the longest x4 254 us: scatter(): pl.pallas_call(scatter_kernel, out_shape=jax.ShapeDtypeStruct((rows, widt...]
    all_gather x2 -> x0, waiting for transfers between devices: 440 us -> none  [the longest x1 343 us: body(): lax.all_gather(shards[0], 'fsdp', axis=0, tiled=True)]
    concatenate x1 -> x3, other arithmetic: 98.5 us -> 4.52 us  [the longest x1 2.27 us: body(): jnp.concatenate((qkv_grad, gate_up_grad), axis=1).astype(jnp.bfloat16)]
    unnamed x2 -> x0, blocking collectives: 82.3 us -> none
    all_to_all x2 -> x7, waiting for transfers between devices: 0.01 us -> 64 us  [exchange(): return lax.all_to_all(blocks, AXIS, split_axis=0, concat_axis=0, tiled=True)]
    dot_general x4, matrix products: 82.3 us -> 26.6 us  [rows_product(): lax.dot_general(left, right, (((0,), (0,)), ((), ())), preferred_element_...]
    dot_general x5 -> x4, matrix products: 63.3 us -> 28.1 us  [against_rows(): lax.dot_general(left, right, (((1,), (1,)), ((), ())), preferred_element_...]
  transfers between devices with their start and end apart: 6 -> 7, of which waited for: 4 -> 4; matrix products, arithmetic and copies ran while one was open for 5% -> 12% of each run, Pallas kernels for 0% -> 15%
where the time goes in v1:
time: 857 us; the launch traced here: 847 us
  Pallas kernels  487 us (57%)
  local copies, waits for them, and re-layouts  117 us (14%)
  matrix products  102 us (12%)
  waiting for transfers between devices  64 us (7%)
  starting transfers between devices  44.4 us (5%)
  other arithmetic  31.4 us (4%)
    pallas_call x4, Pallas kernels, scatter(): pl.pallas_call(scatter_kernel, out_shape=jax.ShapeDtypeStruct((rows, widt...  254 us
    pallas_call x4, Pallas kernels, gather(): pl.pallas_call(gather_kernel, out_shape=jax.ShapeDtypeStruct((32, rows, w...  233 us
    all_to_all x7, waiting for transfers between devices, exchange(): return lax.all_to_all(blocks, AXIS, split_axis=0, concat_axis=0, tiled=True)  64 us
    all_to_all x7, starting transfers between devices, exchange(): return lax.all_to_all(blocks, AXIS, split_axis=0, concat_axis=0, tiled=True)  44.4 us
    dot_general x9, matrix products, dot(): return jnp.dot(left, right, preferred_element_type=jnp.float32)  32.4 us
    dot_general x4, matrix products, against_rows(): lax.dot_general(left, right, (((1,), (1,)), ((), ())), preferred_element_...  28.1 us
    dot_general x2, local copies, waits for them, and re-layouts, rows_product(): lax.dot_general(left, right, (((0,), (0,)), ((), ())), preferred_element_...  27.6 us
    dot_general x4, matrix products, rows_product(): lax.dot_general(left, right, (((0,), (0,)), ((), ())), preferred_element_...  26.6 us
  transfers between devices with their start and end apart: 7, of which 4 were waited for; matrix products, arithmetic and copies ran while one was open for 12% of the time, Pallas kernels for 15%

profile of v1, /device:TPU:29, one launch (start us, length us, event | category | flops | bytes accessed | tf_op | source)
XLA Modules:
  0.0 847.3 jit_solution(1908240413286204369)
XLA Ops:
  5.8 6.2 all-to-all-start
  15.5 20.5 %all-to-all-done = bf16[32,5,2048]{2,1,0:T(8,128)(2,1)S(1)} async-done(((bf16[32,5,2048]{2,1,0:T(8,128)(2,1)}), bf16[32,5,2048]{2,1,0:T(8,128)(2,1)S(1)}, u32[]{:S(2)}, u32[]{:S(2)}) %all-to-all-start) | async-done | bytes 655392 | tf_op jit(solution)/shard_map/all_to_all | solution.py:605
  60.0 8.7 %all-to-all-done.1 = bf16[32,4,4096]{2,1,0:T(4,128)(2,1)} async-done(((bf16[32,4,4096]{2,1,0:T(4,128)(2,1)}), bf16[32,4,4096]{2,1,0:T(4,128)(2,1)}, u32[]{:S(2)}, u32[]{:S(2)}) %all-to-all-start.1) | async-done | bytes 1048608 | tf_op jit(solution)/shard_map/all_to_all | solution.py:605
  89.6 69.2 %gather_rows.4 = bf16[32,80,2048]{2,1,0:T(8,128)(2,1)} custom-call(bf16[80,2048]{1,0:T(8,128)(2,1)} %fusion.32.a_ref), custom_call_target="tpu_custom_call" | custom-call | tf_op jit(solution)/shard_map/gather_rows/pallas_call | solution.py:414
  158.8 55.5 %gather_rows.6 = bf16[32,80,2048]{2,1,0:T(8,128)(2,1)} custom-call(bf16[80,2048]{1,0:T(8,128)(2,1)} %slice.164.a_ref), custom_call_target="tpu_custom_call" | custom-call | tf_op jit(solution)/shard_map/gather_rows/pallas_call | solution.py:414
  215.8 8.5 %convolution_convert_fusion.8 = bf16[2560,192]{0,1:T(8,128)(2,1)} fusion(bf16[2560,2048]{1,0:T(8,128)(2,1)} %bitcast.107, bf16[2048,512]{1,0:T(8,128)(2,1)S(1)} %bitcast.118), kind=kOutput, calls=%fused_computation.22 | convolution fusion | flops 2013757440 | bytes 12517376 | tf_op jit(solution)/shard_map/dot_general | solution.py:609
  255.0 69.8 %scatter_rows.4 = f32[80,2048]{1,0:T(8,128)} custom-call(bf16[32,80,2048]{2,1,0:T(8,128)(2,1)} %bitcast.105), custom_call_target="tpu_custom_call" | custom-call | tf_op jit(solution)/shard_map/scatter_rows/pallas_call | solution.py:579
  327.9 54.6 %gather_rows.5 = bf16[32,80,2048]{2,1,0:T(8,128)(2,1)} custom-call(bf16[80,2048]{1,0:T(8,128)(2,1)} %multiply_convert_fusion.3.a_ref), custom_call_target="tpu_custom_call" | custom-call | tf_op jit(solution)/shard_map/gather_rows/pallas_call | solution.py:414
  382.5 7.6 fusion.19
  395.6 8.6 %convolution_convert_fusion.3 = bf16[2560,2048]{1,0:T(8,128)(2,1)} fusion(bf16[2048,512]{1,0:T(8,128)(2,1)S(1)} %bitcast.121, bf16[2560,160]{0,1:T(8,128)(2,1)S(1)} %get-tuple-element.29, bf16[2560,160]{0,1:T(8,128)(2,1)S(1)} %get-tuple-element.28), kind=kOutput, calls=%fused_computation.7 | convolution fusion | flops 3363962880 | bytes 13697024 | tf_op jit(solution)/shard_map/dot_general | solution.py:59
  404.3 59.2 %scatter_rows.6 = f32[80,2048]{1,0:T(8,128)} custom-call(bf16[32,80,2048]{2,1,0:T(8,128)(2,1)} %bitcast.115), custom_call_target="tpu_custom_call" | custom-call | tf_op jit(solution)/shard_map/scatter_rows/pallas_call | solution.py:579
  470.4 65.0 %scatter_rows.5 = f32[80,2048]{1,0:T(8,128)} custom-call(bf16[32,80,2048]{2,1,0:T(8,128)(2,1)} %bitcast.106), custom_call_target="tpu_custom_call" | custom-call | tf_op jit(solution)/shard_map/scatter_rows/pallas_call | solution.py:579
  537.9 53.7 %gather_rows.7 = bf16[32,80,2048]{2,1,0:T(8,128)(2,1)} custom-call(bf16[80,2048]{1,0:T(8,128)(2,1)} %get-tuple-element.24.a_ref), custom_call_target="tpu_custom_call" | custom-call | tf_op jit(solution)/shard_map/gather_rows/pallas_call | solution.py:414
  591.5 7.3 convolution_convert_fusion.9
  621.9 6.7 convolution_convert_fusion
  628.6 59.7 %scatter_rows.7 = f32[80,2048]{1,0:T(8,128)} custom-call(bf16[32,80,2048]{2,1,0:T(8,128)(2,1)} %bitcast.104), custom_call_target="tpu_custom_call" | custom-call | tf_op jit(solution)/shard_map/scatter_rows/pallas_call | solution.py:579
  692.9 8.2 all-to-all-start.3
  701.1 13.8 %copy.127 = bf16[2048,2560]{1,0:T(8,128)(2,1)} copy(bf16[2048,2560]{0,1:T(8,128)(2,1)} %bitcast.108) | data formatting | bytes 20971520 | tf_op jit(solution)/shard_map/dot_general | solution.py:53
  716.6 13.8 %copy.129 = bf16[2048,2560]{1,0:T(8,128)(2,1)} copy(bf16[2048,2560]{0,1:T(8,128)(2,1)} %bitcast.110) | data formatting | bytes 20971520 | tf_op jit(solution)/shard_map/dot_general | solution.py:53
  730.5 9.7 %convolution_convert_fusion.10 = bf16[32,64,320]{2,1,0:T(8,128)(2,1)} fusion(bf16[32,64,2560]{2,1,0:T(8,128)(2,1)} %bitcast.114, bf16[2560,160]{0,1:T(8,128)(2,1)} %copy-done.50, bf16[2560,160]{0,1:T(8,128)(2,1)} %copy-done.49), kind=kOutput, calls=%fused_computation.36 | convolution fusion | flops 3359375360 | bytes 13434880 | tf_op jit(solution)/shard_map/dot_general | solution.py:53
  756.6 7.0 convolution_convert_fusion.11
  769.1 6.6 all-to-all-start.5
  777.4 6.9 fusion.114
  790.4 31.5 %all-to-all-done.5 = bf16[32,64,512]{2,1,0:T(8,128)(2,1)} async-done(((bf16[32,64,512]{2,1,0:T(8,128)(2,1)}), bf16[32,64,512]{2,1,0:T(8,128)(2,1)}, u32[]{:S(2)}, u32[]{:S(2)}) %all-to-all-start.5) | async-done | bytes 2097184 | tf_op jit(solution)/shard_map/all_to_all | solution.py:605
  (262 shorter events, 187.1 us)
Async XLA Ops:
  0.6 389.5 %copy-start = (bf16[160,2048]{1,0:T(8,128)(2,1)S(1)}, bf16[160,2048]{1,0:T(8,128)(2,1)}, u32[]{:S(2)}) copy-start(bf16[160,2048]{1,0:T(8,128)(2,1)} %param.23) | copy-start | bytes 1966084
  5.8 31.1 %copy-start.31 = (bf16[1,128,2048]{2,1,0:T(8,128)(2,1)S(1)}, bf16[1,128,2048]{2,1,0:T(8,128)(2,1)}, u32[]{:S(2)}) copy-start(bf16[1,128,2048]{2,1,0:T(8,128)(2,1)} %param.27) | copy-start | bytes 1572868
  5.8 30.2 %all-to-all-start = ((bf16[32,5,2048]{2,1,0:T(8,128)(2,1)}), bf16[32,5,2048]{2,1,0:T(8,128)(2,1)S(1)}, u32[]{:S(2)}, u32[]{:S(2)}) async-start(bf16[32,5,2048]{2,1,0:T(8,128)(2,1)} %pad_maximum_fusion.4), calls=%async_computation | async-start | bytes 2097152 | tf_op jit(solution)/shard_map/all_to_all | solution.py:605
  14.8 22.6 %copy-start.43 = (pred[128]{0:T(512)(128)(4,1)}, pred[128]{0:T(512)(128)(4,1)S(1)}, u32[]{:S(2)}) copy-start(pred[128]{0:T(512)(128)(4,1)S(1)} %iota_compare_fusion.10) | copy-start | bytes 388
  15.5 22.0 %copy-start.45 = (s32[128]{0:T(128)}, s32[128]{0:T(128)S(1)}, u32[]{:S(2)}) copy-start(s32[128]{0:T(128)S(1)} %and_select_fusion.4) | copy-start | bytes 1540
  38.7 30.0 %all-to-all-start.1 = ((bf16[32,4,4096]{2,1,0:T(4,128)(2,1)}), bf16[32,4,4096]{2,1,0:T(4,128)(2,1)}, u32[]{:S(2)}, u32[]{:S(2)}) async-start(bf16[32,4,4096]{2,1,0:T(4,128)(2,1)} %reshape.471), calls=%async_computation.1 | async-start | bytes 2097152 | tf_op jit(solution)/shard_map/all_to_all | solution.py:605
  68.7 145.7 %all-to-all-start.2 = ((bf16[32,64,512]{2,1,0:T(8,128)(2,1)}), bf16[32,64,512]{2,1,0:T(8,128)(2,1)S(1)}, u32[]{:S(2)}, u32[]{:S(2)}) async-start(bf16[32,64,512]{2,1,0:T(8,128)(2,1)} %copy.111), calls=%async_computation.2 | async-start | bytes 4194304 | tf_op jit(solution)/shard_map/all_to_all | solution.py:605
  327.9 62.2 %slice-start = ((s8[10485760]{0:T(1024)(128)(4,1)}), s8[2097152]{0:T(1024)(128)(4,1)S(1)}, s32[]{:S(2)}) async-start(s8[10485760]{0:T(1024)(128)(4,1)} %bitcast.98), calls=%async_computation.7 | async-start | bytes 4194304
  404.3 59.2 %copy-start.6 = (f32[80,2048]{1,0:T(8,128)S(1)}, f32[80,2048]{1,0:T(8,128)}, u32[]{:S(2)}) copy-start(f32[80,2048]{1,0:T(8,128)} %copy-done.5) | copy-start | bytes 1966084
  404.3 60.6 %copy-start.9 = (bf16[2560,160]{0,1:T(8,128)(2,1)S(1)}, bf16[2560,160]{0,1:T(8,128)(2,1)}, u32[]{:S(2)}) copy-start(bf16[2560,160]{0,1:T(8,128)(2,1)} %get-tuple-element.35) | copy-start | bytes 2457604
  470.4 65.0 %copy-start.11 = (f32[80,2048]{1,0:T(8,128)S(1)}, f32[80,2048]{1,0:T(8,128)}, u32[]{:S(2)}) copy-start(f32[80,2048]{1,0:T(8,128)} %scatter_rows.6) | copy-start | bytes 1966084
  537.9 53.7 %copy-start.24 = (bf16[64,2048]{1,0:T(8,128)(2,1)S(1)}, bf16[64,2048]{1,0:T(8,128)(2,1)}, u32[]{:S(2)}) copy-start(bf16[64,2048]{1,0:T(8,128)(2,1)} %param.20) | copy-start | bytes 786436
  628.6 61.1 %copy-start.16 = (f32[80,2048]{1,0:T(8,128)S(1)}, f32[80,2048]{1,0:T(8,128)}, u32[]{:S(2)}) copy-start(f32[80,2048]{1,0:T(8,128)} %get-tuple-element.25) | copy-start | bytes 1966084
  691.6 9.4 %copy-start.25 = (s32[49152]{0:T(1024)S(1)}, s32[49152]{0:T(1024)}, u32[]{:S(2)}) copy-start(s32[49152]{0:T(1024)} %reshape.549) | copy-start | bytes 589828
  691.6 9.4 %copy-start.26 = (s32[49152]{0:T(1024)S(1)}, s32[49152]{0:T(1024)}, u32[]{:S(2)}) copy-start(s32[49152]{0:T(1024)} %abs.14) | copy-start | bytes 589828
  691.7 9.4 %copy-start.27 = (s32[49152]{0:T(1024)S(1)}, s32[49152]{0:T(1024)}, u32[]{:S(2)}) copy-start(s32[49152]{0:T(1024)} %select_n.115) | copy-start | bytes 589828
  692.9 47.3 %all-to-all-start.3 = ((bf16[32,4,4096]{2,1,0:T(4,128)(2,1)}), bf16[32,4,4096]{2,1,0:T(4,128)(2,1)S(1)}, u32[]{:S(2)}, u32[]{:S(2)}) async-start(bf16[32,4,4096]{2,1,0:T(4,128)(2,1)} %reshape.495), calls=%async_computation.3 | async-start | bytes 2097152 | tf_op jit(solution)/shard_map/all_to_all | solution.py:605
  701.1 13.9 %copy-start.28 = (f32[128,384]{1,0:T(8,128)S(1)}, f32[128,384]{1,0:T(8,128)}, u32[]{:S(2)}) copy-start(f32[128,384]{1,0:T(8,128)} %get-tuple-element.22) | copy-start | bytes 589828
  740.1 10.6 %all-to-all-start.6 = ((f32[32,1,256]{2,1,0:T(1,128)}), f32[32,1,256]{2,1,0:T(1,128)S(1)}, u32[]{:S(2)}, u32[]{:S(2)}) async-start(f32[32,1,256]{2,1,0:T(1,128)} %copy.136), calls=%async_computation.6 | async-start | bytes 65536 | tf_op jit(solution)/shard_map/all_to_all | solution.py:605
  750.7 18.4 %all-to-all-start.4 = ((bf16[32,4,2048]{2,1,0:T(4,128)(2,1)}), bf16[32,4,2048]{2,1,0:T(4,128)(2,1)S(1)}, u32[]{:S(2)}, u32[]{:S(2)}) async-start(bf16[32,4,2048]{2,1,0:T(4,128)(2,1)} %reshape.497), calls=%async_computation.4 | async-start | bytes 1048576 | tf_op jit(solution)/shard_map/all_to_all | solution.py:605
  763.6 20.7 %slice-start.3 = ((s8[10485760]{0:T(1024)(128)(4,1)}), s8[2097152]{0:T(1024)(128)(4,1)S(1)}, s32[]{:S(2)}) async-start(s8[10485760]{0:T(1024)(128)(4,1)} %bitcast.101), calls=%async_computation.10 | async-start | bytes 4194304
  765.9 9.9 %copy-start.48 = (s32[32]{0:T(128)S(1)}, s32[32]{0:T(128)}, u32[]{:S(2)}) copy-start(s32[32]{0:T(128)} %param.16) | copy-start | bytes 388
  765.9 11.5 %copy-start.4 = (bf16[32,20,4,64]{3,2,1,0:T(4,128)(2,1)S(1)}, bf16[32,20,4,64]{3,2,1,0:T(4,128)(2,1)}, u32[]{:S(2)}) copy-start(bf16[32,20,4,64]{3,2,1,0:T(4,128)(2,1)} %copy-done.3) | copy-start | bytes 983044
  769.1 52.8 %all-to-all-start.5 = ((bf16[32,64,512]{2,1,0:T(8,128)(2,1)}), bf16[32,64,512]{2,1,0:T(8,128)(2,1)}, u32[]{:S(2)}, u32[]{:S(2)}) async-start(bf16[32,64,512]{2,1,0:T(8,128)(2,1)} %pad_maximum_fusion), calls=%async_computation.5 | async-start | bytes 4194304 | tf_op jit(solution)/shard_map/all_to_all | solution.py:605
  (40 other events, 203.4 us)

commit v2 on v1

--- a/solution.py
+++ b/solution.py
@@ -654,6 +654,65 @@
     )
 
 
+def beside(sent, chain, kernel):
+    sent, chain = lax.optimization_barrier((sent, chain))
+    return lax.optimization_barrier((exchange(sent), kernel(chain)))
+
+
+def pack_kernel(query_ref, key_ref, value_ref, gate_ref, up_ref, first_ref, second_ref):
+    count = first_ref.shape[0]
+    head = query_ref.shape[1] // count
+    units = gate_ref.shape[1] // count
+    for j in range(count):
+        for i, ref in enumerate((query_ref, key_ref, value_ref)):
+            first_ref[j, :, i * head : (i + 1) * head] = ref[:, j * head : (j + 1) * head]
+        first_ref[j, :, 3 * head :] = gate_ref[:, j * units : j * units + head]
+        second_ref[j, :, : units - head] = gate_ref[:, j * units + head : (j + 1) * units]
+        second_ref[j, :, units - head :] = up_ref[:, j * units : (j + 1) * units]
+
+
+def pack(shards, count):
+    rows, width = shards[0].shape
+    head, units = width // count, shards[3].shape[1] // count
+    return pl.pallas_call(
+        pack_kernel,
+        out_shape=[
+            jax.ShapeDtypeStruct((count, rows, 4 * head), jnp.bfloat16),
+            jax.ShapeDtypeStruct((count, rows, 2 * units - head), jnp.bfloat16),
+        ],
+        in_specs=[pl.BlockSpec(memory_space=pltpu.VMEM)] * 5,
+        out_specs=[pl.BlockSpec(memory_space=pltpu.VMEM)] * 2,
+        name="pack_columns",
+        compiler_params=pltpu.CompilerParams(vmem_limit_bytes=32 * 2**20),
+    )(*shards)
+
+
+def unpack_kernel(first_ref, second_ref, query_ref, key_ref, value_ref, gate_ref, up_ref):
+    count = first_ref.shape[0]
+    head = query_ref.shape[1] // count
+    units = gate_ref.shape[1] // count
+    wide = jnp.float32
+    for j in range(count):
+        for i, ref in enumerate((query_ref, key_ref, value_ref)):
+            ref[:, j * head : (j + 1) * head] = first_ref[j, :, i * head : (i + 1) * head].astype(wide)
+        gate_ref[:, j * units : j * units + head] = first_ref[j, :, 3 * head :].astype(wide)
+        gate_ref[:, j * units + head : (j + 1) * units] = second_ref[j, :, : units - head].astype(wide)
+        up_ref[:, j * units : (j + 1) * units] = second_ref[j, :, units - head :].astype(wide)
+
+
+def unpack(first, second, width, hidden):
+    rows = first.shape[1]
+    widths = (width, width, width, hidden, hidden)
+    return pl.pallas_call(
+        unpack_kernel,
+        out_shape=[jax.ShapeDtypeStruct((rows, columns), jnp.float32) for columns in widths],
+        in_specs=[pl.BlockSpec(memory_space=pltpu.VMEM)] * 2,
+        out_specs=[pl.BlockSpec(memory_space=pltpu.VMEM)] * 5,
+        name="unpack_columns",
+        compiler_params=pltpu.CompilerParams(vmem_limit_bytes=32 * 2**20),
+    )(first, second)
+
+
 def body(
     tokens,
     lengths,
@@ -682,27 +741,15 @@
     tiles = -(-total // length)
     slots = tiles * grain
 
-    columns = jnp.concatenate(
-        (
-            query_weight.reshape(shard, count, head),
-            key_weight.reshape(shard, count, head),
-            value_weight.reshape(shard, count, head),
-            gate_weight.reshape(shard, count, hidden_width),
-            up_weight.reshape(shard, count, hidden_width),
-        ),
-        axis=2,
-    )
-    columns = exchange(columns.transpose(1, 0, 2)).reshape(count * shard, -1)
-    qkv_columns, gate_up_columns = columns[:, : 3 * head], columns[:, 3 * head :]
-
     small = jnp.concatenate((gain_attention, gain_feedforward, bias_table))
-    small = jnp.pad(small, (0, width - small.shape[0]))
-    small = jnp.broadcast_to(small, (count, 1, width))
-    came = exchange(jnp.concatenate((tokens[permutation], small), axis=1))
-    dealt = came[:, :grain].reshape(length, width)
-    gain_one = came[:, grain, :shard].reshape(-1).astype(jnp.float32)
-    gain_two = came[:, grain, shard : 2 * shard].reshape(-1).astype(jnp.float32)
-    table = came[:, grain, 2 * shard : 2 * shard + HEADS]
+    small = jnp.pad(small, (0, grain * 128 - small.shape[0])).reshape(1, grain, 128)
+    small = jnp.broadcast_to(small, (count, grain, 128))
+    came = exchange(jnp.concatenate((tokens[permutation], small), axis=2))
+    dealt = came[:, :, :width].reshape(length, width)
+    small = came[:, :, width:].reshape(count, -1)
+    gain_one = small[:, :shard].reshape(-1).astype(jnp.float32)
+    gain_two = small[:, shard : 2 * shard].reshape(-1).astype(jnp.float32)
+    table = small[:, 2 * shard : 2 * shard + HEADS]
 
     dealt_lengths = lengths[permutation]
     ends = jnp.cumsum(dealt_lengths)
@@ -712,16 +759,22 @@
     turn = (
         (place_in[:, None] - my_start) % length == place_in[None, :]
     ) & (place_in[None, :] < my_length)
-    rolled = select(turn, jnp.concatenate((dealt, cotangent[0]), axis=1))
-    came = exchange(rolled.reshape(count, grain, 2 * width)).reshape(length, 2 * width)
     slot_ids = jnp.arange(slots, dtype=jnp.int32)
     packed_ids = slot_ids // grain * length + me * grain + slot_ids % grain
     source_seq = jnp.sum((packed_ids[:, None] >= ends[None, :]).astype(jnp.int32), axis=1)
     pick = (source_seq * grain + slot_ids % grain)[:, None] == place_in[None, :]
-    blocks = select(pick, came)
-    rows_in = blocks[:, :width].astype(jnp.float32)
-    upstream_low = blocks[:, width:]
-    upstream = upstream_low.astype(jnp.float32)
+
+    def spread_out(rows):
+        return select(turn, rows).reshape(count, grain, width)
+
+    def packed_block(came):
+        return select(pick, came.reshape(length, width))
+
+    rows_low = packed_block(exchange(spread_out(dealt)))
+    rows_in = rows_low.astype(jnp.float32)
+    first_columns, second_columns = pack(
+        (query_weight, key_weight, value_weight, gate_weight, up_weight), count
+    )
 
     all_ids = jnp.arange(tiles * length, dtype=jnp.int32)
     segment = jnp.sum((all_ids[:, None] >= ends[None, :]).astype(jnp.int32), axis=1) + 1
@@ -734,9 +787,20 @@
     head_table = lax.dynamic_slice_in_dim(table, me, 1, axis=1)
     rel_bias = dot(head_table.T, onehot.astype(jnp.bfloat16)).reshape(1, length, 3 * length)
 
+    def owners_share(turned):
+        return lax.optimization_barrier(turned).T.reshape(count, shard, -1)
+
     scale_one = norm_scale(rows_in)
     normed = (rows_in * scale_one * gain_one).astype(jnp.bfloat16)
-    normed_all = gather(normed).reshape(-1, width)
+    cut = (count, -1, 4 * head)
+    sent = jnp.concatenate((first_columns, spread_out(cotangent[0]).reshape(cut)), axis=1)
+    came, normed_all = beside(sent, normed, gather)
+    normed_all = normed_all.reshape(-1, width)
+    first_columns = came[:, :shard].reshape(-1, 4 * head)
+    upstream_low = packed_block(came[:, shard:])
+    upstream = upstream_low.astype(jnp.float32)
+    upstream_all = lax.all_gather(upstream_low, AXIS, axis=0, tiled=True)
+    qkv_columns = first_columns[:, : 3 * head]
     qkv = natural(dot(normed_all, qkv_columns).astype(jnp.bfloat16), count, tiles)
     query, key, value = qkv[:, :, :head], qkv[:, :, head : 2 * head], qkv[:, :, 2 * head :]
     key_window, value_window = windows(key), windows(value)
@@ -744,11 +808,15 @@
     probs = jax.nn.softmax(scores, axis=-1)
     probs_low = probs.astype(jnp.bfloat16)
     attended = dealt_order(batched(probs_low, value_window, 2, 1).astype(jnp.bfloat16), count)
-    branch = scatter(dot(attended, out_weight).astype(jnp.bfloat16).reshape(count, slots, width))
+    partial = dot(attended, out_weight).astype(jnp.bfloat16).reshape(count, slots, width)
+    came, branch = beside(second_columns, partial, scatter)
+    second_columns = came.reshape(count * shard, -1)
+    gate_up_columns = jnp.concatenate((first_columns[:, 3 * head :], second_columns), axis=1)
     middle = rows_in + branch
 
     scale_two = norm_scale(middle)
     normed_two = (middle * scale_two * gain_two).astype(jnp.bfloat16)
+    normed_two, upstream_all = lax.optimization_barrier((normed_two, upstream_all))
     normed_two_all = gather(normed_two).reshape(-1, width)
     gate_up = dot(normed_two_all, gate_up_columns)
 
@@ -759,24 +827,30 @@
         gelu_product, gate_up[:, :hidden_width], gate_up[:, hidden_width:]
     )
     hidden = hidden_full.astype(jnp.bfloat16)
-    down = scatter(dot(hidden, down_weight).astype(jnp.bfloat16).reshape(count, slots, width))
-    result = (middle + down).astype(jnp.bfloat16)
-
-    upstream_all = gather(upstream_low).reshape(-1, width)
+
     d_gate, d_up = gelu_pull(against_rows(upstream_all, down_weight))
     d_gate_up = jnp.concatenate((d_gate, d_up), axis=1).astype(jnp.bfloat16)
-    down_grad = rows_product(hidden, upstream_all)
-    gate_up_grad = rows_product(normed_two_all, d_gate_up)
-    d_normed_two = scatter(
-        against_rows(d_gate_up, gate_up_columns)
-        .astype(jnp.bfloat16)
-        .reshape(count, slots, width)
-    )
+    gate_up_grad = rows_product(d_gate_up, normed_two_all).astype(jnp.bfloat16)
+    partial = against_rows(d_gate_up, gate_up_columns).astype(jnp.bfloat16)
+    d_normed_two = scatter(partial.reshape(count, slots, width))
+    partial = dot(hidden, down_weight).astype(jnp.bfloat16)
+    partial, d_normed_two = lax.optimization_barrier((partial, d_normed_two))
+    down = scatter(partial.reshape(count, slots, width))
+    d_normed_two, down = lax.optimization_barrier((d_normed_two, down))
+    result = (middle + down).astype(jnp.bfloat16)
     gain_two_grad = jnp.sum(d_normed_two * middle * scale_two, axis=0)
     d_middle = upstream + norm_back(middle, scale_two, gain_two, d_normed_two)
-
-    d_branch_all = gather(d_middle.astype(jnp.bfloat16)).reshape(-1, width)
-    out_grad = rows_product(attended, d_branch_all)
+    turned = starts + (me * grain + jnp.arange(grain, dtype=jnp.int32)[:, None] - starts) % length
+    back_slot = (turned // length * grain + jnp.arange(grain, dtype=jnp.int32)[:, None]).T
+    spread = back_slot.reshape(-1, 1) == slot_ids[None, :]
+
+    sent = jnp.concatenate(
+        (owners_share(gate_up_grad[head:]), select(spread, result).reshape(cut)), axis=1
+    )
+    came, d_branch_all = beside(sent, d_middle.astype(jnp.bfloat16), gather)
+    second_grad = came[:, :shard]
+    layer_output = select(turn.T, came[:, shard:].reshape(length, width))[None]
+    d_branch_all = d_branch_all.reshape(-1, width)
     d_attended = natural(
         against_rows(d_branch_all, out_weight).astype(jnp.bfloat16), count, tiles
     )
@@ -791,29 +865,19 @@
     d_qkv = dealt_order(
         jnp.concatenate((d_query, d_key, d_value), axis=2).astype(jnp.bfloat16), count
     )
-    qkv_grad = rows_product(normed_all, d_qkv)
-    d_normed = scatter(
-        against_rows(d_qkv, qkv_columns).astype(jnp.bfloat16).reshape(count, slots, width)
-    )
+    qkv_grad = rows_product(d_qkv, normed_all).astype(jnp.bfloat16)
+    sent = owners_share(jnp.concatenate((qkv_grad, gate_up_grad[:head]), axis=0))
+    partial = against_rows(d_qkv, qkv_columns).astype(jnp.bfloat16)
+    first_grad, d_normed = beside(sent, partial.reshape(count, slots, width), scatter)
+    first_grad, second_grad, attended, hidden, d_normed = lax.optimization_barrier(
+        (first_grad, second_grad, attended, hidden, d_normed)
+    )
+    out_grad = rows_product(attended, d_branch_all)
+    down_grad = rows_product(hidden, upstream_all)
     gain_one_grad = jnp.sum(d_normed * rows_in * scale_one, axis=0)
     d_dealt = (d_middle + norm_back(rows_in, scale_one, gain_one, d_normed)).astype(jnp.bfloat16)
 
-    turned = starts + (me * grain + jnp.arange(grain, dtype=jnp.int32)[:, None] - starts) % length
-    back_slot = (turned // length * grain + jnp.arange(grain, dtype=jnp.int32)[:, None]).T
-    spread = back_slot.reshape(-1, 1) == slot_ids[None, :]
-    going = select(spread, jnp.concatenate((result, d_dealt), axis=1))
-    came = exchange(going.reshape(count, grain, 2 * width)).reshape(length, 2 * width)
-    came = select(turn.T, came)
-    layer_output = came[None, :, :width]
-    tokens_grad = exchange(came[:, width:].reshape(count, grain, width))[jnp.argsort(permutation)]
-
-    going = jnp.concatenate((qkv_grad, gate_up_grad), axis=1).astype(jnp.bfloat16)
-    grads = exchange(going.reshape(count, shard, -1)).astype(jnp.float32)
-
-    def owned(first, size):
-        return grads[:, :, first : first + size].transpose(1, 0, 2).reshape(shard, -1)
-
-    going = jnp.concatenate(
+    sums = jnp.concatenate(
         (
             gain_one_grad.reshape(count, shard),
             gain_two_grad.reshape(count, shard),
@@ -821,20 +885,32 @@
         ),
         axis=1,
     )
-    came = exchange(jnp.pad(going, ((0, 0), (0, 256 - going.shape[1]))))
+    high = lax.reduce_precision(sums, 8, 7)
+    sums = jnp.concatenate((high, sums - high), axis=1).astype(jnp.bfloat16)
+    sums = jnp.pad(sums, ((0, 0), (0, grain * 128 - sums.shape[1]))).reshape(count, grain, 128)
+    going = select(spread, d_dealt).reshape(count, grain, width)
+    came = exchange(jnp.concatenate((going, sums), axis=2))
+    sums = came[:, :, width:].reshape(count, -1).astype(jnp.float32)
+    sums = sums[:, : 2 * shard + 1] + sums[:, 2 * shard + 1 : 4 * shard + 2]
+    came = select(turn.T, came[:, :, :width].reshape(length, width))
+    tokens_grad = exchange(came.reshape(count, grain, width))[jnp.argsort(permutation)]
+
+    query_grad, key_grad, value_grad, gate_grad, up_grad = unpack(
+        first_grad, second_grad, width, hidden_width * count
+    )
     return (
         layer_output,
         tokens_grad,
-        owned(0, head),
-        owned(head, head),
-        owned(2 * head, head),
+        query_grad,
+        key_grad,
+        value_grad,
         out_grad,
-        owned(3 * head, hidden_width),
-        owned(3 * head + hidden_width, hidden_width),
+        gate_grad,
+        up_grad,
         down_grad,
-        jnp.sum(came[:, :shard], axis=0),
-        jnp.sum(came[:, shard : 2 * shard], axis=0),
-        came[:, 2 * shard],
+        jnp.sum(sums[:, :shard], axis=0),
+        jnp.sum(sums[:, shard : 2 * shard], axis=0),
+        sums[:, 2 * shard],
     )
 
 

time: 857 us -> 776 us (0.905)
  local copies, waits for them, and re-layouts: 117 us -> 61.4 us
  waiting for transfers between devices: 64 us -> 18.1 us
  between operations: 1.94 us -> 15.7 us
    all_to_all x7 -> x8, waiting for transfers between devices: 64 us -> 18.1 us  [exchange(): return lax.all_to_all(blocks, AXIS, split_axis=0, concat_axis=0, tiled=True)]
    dot_general x2 -> x0, local copies, waits for them, and re-layouts: 27.6 us -> none  [rows_product(): lax.dot_general(left, right, (((0,), (0,)), ((), ())), preferred_element_...]
    pallas_call x4 -> x3, Pallas kernels: 233 us -> 205 us  [gather(): pl.pallas_call(gather_kernel, out_shape=jax.ShapeDtypeStruct((32, rows, w...]
    pallas_call x4, Pallas kernels: 254 us -> 277 us  [scatter(): pl.pallas_call(scatter_kernel, out_shape=jax.ShapeDtypeStruct((rows, widt...]
    transpose x8 -> x2, local copies, waits for them, and re-layouts: 16.6 us -> 2.78 us  [owners_share(): return lax.optimization_barrier(turned).T.reshape(count, shard, -1)]
    reshape x16 -> x10, local copies, waits for them, and re-layouts: 23.4 us -> 10.5 us  [the longest x2 2.44 us: packed_block(): return select(pick, came.reshape(length, width))]
    dot_general x9 -> x13, matrix products: 32.4 us -> 40.6 us  [dot(): return jnp.dot(left, right, preferred_element_type=jnp.float32)]
    all_to_all x7 -> x8, starting transfers between devices: 44.4 us -> 46.4 us  [exchange(): return lax.all_to_all(blocks, AXIS, split_axis=0, concat_axis=0, tiled=True)]
  transfers between devices with their start and end apart: 7 -> 9, of which waited for: 4 -> 3; matrix products, arithmetic and copies ran while one was open for 12% -> 11% of each run, Pallas kernels for 15% -> 40%
where the time goes in v2:
time: 776 us; the launch traced here: 762 us
  Pallas kernels  487 us (63%)
  matrix products  107 us (14%)
  local copies, waits for them, and re-layouts  61.4 us (8%)
  starting transfers between devices  46.4 us (6%)
  other arithmetic  27.3 us (4%)
  waiting for transfers between devices  18.1 us (2%)
  between operations  15.7 us (2%)
    pallas_call x4, Pallas kernels, scatter(): pl.pallas_call(scatter_kernel, out_shape=jax.ShapeDtypeStruct((rows, widt...  277 us
    pallas_call x3, Pallas kernels, gather(): pl.pallas_call(gather_kernel, out_shape=jax.ShapeDtypeStruct((32, rows, w...  205 us
    all_to_all x8, starting transfers between devices, exchange(): return lax.all_to_all(blocks, AXIS, split_axis=0, concat_axis=0, tiled=True)  46.4 us
    dot_general x13, matrix products, dot(): return jnp.dot(left, right, preferred_element_type=jnp.float32)  40.6 us
    dot_general x4, matrix products, against_rows(): lax.dot_general(left, right, (((1,), (1,)), ((), ())), preferred_element_...  27.5 us
    dot_general x4, matrix products, rows_product(): lax.dot_general(left, right, (((0,), (0,)), ((), ())), preferred_element_...  23.5 us
    all_to_all x8, waiting for transfers between devices, exchange(): return lax.all_to_all(blocks, AXIS, split_axis=0, concat_axis=0, tiled=True)  18.1 us
  transfers between devices with their start and end apart: 9, of which 3 were waited for; matrix products, arithmetic and copies ran while one was open for 11% of the time, Pallas kernels for 40%

profile of v2, /device:TPU:29, one launch (start us, length us, event | category | flops | bytes accessed | tf_op | source)
XLA Modules:
  0.0 762.4 jit_solution(14713013695762871100)
XLA Ops:
  11.8 6.2 all-to-all-start
  21.5 9.8 %all-to-all-done = bf16[32,4,2176]{2,1,0:T(4,128)(2,1)S(1)} async-done(((bf16[32,4,2176]{2,1,0:T(4,128)(2,1)}), bf16[32,4,2176]{2,1,0:T(4,128)(2,1)S(1)}, u32[]{:S(2)}, u32[]{:S(2)}) %all-to-all-start) | async-done | bytes 557088 | tf_op jit(solution)/shard_map/all_to_all | solution.py:605
  35.0 6.1 all-to-all-start.1
  56.7 6.1 all-to-all-start.2
  62.8 75.5 %gather_rows.3 = bf16[32,80,2048]{2,1,0:T(8,128)(2,1)} custom-call(bf16[80,2048]{1,0:T(8,128)(2,1)} %multiply_convert_fusion.4.a_ref), custom_call_target="tpu_custom_call" | custom-call | tf_op jit(solution)/shard_map/gather_rows/pallas_call | solution.py:414
  145.5 8.5 %convolution_convert_fusion.4 = bf16[2560,192]{0,1:T(8,128)(2,1)} fusion(bf16[2560,2048]{1,0:T(8,128)(2,1)} %bitcast.94, bf16[2048,256]{1,0:T(8,128)(2,1)S(1)} %bitcast.106), kind=kOutput, calls=%fused_computation.18 | convolution fusion | flops 2013757440 | bytes 12517376 | tf_op jit(solution)/shard_map/dot_general | solution.py:609
  191.3 86.2 %scatter_rows.4 = f32[80,2048]{1,0:T(8,128)} custom-call(bf16[32,80,2048]{2,1,0:T(8,128)(2,1)} %bitcast.97), custom_call_target="tpu_custom_call" | custom-call | tf_op jit(solution)/shard_map/scatter_rows/pallas_call | solution.py:579
  281.0 54.5 %gather_rows.4 = bf16[32,80,2048]{2,1,0:T(8,128)(2,1)} custom-call(bf16[80,2048]{1,0:T(8,128)(2,1)} %multiply_convert_fusion.3.a_ref), custom_call_target="tpu_custom_call" | custom-call | tf_op jit(solution)/shard_map/gather_rows/pallas_call | solution.py:414
  335.6 8.0 %fusion.19 = f32[2560,320]{0,1:T(8,128)S(1)} fusion(bf16[2560,2048]{1,0:T(8,128)(2,1)} %bitcast.103, bf16[2048,256]{1,0:T(8,128)(2,1)} %bitcast.118, bf16[2048,64]{1,0:T(8,128)(2,1)} %slice.169), kind=kOutput, calls=%fused_computation.59 | convolution fusion | flops 3358064640 | bytes 15073280 | tf_op jit(solution)/shard_map/dot_general | solution.py:609
  343.6 5.5 fusion.18
  352.7 8.7 %convolution_convert_fusion.3 = bf16[2560,2048]{1,0:T(8,128)(2,1)} fusion(bf16[2560,160]{0,1:T(8,128)(2,1)S(1)} %get-tuple-element.95, bf16[2560,160]{0,1:T(8,128)(2,1)S(1)} %get-tuple-element.94, bf16[2048,256]{1,0:T(8,128)(2,1)S(1)} %bitcast.119, bf16[2048,64]{1,0:T(8,128)(2,1)S(1)} %copy-done.38), kind=kOutput, calls=%fused_computation.7 | convolution fusion | flops 3366584320 | bytes 13434880 | tf_op jit(solution)/shard_map/dot_general | solution.py:59
  363.9 59.4 %scatter_rows.5 = f32[80,2048]{1,0:T(8,128)} custom-call(bf16[32,80,2048]{2,1,0:T(8,128)(2,1)} %bitcast.105), custom_call_target="tpu_custom_call" | custom-call | tf_op jit(solution)/shard_map/scatter_rows/pallas_call | solution.py:579
  423.3 5.4 convolution_convert_fusion.1
  428.8 65.4 %scatter_rows.6 = f32[80,2048]{1,0:T(8,128)} custom-call(bf16[32,80,2048]{2,1,0:T(8,128)(2,1)} %bitcast.98), custom_call_target="tpu_custom_call" | custom-call | tf_op jit(solution)/shard_map/scatter_rows/pallas_call | solution.py:579
  501.7 6.0 all-to-all-start.4
  507.7 75.5 %gather_rows.5 = bf16[32,80,2048]{2,1,0:T(8,128)(2,1)} custom-call(bf16[80,2048]{1,0:T(8,128)(2,1)} %get-tuple-element.64.a_ref), custom_call_target="tpu_custom_call" | custom-call | tf_op jit(solution)/shard_map/gather_rows/pallas_call | solution.py:414
  583.2 7.8 %convolution_convert_fusion.5 = bf16[2560,64]{0,1:T(8,128)(2,1)S(1)} fusion(bf16[2560,2048]{1,0:T(8,128)(2,1)} %bitcast.92, bf16[64,2048]{1,0:T(8,128)(2,1)S(1)} %copy-done.32), kind=kOutput, calls=%fused_computation.19 | convolution fusion | flops 671252480 | bytes 11075584 | tf_op jit(solution)/shard_map/dot_general | solution.py:59
  614.4 6.3 convolution_convert_fusion.7
  620.7 5.5 convolution_convert_fusion
  637.2 65.7 %scatter_rows.7 = f32[80,2048]{1,0:T(8,128)} custom-call(bf16[32,80,2048]{2,1,0:T(8,128)(2,1)} %bitcast.96), custom_call_target="tpu_custom_call" | custom-call | tf_op jit(solution)/shard_map/scatter_rows/pallas_call | solution.py:579
  709.3 6.9 all-to-all-start.6
  725.3 6.9 fusion.110
  735.0 5.8 all-to-all-start.7
  740.8 6.8 fusion.109
  (277 shorter events, 148.3 us)
Async XLA Ops:
  7.2 336.4 %copy-start = (bf16[160,2048]{1,0:T(8,128)(2,1)S(1)}, bf16[160,2048]{1,0:T(8,128)(2,1)}, u32[]{:S(2)}) copy-start(bf16[160,2048]{1,0:T(8,128)(2,1)} %param.23) | copy-start | bytes 1966084
  11.8 19.5 %all-to-all-start = ((bf16[32,4,2176]{2,1,0:T(4,128)(2,1)}), bf16[32,4,2176]{2,1,0:T(4,128)(2,1)S(1)}, u32[]{:S(2)}, u32[]{:S(2)}) async-start(bf16[32,4,2176]{2,1,0:T(4,128)(2,1)} %pad_maximum_fusion.11), calls=%async_computation | async-start | bytes 1114112 | tf_op jit(solution)/shard_map/all_to_all | solution.py:605
  20.8 20.3 %copy-start.46 = (pred[128]{0:T(512)(128)(4,1)}, pred[128]{0:T(512)(128)(4,1)S(1)}, u32[]{:S(2)}) copy-start(pred[128]{0:T(512)(128)(4,1)S(1)} %iota_compare_fusion.12) | copy-start | bytes 388
  21.5 19.7 %copy-start.48 = (s32[128]{0:T(128)}, s32[128]{0:T(128)S(1)}, u32[]{:S(2)}) copy-start(s32[128]{0:T(128)S(1)} %and_select_fusion.4) | copy-start | bytes 1540
  32.9 12.6 %copy-start.6 = (bf16[64,2048]{1,0:T(8,128)(2,1)S(1)}, bf16[64,2048]{1,0:T(8,128)(2,1)}, u32[]{:S(2)}) copy-start(bf16[64,2048]{1,0:T(8,128)(2,1)} %value_ref.1) | copy-start | bytes 786436
  35.0 18.7 %all-to-all-start.1 = ((bf16[32,4,2048]{2,1,0:T(4,128)(2,1)}), bf16[32,4,2048]{2,1,0:T(4,128)(2,1)}, u32[]{:S(2)}, u32[]{:S(2)}) async-start(bf16[32,4,2048]{2,1,0:T(4,128)(2,1)} %reshape.460), calls=%async_computation.1 | async-start | bytes 1048576 | tf_op jit(solution)/shard_map/all_to_all | solution.py:605
  56.7 81.6 %all-to-all-start.2 = ((bf16[32,96,256]{2,1,0:T(8,128)(2,1)}), bf16[32,96,256]{2,1,0:T(8,128)(2,1)S(1)}, u32[]{:S(2)}, u32[]{:S(2)}) async-start(bf16[32,96,256]{2,1,0:T(8,128)(2,1)} %pad_maximum_fusion.1), calls=%async_computation.2 | async-start | bytes 3145728 | tf_op jit(solution)/shard_map/all_to_all | solution.py:605
  62.7 218.2 %all-gather.2.cloned.1.call-start = ((), (), s32[]{:S(2)}) async-start(), calls=%async_computation.8 | async-start | bytes 10813440 | tf_op jit(solution)/shard_map/all_gather | solution.py:802
  185.1 92.5 %all-to-all-start.3 = ((bf16[32,64,256]{2,1,0:T(8,128)(2,1)}), bf16[32,64,256]{2,1,0:T(8,128)(2,1)S(1)}, u32[]{:S(2)}, u32[]{:S(2)}) async-start(bf16[32,64,256]{2,1,0:T(8,128)(2,1)} %get-tuple-element.53), calls=%async_computation.3 | async-start | bytes 2097152 | tf_op jit(solution)/shard_map/all_to_all | solution.py:605
  190.2 304.0 %copy-start.54 = (s32[128]{0:T(128)}, s32[128]{0:T(128)S(1)}, u32[]{:S(2)}) copy-start(s32[128]{0:T(128)S(1)} %multiply_add_fusion) | copy-start | bytes 1540
  279.8 55.7 %copy-start.52 = (f32[80]{0:T(128)}, f32[80]{0:T(128)S(1)}, u32[]{:S(2)}) copy-start(f32[80]{0:T(128)S(1)} %get-tuple-element.122) | copy-start | bytes 964
  281.0 62.6 %slice-start = ((s8[10485760]{0:T(1024)(128)(4,1)}), s8[2097152]{0:T(1024)(128)(4,1)S(1)}, s32[]{:S(2)}) async-start(s8[10485760]{0:T(1024)(128)(4,1)} %bitcast.99), calls=%async_computation.9 | async-start | bytes 4194304
  363.9 59.4 %copy-start.18 = (bf16[2560,160]{0,1:T(8,128)(2,1)S(1)}, bf16[2560,160]{0,1:T(8,128)(2,1)}, u32[]{:S(2)}) copy-start(bf16[2560,160]{0,1:T(8,128)(2,1)} %get-tuple-element.81) | copy-start | bytes 2457604
  428.8 65.4 %copy-start.9 = (f32[80,2048]{1,0:T(8,128)S(1)}, f32[80,2048]{1,0:T(8,128)}, u32[]{:S(2)}) copy-start(f32[80,2048]{1,0:T(8,128)} %copy-done.8) | copy-start | bytes 1966084
  501.7 81.5 %all-to-all-start.4 = ((bf16[32,96,256]{2,1,0:T(8,128)(2,1)}), bf16[32,96,256]{2,1,0:T(8,128)(2,1)S(1)}, u32[]{:S(2)}, u32[]{:S(2)}) async-start(bf16[32,96,256]{2,1,0:T(8,128)(2,1)} %pad_maximum_fusion.3), calls=%async_computation.4 | async-start | bytes 3145728 | tf_op jit(solution)/shard_map/all_to_all | solution.py:605
  507.7 75.5 %copy-start.32 = (bf16[64,2048]{1,0:T(8,128)(2,1)S(1)}, bf16[64,2048]{1,0:T(8,128)(2,1)}, u32[]{:S(2)}) copy-start(bf16[64,2048]{1,0:T(8,128)(2,1)} %param.20) | copy-start | bytes 786436
  627.6 75.3 %all-to-all-start.5 = ((bf16[32,64,256]{2,1,0:T(8,128)(2,1)}), bf16[32,64,256]{2,1,0:T(8,128)(2,1)S(1)}, u32[]{:S(2)}, u32[]{:S(2)}) async-start(bf16[32,64,256]{2,1,0:T(8,128)(2,1)} %bitcast.35), calls=%async_computation.5 | async-start | bytes 2097152 | tf_op jit(solution)/shard_map/all_to_all | solution.py:605
  637.2 65.8 %copy-start.51 = (f32[80]{0:T(128)S(1)}, f32[80]{0:T(128)}, u32[]{:S(2)}) copy-start(f32[80]{0:T(128)} %copy-done.50) | copy-start | bytes 964
  637.2 67.2 %copy-start.24 = (f32[80,2048]{1,0:T(8,128)S(1)}, f32[80,2048]{1,0:T(8,128)}, u32[]{:S(2)}) copy-start(f32[80,2048]{1,0:T(8,128)} %get-tuple-element.91) | copy-start | bytes 1966084
  637.2 67.2 %copy-start.55 = (s32[128]{0:T(128)S(1)}, s32[128]{0:T(128)}, u32[]{:S(2)}) copy-start(s32[128]{0:T(128)} %copy-done.54) | copy-start | bytes 1540
  637.2 67.2 %copy-start.56 = (f32[80]{0:T(128)S(1)}, f32[80]{0:T(128)}, u32[]{:S(2)}) copy-start(f32[80]{0:T(128)} %get-tuple-element.119) | copy-start | bytes 964
  709.3 22.9 %all-to-all-start.6 = ((bf16[32,4,2176]{2,1,0:T(4,128)(2,1)}), bf16[32,4,2176]{2,1,0:T(4,128)(2,1)}, u32[]{:S(2)}, u32[]{:S(2)}) async-start(bf16[32,4,2176]{2,1,0:T(4,128)(2,1)} %pad_maximum_fusion.12), calls=%async_computation.6 | async-start | bytes 1114112 | tf_op jit(solution)/shard_map/all_to_all | solution.py:605
  735.0 18.4 %all-to-all-start.7 = ((bf16[32,4,2048]{2,1,0:T(4,128)(2,1)}), bf16[32,4,2048]{2,1,0:T(4,128)(2,1)S(1)}, u32[]{:S(2)}, u32[]{:S(2)}) async-start(bf16[32,4,2048]{2,1,0:T(4,128)(2,1)} %reshape.491), calls=%async_computation.7 | async-start | bytes 1048576 | tf_op jit(solution)/shard_map/all_to_all | solution.py:605
  740.8 14.3 %copy-start.1 = (bf16[160,2048]{1,0:T(8,128)(2,1)S(1)}, bf16[160,2048]{1,0:T(8,128)(2,1)}, u32[]{:S(2)}) copy-start(bf16[160,2048]{1,0:T(8,128)(2,1)} %param.23) | copy-start | bytes 1966084
  (48 other events, 264.1 us)
Sparse Core Ops, SparseCore 0:
  141.6 111.8 all-gather.1

commit v3 on v2

--- a/solution.py
+++ b/solution.py
@@ -408,7 +408,7 @@
             pl.when(when)(finish)
 
 
-def gather(block, cid=0):
+def gather(block):
     rows, width = block.shape
     n_sends = 10 + 3 * 2 * 4 + 4 * 2 * 2 + 8 * 2
     return pl.pallas_call(
@@ -422,15 +422,17 @@
             pltpu.SemaphoreType.DMA((2, 32)),
         ],
         name="gather_rows",
-        compiler_params=pltpu.CompilerParams(collective_id=cid, has_side_effects=True),
+        compiler_params=pltpu.CompilerParams(collective_id=0, has_side_effects=True),
     )(block)
 
 
-def scatter_kernel(p_ref, o_ref, m_ref, s_ref, first_ref, second_ref, za_ref, zb_ref,
-                   lsem, ssem, csem, fsem, gsem, zasem, zbsem):
+def scatter_kernel(given, *refs):
+    p_refs, o_refs, refs = refs[:given], refs[given : 2 * given], refs[2 * given :]
+    m_ref, s_ref, first_ref, second_ref, za_ref, zb_ref = refs[:6]
+    lsem, ssem, csem, fsem, gsem, zasem, zbsem = refs[6:]
     me, c, x, y, z = place()
-    rows, width = o_ref.shape
-    half = width // 2
+    rows, width = o_refs[0].shape
+    half = given * width // 2
     mid = (z == 1) | (z == 2)
     end = jnp.logical_not(mid)
     z1, z2, z3 = z + 1 - 2 * (z % 2), 2 - z // 2, 3 - 3 * (z // 2)
@@ -469,18 +471,24 @@
         lax.fori_loop(0, rows // 16, step, 0)
 
     plane = (me, nx, ny, diag)
-    order = [(q, j) for q in (3, 1, 2, 0) for j in (3, 2, 1, 0)]
-    for q, j in order:
-        b = plane[q] + 8 * (zs[j] - z)
-        slot = q * 4 + zs[j]
-        pltpu.make_async_copy(p_ref.at[b], m_ref.at[slot], lsem.at[slot]).start()
-        push(p_ref.at[b + nc - me], s_ref.at[slot], csem.at[slot], nc)
+    def pair_exchange(j):
+        for q in (3, 2, 1, 0):
+            b = plane[q] + 8 * (zs[j] - z)
+            slot = q * 4 + zs[j]
+            for i, p_ref in enumerate(p_refs):
+                own = pl.ds(i * width, width)
+                push(p_ref.at[b + nc - me], s_ref.at[slot, :, own], csem.at[i, slot], nc)
+                pltpu.make_async_copy(p_ref.at[b], m_ref.at[slot, :, own], lsem.at[i, slot]).start()
+
+    pair_exchange(3)
     first_peer, second_peer = (ny, nx), (nx, ny)
 
     def joined(q, j):
         slot = q * 4 + zs[j]
-        pltpu.make_async_copy(p_ref.at[0], m_ref.at[slot], lsem.at[slot]).wait()
-        arrive(s_ref.at[slot], csem.at[slot])
+        for i, p_ref in enumerate(p_refs):
+            own = pl.ds(i * width, width)
+            pltpu.make_async_copy(p_ref.at[0], m_ref.at[slot, :, own], lsem.at[i, slot]).wait()
+            arrive(s_ref.at[slot, :, own], csem.at[i, slot])
         add_into(m_ref.at[slot], s_ref.at[slot])
 
     def to_first(part, q, j):
@@ -488,16 +496,18 @@
         push(m_ref.at[q * 4 + zs[j], :, cols[part]], first_ref.at[part, far + zs[j]],
              fsem.at[part, far + zs[j]], first_peer[part])
 
-    for j in (3, 2, 1, 0):
+    def first_stage(j):
         joined(3, j)
+        if j:
+            pair_exchange(j - 1)
         to_first(0, 3, j)
         to_first(1, 3, j)
-    for j in (3, 2, 1, 0):
         joined(2, j)
         to_first(0, 2, j)
         joined(1, j)
         to_first(1, 1, j)
-    for j in (3, 2, 1, 0):
+
+    def second_stage(j):
         for part in (0, 1):
             arrive(first_ref.at[part, 4 + zs[j]], fsem.at[part, 4 + zs[j]])
             q = (1, 2)[part]
@@ -512,38 +522,35 @@
         arrive(second_ref.at[part, zs[j]], gsem.at[part, zs[j]])
         add_into(m, first_ref.at[part, zs[j]], second_ref.at[part, zs[j]])
         return m
-    for part in (0, 1):
-        pass
-    for j in (3, 2, 1, 0):
+
+    def z_send(j):
         for part in (0, 1):
             m = plane_sum(part, j)
-            if j == 3:
-                push(m, za_ref.at[part, 0], zasem.at[part, 0], n1, end)
-
-                @pl.when(mid)
-                def _():
-                    arrive(za_ref.at[part, 0], zasem.at[part, 0])
-                    add_into(m, za_ref.at[part, 0])
-                push(m, zb_ref.at[part, 0], zbsem.at[part, 0], n2, mid)
-            elif j == 2:
-                push(m, za_ref.at[part, 1], zasem.at[part, 1], n1, end)
-
-                @pl.when(mid)
-                def _():
-                    arrive(za_ref.at[part, 1], zasem.at[part, 1])
-                    add_into(m, za_ref.at[part, 1])
-                push(m, zb_ref.at[part, 1], zbsem.at[part, 1], n2, mid)
-            elif j == 1:
-                push(m, za_ref.at[part, 2], zasem.at[part, 2], n1, end)
-
-                @pl.when(mid)
-                def _():
-                    arrive(zb_ref.at[part, 0], zbsem.at[part, 0])
-                    add_into(m, zb_ref.at[part, 0])
-                push(m, zb_ref.at[part, 0], zbsem.at[part, 0], n1, mid)
+            if j:
+                push(m, za_ref.at[part, 3 - j], zasem.at[part, 3 - j], n1, end)
+
+    def z_relay(j):
+        for part in (0, 1):
+            m = m_ref.at[zs[j], :, cols[part]]
+            came, sem = (za_ref, zasem) if j > 1 else (zb_ref, zbsem)
+            slot = 3 - j if j > 1 else 0
+
+            @pl.when(mid)
+            def _():
+                arrive(came.at[part, slot], sem.at[part, slot])
+                add_into(m, came.at[part, slot])
+            out = 3 - j if j > 1 else 0
+            push(m, zb_ref.at[part, out], zbsem.at[part, out], n2 if j > 1 else n1, mid)
+
+    stages = (first_stage, second_stage, z_send, z_relay)
+    for step in range(4 + len(stages) - 1):
+        for stage, what in enumerate(stages):
+            j = 3 - (step - stage)
+            if 0 <= j <= 3 and not (what is z_relay and j == 0):
+                what(j)
     for part in (0, 1):
         m = m_ref.at[zs[0], :, cols[part]]
-        o = o_ref.at[:, cols[part]]
+        o = o_refs[part] if given == 2 else o_refs[0].at[:, cols[part]]
 
         def total(*more):
             def step(i, _):
@@ -572,33 +579,715 @@
             pl.when(when)(finish)
 
 
-def scatter(parts, cid=1):
-    n, rows, width = parts.shape
-    dt = parts.dtype
-    half = width // 2
-    return pl.pallas_call(
-        scatter_kernel,
-        out_shape=jax.ShapeDtypeStruct((rows, width), jnp.float32),
-        in_specs=[pl.BlockSpec(memory_space=pl.ANY)],
-        out_specs=pl.BlockSpec(memory_space=pltpu.VMEM),
+def scatter(*partials):
+    given = len(partials)
+    n, rows, width = partials[0].shape
+    kind = partials[0].dtype
+    whole, half = given * width, given * width // 2
+    sums = pl.pallas_call(
+        functools.partial(scatter_kernel, given),
+        out_shape=[jax.ShapeDtypeStruct((rows, width), jnp.float32)] * given,
+        in_specs=[pl.BlockSpec(memory_space=pl.ANY)] * given,
+        out_specs=[pl.BlockSpec(memory_space=pltpu.VMEM)] * given,
         scratch_shapes=[
-            pltpu.VMEM((16, rows, width), dt),
-            pltpu.VMEM((16, rows, width), dt),
-            pltpu.VMEM((2, 8, rows, half), dt),
-            pltpu.VMEM((2, 4, rows, half), dt),
-            pltpu.VMEM((2, 3, rows, half), dt),
-            pltpu.VMEM((2, 2, rows, half), dt),
-            pltpu.SemaphoreType.DMA((16,)),
-            pltpu.SemaphoreType.DMA((16 + 16 + 8 + 12,)),
-            pltpu.SemaphoreType.DMA((16,)),
+            pltpu.VMEM((16, rows, whole), kind),
+            pltpu.VMEM((16, rows, whole), kind),
+            pltpu.VMEM((2, 8, rows, half), kind),
+            pltpu.VMEM((2, 4, rows, half), kind),
+            pltpu.VMEM((2, 3, rows, half), kind),
+            pltpu.VMEM((2, 2, rows, half), kind),
+            pltpu.SemaphoreType.DMA((given, 16)),
+            pltpu.SemaphoreType.DMA((16 * given + 36,)),
+            pltpu.SemaphoreType.DMA((given, 16)),
             pltpu.SemaphoreType.DMA((2, 8)),
             pltpu.SemaphoreType.DMA((2, 4)),
             pltpu.SemaphoreType.DMA((2, 3)),
             pltpu.SemaphoreType.DMA((2, 2)),
         ],
         name="scatter_rows",
-        compiler_params=pltpu.CompilerParams(collective_id=cid, has_side_effects=True, vmem_limit_bytes=56 * 2**20),
-    )(parts)
+        compiler_params=pltpu.CompilerParams(
+            collective_id=given, has_side_effects=True, vmem_limit_bytes=56 * 2**20
+        ),
+    )(*partials)
+    return sums if given > 1 else sums[0]
+
+
+def over(left, right, left_dim=1, right_dim=0):
+    return lax.dot_general(
+        left, right, (((left_dim,), (right_dim,)), ((), ())), preferred_element_type=jnp.float32
+    )
+
+
+def low(values):
+    return values.astype(jnp.bfloat16)
+
+
+def tile_probs(query, key, bias, same):
+    scores = jnp.where(same, over(query, key, 1, 1) + bias, masked_score)
+    grown = jnp.exp(scores - jnp.max(scores, axis=-1, keepdims=True))
+    return grown / jnp.sum(grown, axis=-1, keepdims=True)
+
+
+def attend_kernel(
+    groups, x_ref, w_ref, wo_ref, perm_ref, bias_ref, col_ref, row_ref, qkv_ref, att_ref, part_ref
+):
+    step = pl.program_id(0)
+    length = bias_ref.shape[0]
+    head = wo_ref.shape[0]
+    size = perm_ref.shape[0]
+    perm = perm_ref[...]
+
+    @pl.when(step == 0)
+    def _():
+        qkv_ref[:length, :] = jnp.zeros_like(qkv_ref[:length, :])
+        qkv_ref[length + groups * size :, :] = jnp.zeros_like(qkv_ref[:length, :])
+
+    @pl.when(step < groups)
+    def _():
+        rows = low(over(x_ref[...].reshape(size, -1), w_ref[...]))
+        at = pl.multiple_of(length + step * size, length)
+        qkv_ref[pl.ds(at, size), :] = low(over(perm, rows))
+
+    @pl.when(step > 0)
+    def _():
+        attended = []
+        for tile in range(size // length):
+            base = pl.multiple_of((step - 1) * size + tile * length, length)
+            query = qkv_ref[pl.ds(base + length, length), :head]
+            key = qkv_ref[pl.ds(base, 3 * length), head : 2 * head]
+            value = qkv_ref[pl.ds(base, 3 * length), 2 * head :]
+            same = col_ref[pl.ds(base, length), :] == row_ref[:, pl.ds(base, 3 * length)]
+            probs = tile_probs(query, key, bias_ref[...], same)
+            attended.append(low(over(low(probs), value)))
+        rows = low(over(perm, jnp.concatenate(attended, axis=0), 0, 0))
+        att_ref[...] = rows.reshape(att_ref.shape)
+        part_ref[...] = low(over(rows, wo_ref[...])).reshape(part_ref.shape)
+
+
+def attend(x_all, w, wo, perm, bias, col, row):
+    count, slots, width = x_all.shape
+    head, length, size = wo.shape[0], bias.shape[0], perm.shape[0]
+    grain = size // count
+    groups = slots // grain
+
+    def now(i):
+        return (0, jnp.minimum(i, groups - 1), 0)
+
+    def late(i):
+        return (0, jnp.maximum(i - 1, 0), 0)
+
+    def whole(array):
+        return pl.BlockSpec(array.shape, lambda i: (0,) * array.ndim)
+
+    qkv_shape = ((groups * size + 2 * length), 3 * head)
+    return pl.pallas_call(
+        functools.partial(attend_kernel, groups),
+        grid=(groups + 1,),
+        out_shape=[
+            jax.ShapeDtypeStruct(qkv_shape, jnp.bfloat16),
+            jax.ShapeDtypeStruct((count, slots, head), jnp.bfloat16),
+            jax.ShapeDtypeStruct((count, slots, width), jnp.bfloat16),
+        ],
+        in_specs=[pl.BlockSpec((count, grain, width), now)]
+        + [whole(array) for array in (w, wo, perm, bias, col, row)],
+        out_specs=[
+            pl.BlockSpec(qkv_shape, lambda i: (0, 0)),
+            pl.BlockSpec((count, grain, head), late),
+            pl.BlockSpec((count, grain, width), late),
+        ],
+        name="attend",
+        compiler_params=pltpu.CompilerParams(vmem_limit_bytes=56 * 2**20),
+    )(x_all, w, wo, perm, bias, col, row)
+
+
+def attend_back_kernel(
+    groups, d_ref, x_ref, att_ref, qkv_ref, w_ref, wo_ref, perm_ref, bias_ref, col_ref, row_ref,
+    part_ref, wo_grad_ref, w_grad_ref, bias_grad_ref, dq_ref, dk_ref, dv_ref,
+):
+    step = pl.program_id(0)
+    length = bias_ref.shape[0]
+    head = wo_ref.shape[0]
+    size = perm_ref.shape[0]
+    perm = perm_ref[...]
+
+    @pl.when(step == 0)
+    def _():
+        for ref in (wo_grad_ref, w_grad_ref, bias_grad_ref, dk_ref, dv_ref):
+            ref[...] = jnp.zeros_like(ref)
+
+    @pl.when(step < groups)
+    def _():
+        d_branch = d_ref[...].reshape(size, -1)
+        wo_grad_ref[...] += over(att_ref[...].reshape(size, head), d_branch, 0, 0)
+        d_attended = low(over(perm, low(over(d_branch, wo_ref[...], 1, 1))))
+        for tile in range(size // length):
+            base = pl.multiple_of(step * size + tile * length, length)
+            query = qkv_ref[pl.ds(base + length, length), :head]
+            key = qkv_ref[pl.ds(base, 3 * length), head : 2 * head]
+            value = qkv_ref[pl.ds(base, 3 * length), 2 * head :]
+            same = col_ref[pl.ds(base, length), :] == row_ref[:, pl.ds(base, 3 * length)]
+            probs = tile_probs(query, key, bias_ref[...], same)
+            d_out = d_attended[tile * length : (tile + 1) * length, :]
+            d_probs = over(d_out, value, 1, 1)
+            inner = jnp.sum(probs * d_probs, axis=-1, keepdims=True)
+            d_scores = low(probs * (d_probs - inner))
+            bias_grad_ref[...] += d_scores.astype(jnp.float32)
+            dq_ref[pl.ds(base + length, length), :] = over(d_scores, key)
+            dk_ref[pl.ds(base, 3 * length), :] += over(d_scores, query, 0, 0)
+            dv_ref[pl.ds(base, 3 * length), :] += over(low(probs), d_out, 0, 0)
+
+    @pl.when(step > 0)
+    def _():
+        at = pl.multiple_of(length + (step - 1) * size, length)
+        rows = jnp.concatenate([low(ref[pl.ds(at, size), :]) for ref in (dq_ref, dk_ref, dv_ref)], axis=1)
+        rows = low(over(perm, rows, 0, 0))
+        w_grad_ref[...] += over(rows, x_ref[...].reshape(size, -1), 0, 0)
+        part_ref[...] = low(over(rows, w_ref[...], 1, 1)).reshape(part_ref.shape)
+
+
+def attend_back(d_all, x_all, att, qkv, w, wo, perm, bias, col, row):
+    count, slots, width = x_all.shape
+    head, length, size = wo.shape[0], bias.shape[0], perm.shape[0]
+    grain = size // count
+    groups = slots // grain
+
+    def now(i):
+        return (0, jnp.minimum(i, groups - 1), 0)
+
+    def late(i):
+        return (0, jnp.maximum(i - 1, 0), 0)
+
+    def whole(shape):
+        return pl.BlockSpec(shape, lambda i: (0,) * len(shape))
+
+    grads = [(head, width), (3 * head, width), bias.shape]
+    return pl.pallas_call(
+        functools.partial(attend_back_kernel, groups),
+        grid=(groups + 1,),
+        out_shape=[jax.ShapeDtypeStruct((count, slots, width), jnp.bfloat16)]
+        + [jax.ShapeDtypeStruct(shape, jnp.float32) for shape in grads],
+        in_specs=[
+            pl.BlockSpec((count, grain, width), now),
+            pl.BlockSpec((count, grain, width), late),
+            pl.BlockSpec((count, grain, head), now),
+        ]
+        + [whole(array.shape) for array in (qkv, w, wo, perm, bias, col, row)],
+        out_specs=[pl.BlockSpec((count, grain, width), late)] + [whole(shape) for shape in grads],
+        scratch_shapes=[pltpu.VMEM((qkv.shape[0], head), jnp.float32)] * 3,
+        name="attend_back",
+        compiler_params=pltpu.CompilerParams(vmem_limit_bytes=56 * 2**20),
+    )(d_all, x_all, att, qkv, w, wo, perm, bias, col, row)
+
+
+def feed_kernel(x_ref, up_ref, w_ref, wd_ref, back_ref, down_ref, w_grad_ref, wd_grad_ref):
+    units = wd_ref.shape[0]
+
+    @pl.when(pl.program_id(0) == 0)
+    def _():
+        w_grad_ref[...] = jnp.zeros_like(w_grad_ref)
+        wd_grad_ref[...] = jnp.zeros_like(wd_grad_ref)
+
+    x, upstream = x_ref[...], up_ref[...]
+    both = over(x, w_ref[...])
+    gate, up = both[:, :units], both[:, units:]
+    d_hidden = over(upstream, wd_ref[...], 1, 1)
+    slope = 0.7978845608028654
+    squared = gate * gate
+    bent = jnp.tanh(slope * (gate + 0.044715 * gate * squared))
+    gelu = 0.5 * gate * (1.0 + bent)
+    d_gelu = 0.5 * (1.0 + bent) + 0.5 * gate * (1.0 - bent * bent) * slope * (
+        1.0 + 3.0 * 0.044715 * squared
+    )
+    hidden = low(gelu * up)
+    d_both = jnp.concatenate((low(d_hidden * up * d_gelu), low(d_hidden * gelu)), axis=1)
+    back_ref[...] = low(over(d_both, w_ref[...], 1, 1))
+    down_ref[...] = low(over(hidden, wd_ref[...]))
+    w_grad_ref[...] += over(d_both, x, 0, 0)
+    wd_grad_ref[...] += over(hidden, upstream, 0, 0)
+
+
+def feed(x_all, upstream_all, w, wd):
+    rows, width = x_all.shape
+    step = 512 if rows % 512 == 0 else rows
+    block = pl.BlockSpec((step, width), lambda i: (i, 0))
+
+    def whole(shape):
+        return pl.BlockSpec(shape, lambda i: (0, 0))
+
+    grads = [(w.shape[1], width), wd.shape]
+    return pl.pallas_call(
+        feed_kernel,
+        grid=(rows // step,),
+        out_shape=[jax.ShapeDtypeStruct((rows, width), jnp.bfloat16)] * 2
+        + [jax.ShapeDtypeStruct(shape, jnp.float32) for shape in grads],
+        in_specs=[block, block, whole(w.shape), whole(wd.shape)],
+        out_specs=[block, block] + [whole(shape) for shape in grads],
+        name="feed_forward_and_back",
+        compiler_params=pltpu.CompilerParams(vmem_limit_bytes=56 * 2**20),
+    )(x_all, upstream_all, w, wd)
+
+
+class Spot:
+    def __init__(self):
+        me = lax.axis_index(AXIS)
+        c, x, y, z = me % 2, (me // 2) % 2, (me // 4) % 2, me // 8
+        self.me = me
+        self.mid = (z == 1) | (z == 2)
+        self.end = jnp.logical_not(self.mid)
+        self.zs = (z, z + 1 - 2 * (z % 2), 2 - z // 2, 3 - 3 * (z // 2))
+        self.shift = [8 * (zz - z) for zz in self.zs]
+        self.core, self.x, self.y = me + 1 - 2 * c, me + 2 - 4 * x, me + 4 - 8 * y
+        self.diag = self.x + self.y - me
+        self.n1, self.n2 = me + self.shift[1], me + self.shift[2]
+
+    def greet(self):
+        bar = pltpu.get_barrier_semaphore()
+        for peer in (self.core, self.x, self.y, self.n1):
+            pl.semaphore_signal(bar, inc=1, device_id=(peer,), device_id_type=MESH)
+
+        @pl.when(self.mid)
+        def _():
+            pl.semaphore_signal(bar, inc=1, device_id=(self.n2,), device_id_type=MESH)
+
+        pl.semaphore_wait(bar, 4 + self.mid.astype(jnp.int32))
+
+
+class Sends:
+    def __init__(self, sems):
+        self.sems, self.used, self.open = sems, 0, []
+
+    def push(self, src, dst, rsem, peer, when=None):
+        ssem = self.sems.at[self.used]
+        self.used += 1
+
+        def copy():
+            return pltpu.make_async_remote_copy(
+                src, dst, ssem, rsem, device_id=(peer,), device_id_type=MESH
+            )
+
+        if when is None:
+            copy().start()
+        else:
+            pl.when(when)(lambda: copy().start())
+        self.open.append((lambda: copy().wait_send(), when))
+
+    def finish(self):
+        for wait, when in self.open:
+            if when is None:
+                wait()
+            else:
+                pl.when(when)(wait)
+        self.open = []
+
+
+def arrive(dst, rsem, spot):
+    pltpu.make_async_remote_copy(
+        dst, dst, rsem, rsem, device_id=(spot.core,), device_id_type=MESH
+    ).wait_recv()
+
+
+def gather_steps(spot, src, dst, rows, sends, rsem, own_sem):
+    half = src.shape[1] // 2
+    cols = (pl.ds(0, half), pl.ds(half, half))
+    me, mid, shift = spot.me, spot.mid, spot.shift
+    first, last = (spot.x, spot.y), (spot.y, spot.x)
+    own = pltpu.make_async_copy(src.at[rows, :], dst.at[me, rows, :], own_sem)
+    own.start()
+
+    def push(part, block, peer, mine=False, when=None):
+        there = dst.at[block, rows, cols[part]]
+        here = src.at[rows, cols[part]] if mine else there
+        sends.push(here, there, rsem.at[part, block], peer, when)
+
+    def landed(part, block):
+        arrive(dst.at[block, rows, cols[part]], rsem.at[part, block], spot)
+
+    for part in (0, 1):
+        push(part, me, spot.n1, True)
+        push(part, me, spot.n2, True, mid)
+        push(part, me, first[part], True)
+        push(part, me, last[part], True)
+    for part in (0, 1):
+        push(part, me, spot.core, True)
+    yield
+
+    def from_z(part, j):
+        b = me + shift[j]
+        landed(part, b)
+        push(part, b, spot.n2 if j == 1 else spot.n1, when=mid)
+        push(part, b, first[part])
+        push(part, b, last[part])
+        push(part, b, spot.core)
+
+    def from_first(part, j):
+        b = first[part] + shift[j]
+        landed(part, b)
+        push(part, b, last[part])
+        push(part, b, spot.core)
+
+    def from_last(part, b):
+        landed(part, b)
+        push(part, b, spot.core)
+
+    for j in range(4):
+        if j:
+            for part in (0, 1):
+                from_z(part, j)
+                yield
+        for part in (0, 1):
+            from_first(part, j)
+        yield
+        if j:
+            for part in (0, 1):
+                from_last(part, last[part] + shift[j - 1])
+            yield
+    for part in (0, 1):
+        from_last(part, last[part] + shift[3])
+    yield
+    for j in range(4):
+        for part in (0, 1):
+            from_last(part, spot.diag + shift[j])
+        yield
+    for j in range(4):
+        for base in (me, spot.x, spot.y, spot.diag):
+            for part in (0, 1):
+                landed(part, base + spot.core - me + shift[j])
+    own.wait()
+    yield
+
+
+def scatter_steps(spot, p_refs, o_refs, rows, bufs, sems, sends):
+    m_ref, s_ref, first_ref, second_ref, za_ref, zb_ref = bufs
+    lsem, csem, fsem, gsem, zasem, zbsem = sems
+    given = len(p_refs)
+    width = p_refs[0].shape[2]
+    half = given * width // 2
+    me, mid, end, zs = spot.me, spot.mid, spot.end, spot.zs
+    cols, short = (pl.ds(0, half), pl.ds(half, half)), pl.ds(0, half)
+    plane = (me, spot.x, spot.y, spot.diag)
+    first_peer, second_peer = (spot.y, spot.x), (spot.x, spot.y)
+    start, size = rows.start, rows.size
+
+    def mine(q, j, part):
+        return m_ref.at[q * 4 + zs[j], rows, cols[part]]
+
+    def held(ref, part, slot):
+        return ref.at[part, slot, rows, short]
+
+    def chunks(count, step):
+        lax.fori_loop(0, size // 16, lambda i, _: step(pl.ds(pl.multiple_of(start + i * 16, 16), 16)) or _, 0)
+
+    def add(q, j, part, *more):
+        def step(r):
+            v = m_ref[q * 4 + zs[j], r, cols[part]].astype(jnp.float32)
+            for ref, slot in more:
+                v = v + ref[part, slot, r, short].astype(jnp.float32)
+            m_ref[q * 4 + zs[j], r, cols[part]] = v.astype(m_ref.dtype)
+
+        chunks(size, step)
+
+    def pair_exchange(j):
+        for q in (3, 2, 1, 0):
+            b = plane[q] + spot.shift[j]
+            slot = q * 4 + zs[j]
+            for i, p_ref in enumerate(p_refs):
+                own = pl.ds(i * width, width)
+                sends.push(p_ref.at[b + spot.core - me, rows, :], s_ref.at[slot, rows, own], csem.at[i, slot], spot.core)
+                pltpu.make_async_copy(p_ref.at[b, rows, :], m_ref.at[slot, rows, own], lsem.at[i, slot]).start()
+
+    def joined(q, j):
+        slot = q * 4 + zs[j]
+        for i, p_ref in enumerate(p_refs):
+            own = pl.ds(i * width, width)
+            pltpu.make_async_copy(p_ref.at[0, rows, :], m_ref.at[slot, rows, own], lsem.at[i, slot]).wait()
+            arrive(s_ref.at[slot, rows, own], csem.at[i, slot], spot)
+        everything = pl.ds(0, given * width)
+
+        def step(r):
+            v = m_ref[slot, r, everything].astype(jnp.float32) + s_ref[slot, r, everything].astype(jnp.float32)
+            m_ref[slot, r, everything] = v.astype(m_ref.dtype)
+
+        chunks(size, step)
+
+    def to_first(part, q, j):
+        slot = (4 if q == 3 else 0) + zs[j]
+        sends.push(mine(q, j, part), held(first_ref, part, slot), fsem.at[part, slot], first_peer[part])
+
+    def first_stage(j):
+        joined(3, j)
+        if j:
+            pair_exchange(j - 1)
+        to_first(0, 3, j)
+        to_first(1, 3, j)
+        joined(2, j)
+        to_first(0, 2, j)
+        joined(1, j)
+        to_first(1, 1, j)
+
+    def second_stage(j):
+        for part in (0, 1):
+            q, slot = (1, 2)[part], 4 + zs[j]
+            arrive(held(first_ref, part, slot), fsem.at[part, slot], spot)
+            add(q, j, part, (first_ref, slot))
+            sends.push(mine(q, j, part), held(second_ref, part, zs[j]), gsem.at[part, zs[j]], second_peer[part])
+        joined(0, j)
+
+    def z_send(j):
+        for part in (0, 1):
+            arrive(held(first_ref, part, zs[j]), fsem.at[part, zs[j]], spot)
+            arrive(held(second_ref, part, zs[j]), gsem.at[part, zs[j]], spot)
+            add(0, j, part, (first_ref, zs[j]), (second_ref, zs[j]))
+            if j:
+                sends.push(mine(0, j, part), held(za_ref, part, 3 - j), zasem.at[part, 3 - j], spot.n1, end)
+
+    def z_relay(j):
+        if not j:
+            return
+        for part in (0, 1):
+            came, sem, slot = (za_ref, zasem, 3 - j) if j > 1 else (zb_ref, zbsem, 0)
+
+            @pl.when(mid)
+            def _():
+                arrive(held(came, part, slot), sem.at[part, slot], spot)
+                add(0, j, part, (came, slot))
+
+            slot = 3 - j if j > 1 else 0
+            peer = spot.n2 if j > 1 else spot.n1
+            sends.push(mine(0, j, part), held(zb_ref, part, slot), zbsem.at[part, slot], peer, mid)
+
+    pair_exchange(3)
+    stages = (first_stage, second_stage, z_send, z_relay)
+    for step in range(4 + len(stages) - 1):
+        for stage, what in enumerate(stages):
+            j = 3 - (step - stage)
+            if 0 <= j <= 3:
+                what(j)
+                yield
+    for part in (0, 1):
+        o_ref, there = (o_refs[part], pl.ds(0, half)) if given == 2 else (o_refs[0], cols[part])
+
+        def total(*more):
+            def step(r):
+                v = m_ref[zs[0], r, cols[part]].astype(jnp.float32)
+                for ref, slot in more:
+                    v = v + ref[part, slot, r, short].astype(jnp.float32)
+                o_ref[r, there] = v
+
+            chunks(size, step)
+
+        @pl.when(mid)
+        def _():
+            arrive(held(za_ref, part, 2), zasem.at[part, 2], spot)
+            arrive(held(zb_ref, part, 1), zbsem.at[part, 1], spot)
+            total((za_ref, 2), (zb_ref, 1))
+
+        @pl.when(end)
+        def _():
+            arrive(held(zb_ref, part, 0), zbsem.at[part, 0], spot)
+            total((zb_ref, 0))
+
+    yield
+
+
+def weave(tasks):
+    ended, clocks, left = {}, {}, dict(tasks)
+    while left:
+        best = None
+        for name, (after, delay, pace, _) in left.items():
+            if any(other not in ended for other in after):
+                continue
+            at = clocks.get(name, max([ended[other] for other in after], default=0.0) + delay)
+            if best is None or at < best[0]:
+                best = (at, name)
+        at, name = best
+        _, _, pace, steps = left[name]
+        try:
+            next(steps)
+            clocks[name] = at + pace
+        except StopIteration:
+            ended[name] = at
+            del left[name]
+
+
+N_GATHER_SENDS = 66
+FEED_BLOCKS = 8
+
+
+def middle_kernel(cuts, *refs):
+    part_ref, rows_ref, up_ref, gain_ref, w_ref, wd_ref = refs[:6]
+    d_all_ref, result_ref, d_mid_ref, gain_grad_ref, w_grad_ref, wd_grad_ref = refs[6:12]
+    up_all_ref, x_all_ref, back_ref, forth_ref = refs[12:16]
+    branch_ref, middle_ref, x_ref, dn_ref, down_ref, d_ref = refs[16:22]
+    bufs = refs[22:28]
+    x_in, up_in, back_out, forth_out = refs[28:32]
+    own_sem, g_ssem, g_rsem, feed_sem = refs[32:36]
+    one_sems, two_sems = refs[36:43], refs[43:50]
+    spot = Spot()
+    spot.greet()
+    width = rows_ref.shape[1]
+    units = wd_ref.shape[0]
+    count = part_ref.shape[0]
+    ranges = [pl.ds(a, b - a) for a, b in zip(cuts[:-1], cuts[1:])]
+    everything = pl.ds(0, cuts[-1])
+    w_grad_ref[...] = jnp.zeros_like(w_grad_ref)
+    wd_grad_ref[...] = jnp.zeros_like(wd_grad_ref)
+    gain_grad_ref[...] = jnp.zeros_like(gain_grad_ref)
+    sends = {}
+
+    def rows_of(rows):
+        return [pl.ds(rows.start + i, 16) for i in range(0, rows.size, 16)]
+
+    def scale_of(v):
+        return lax.rsqrt(jnp.sum(v * v, axis=1, keepdims=True) / width + EPSILON)
+
+    def gathering(name, at, src, dst, rows):
+        sends[name] = Sends(g_ssem.at[at])
+        yield from gather_steps(spot, src, dst, rows, sends[name], g_rsem.at[at], own_sem.at[at])
+
+    def scattering(name, p_refs, o_refs, rows, sems, at, before=()):
+        for other in before:
+            sends[other].finish()
+        sends[name] = Sends(sems[0].at[at])
+        yield from scatter_steps(spot, p_refs, o_refs, rows, bufs, [sem.at[at] for sem in sems[1:]], sends[name])
+
+    def first_norm(rows):
+        for r in rows_of(rows):
+            v = rows_ref[r, :].astype(jnp.float32) + branch_ref[r, :]
+            middle_ref[r, :] = v
+            x_ref[r, :] = (v * scale_of(v) * gain_ref[...]).astype(x_ref.dtype)
+        yield
+
+    def norm_back_rows(rows):
+        for r in rows_of(rows):
+            v, d, gain = middle_ref[r, :], dn_ref[r, :], gain_ref[...]
+            scale = scale_of(v)
+            result_ref[r, :] = (v + down_ref[r, :]).astype(result_ref.dtype)
+            gain_grad_ref[...] += jnp.sum(d * v * scale, axis=0, keepdims=True)
+            w = gain * d
+            mean = jnp.sum(w * v, axis=1, keepdims=True) / width
+            d_mid = up_ref[r, :].astype(jnp.float32) + scale * w - v * (scale * scale * scale) * mean
+            d_mid_ref[r, :] = d_mid
+            d_ref[r, :] = d_mid.astype(d_ref.dtype)
+        yield
+
+    def feeding(rows):
+        size = rows.size
+        steps = count // FEED_BLOCKS
+        deep = pl.ds(0, size)
+
+        def fetch(step, slot):
+            blocks = pl.ds(step * FEED_BLOCKS, FEED_BLOCKS)
+            return [
+                pltpu.make_async_copy(ref.at[blocks, rows, :], to.at[slot, :, deep, :], feed_sem.at[i, slot])
+                for i, (ref, to) in enumerate(((x_all_ref, x_in), (up_all_ref, up_in)))
+            ]
+
+        def store(step):
+            blocks = pl.ds(step * FEED_BLOCKS, FEED_BLOCKS)
+            return [
+                pltpu.make_async_copy(of.at[:, deep, :], ref.at[blocks, rows, :], feed_sem.at[2 + i, 0])
+                for i, (ref, of) in enumerate(((back_ref, back_out), (forth_ref, forth_out)))
+            ]
+
+        for copy in fetch(0, 0):
+            copy.start()
+        for step in range(steps):
+            slot = step % 2
+            if step + 1 < steps:
+                for copy in fetch(step + 1, 1 - slot):
+                    copy.start()
+            for copy in fetch(step, slot):
+                copy.wait()
+            x = x_in[slot, :, :size, :].reshape(-1, width)
+            upstream = up_in[slot, :, :size, :].reshape(-1, width)
+            both = over(x, w_ref[...])
+            gate, up = both[:, :units], both[:, units:]
+            d_hidden = over(upstream, wd_ref[...], 1, 1)
+            gelu, d_gelu = gelu_pair(gate)
+            hidden = low(gelu * up)
+            d_both = jnp.concatenate((low(d_hidden * up * d_gelu), low(d_hidden * gelu)), axis=1)
+            if step:
+                for copy in store(step - 1):
+                    copy.wait()
+            shape = (FEED_BLOCKS, size, width)
+            back_out[:, :size, :] = low(over(d_both, w_ref[...], 1, 1)).reshape(shape)
+            forth_out[:, :size, :] = low(over(hidden, wd_ref[...])).reshape(shape)
+            for copy in store(step):
+                copy.start()
+            w_grad_ref[...] += over(d_both, x, 0, 0)
+            wd_grad_ref[...] += over(hidden, upstream, 0, 0)
+            yield
+        for copy in store(steps - 1):
+            copy.wait()
+        yield
+
+    tasks = {"up": ([], 12.0, 2.0, gathering("up", 0, up_ref, up_all_ref, everything))}
+    for i, rows in enumerate(ranges):
+        h, k = str(i), len(ranges)
+        earlier = [f"feed{i - 1}"] if i else []
+        tasks |= {
+            "one" + h: ([], 7.0 * i, 2.0, scattering("one" + h, (part_ref,), (branch_ref,), rows, one_sems, i)),
+            "norm" + h: (["one" + h], 0.0, 0.5, first_norm(rows)),
+            "x" + h: (["norm" + h], 0.0, 1.2, gathering("x" + h, 1 + i, x_ref, x_all_ref, rows)),
+            "feed" + h: (["x" + h, "up"] + earlier, 0.0, 4.0, feeding(rows)),
+            "two" + h: (
+                ["feed" + h], 0.0, 3.0,
+                scattering("two" + h, (back_ref, forth_ref), (dn_ref, down_ref), rows, two_sems, i, ["one" + h]),
+            ),
+            "back" + h: (["two" + h], 0.0, 0.5, norm_back_rows(rows)),
+            "d" + h: (["back" + h], 0.0, 1.2, gathering("d" + h, 1 + k + i, d_ref, d_all_ref, rows)),
+        }
+    weave(tasks)
+    for some in sends.values():
+        some.finish()
+
+
+def gelu_pair(gate):
+    slope = 0.7978845608028654
+    squared = gate * gate
+    bent = jnp.tanh(slope * (gate + 0.044715 * gate * squared))
+    gelu = 0.5 * gate * (1.0 + bent)
+    return gelu, 0.5 * (1.0 + bent) + 0.5 * gate * (1.0 - bent * bent) * slope * (1.0 + 3.0 * 0.044715 * squared)
+
+
+def middle_part(partial, rows_low, upstream_low, gain, w, wd):
+    count, rows, width = partial.shape
+    cuts = (0, 48, 80) if rows == 80 else (0, rows)
+    halves = len(cuts) - 1
+    deep = max(b - a for a, b in zip(cuts[:-1], cuts[1:]))
+    low_rows, all_rows = (rows, width), (count, rows, width)
+    bf, wide, dma = jnp.bfloat16, jnp.float32, pltpu.SemaphoreType.DMA
+
+    def scatter_sems(given):
+        return [
+            dma((halves, 16 * given + 36)), dma((halves, given, 16)), dma((halves, given, 16)), dma((halves, 2, 8)),
+            dma((halves, 2, 4)), dma((halves, 2, 3)), dma((halves, 2, 2)),
+        ]
+
+    vmem, hbm = pl.BlockSpec(memory_space=pltpu.VMEM), pl.BlockSpec(memory_space=pl.ANY)
+    shape = jax.ShapeDtypeStruct
+    outs = pl.pallas_call(
+        functools.partial(middle_kernel, cuts),
+        out_shape=[
+            shape(all_rows, bf), shape(low_rows, bf), shape(low_rows, wide), shape((1, width), wide),
+            shape((w.shape[1], width), wide), shape(wd.shape, wide),
+        ] + [shape(all_rows, bf)] * 4,
+        in_specs=[hbm] + [vmem] * 5,
+        out_specs=[hbm] + [vmem] * 5 + [hbm] * 4,
+        scratch_shapes=[
+            pltpu.VMEM(low_rows, wide), pltpu.VMEM(low_rows, wide), pltpu.VMEM(low_rows, bf),
+            pltpu.VMEM(low_rows, wide), pltpu.VMEM(low_rows, wide), pltpu.VMEM(low_rows, bf),
+            pltpu.VMEM((16, rows, 2 * width), bf), pltpu.VMEM((16, rows, 2 * width), bf),
+            pltpu.VMEM((2, 8, rows, width), bf), pltpu.VMEM((2, 4, rows, width), bf),
+            pltpu.VMEM((2, 3, rows, width), bf), pltpu.VMEM((2, 2, rows, width), bf),
+            pltpu.VMEM((2, FEED_BLOCKS, deep, width), bf), pltpu.VMEM((2, FEED_BLOCKS, deep, width), bf),
+            pltpu.VMEM((FEED_BLOCKS, deep, width), bf), pltpu.VMEM((FEED_BLOCKS, deep, width), bf),
+            dma((1 + 2 * halves,)), dma((1 + 2 * halves, N_GATHER_SENDS)), dma((1 + 2 * halves, 2, 32)), dma((4, 2)),
+        ] + scatter_sems(1) + scatter_sems(2),
+        name="middle_part",
+        compiler_params=pltpu.CompilerParams(collective_id=3, has_side_effects=True, vmem_limit_bytes=63 * 2**20),
+    )(partial, rows_low, upstream_low, gain, w, wd)
+    return outs[:6]
 
 
 def exchange(blocks):
@@ -611,47 +1300,6 @@
 
 def select(mask, rows):
     return dot(mask.astype(jnp.bfloat16), rows).astype(jnp.bfloat16)
-
-
-def natural(rows, count, tiles):
-    width = rows.shape[-1]
-    return (
-        rows.reshape(count, tiles, -1, width).transpose(1, 0, 2, 3).reshape(tiles, -1, width)
-    )
-
-
-def dealt_order(rows, count):
-    tiles, length, width = rows.shape
-    return (
-        rows.reshape(tiles, count, length // count, width)
-        .transpose(1, 0, 2, 3)
-        .reshape(-1, width)
-    )
-
-
-def windows(tiled):
-    edge = jnp.zeros_like(tiled[:1])
-    padded = jnp.concatenate((edge, tiled, edge), axis=0)
-    return jnp.concatenate((padded[:-2], padded[1:-1], padded[2:]), axis=1)
-
-
-def unwindow(wide):
-    length = wide.shape[1] // 3
-    edge = jnp.zeros_like(wide[:1, :length])
-    return (
-        jnp.concatenate((wide[1:, :length], edge), axis=0)
-        + wide[:, length : 2 * length]
-        + jnp.concatenate((edge, wide[:-1, 2 * length :]), axis=0)
-    )
-
-
-def batched(left, right, left_dim, right_dim):
-    return lax.dot_general(
-        left,
-        right,
-        (((left_dim,), (right_dim,)), ((0,), (0,))),
-        preferred_element_type=jnp.float32,
-    )
 
 
 def beside(sent, chain, kernel):
@@ -778,14 +1426,17 @@
 
     all_ids = jnp.arange(tiles * length, dtype=jnp.int32)
     segment = jnp.sum((all_ids[:, None] >= ends[None, :]).astype(jnp.int32), axis=1) + 1
-    segment = segment.reshape(tiles, length, 1)
-    same = segment == windows(segment).reshape(tiles, 1, 3 * length)
+    column, row = segment[:, None], jnp.pad(segment, (length, length))[None, :]
     relative = (
         jnp.arange(3 * length, dtype=jnp.int32)[None, :] - length - place_in[:, None]
     ).reshape(-1)
     onehot = bucket_index(relative)[None, :] == jnp.arange(BUCKETS, dtype=jnp.int32)[:, None]
     head_table = lax.dynamic_slice_in_dim(table, me, 1, axis=1)
-    rel_bias = dot(head_table.T, onehot.astype(jnp.bfloat16)).reshape(1, length, 3 * length)
+    rel_bias = dot(head_table.T, onehot.astype(jnp.bfloat16)).reshape(length, 3 * length)
+    few = 16
+    ids = jnp.arange(few * count, dtype=jnp.int32)
+    ids = ids % length // grain * few + ids // length * grain + ids % grain
+    perm = (ids[:, None] == jnp.arange(few * count, dtype=jnp.int32)[None, :]).astype(jnp.bfloat16)
 
     def owners_share(turned):
         return lax.optimization_barrier(turned).T.reshape(count, shard, -1)
@@ -794,52 +1445,24 @@
     normed = (rows_in * scale_one * gain_one).astype(jnp.bfloat16)
     cut = (count, -1, 4 * head)
     sent = jnp.concatenate((first_columns, spread_out(cotangent[0]).reshape(cut)), axis=1)
+    normed, perm, rel_bias, column, row = lax.optimization_barrier(
+        (normed, perm, rel_bias, column, row)
+    )
     came, normed_all = beside(sent, normed, gather)
-    normed_all = normed_all.reshape(-1, width)
     first_columns = came[:, :shard].reshape(-1, 4 * head)
     upstream_low = packed_block(came[:, shard:])
-    upstream = upstream_low.astype(jnp.float32)
-    upstream_all = lax.all_gather(upstream_low, AXIS, axis=0, tiled=True)
     qkv_columns = first_columns[:, : 3 * head]
-    qkv = natural(dot(normed_all, qkv_columns).astype(jnp.bfloat16), count, tiles)
-    query, key, value = qkv[:, :, :head], qkv[:, :, head : 2 * head], qkv[:, :, 2 * head :]
-    key_window, value_window = windows(key), windows(value)
-    scores = jnp.where(same, batched(query, key_window, 2, 2) + rel_bias, masked_score)
-    probs = jax.nn.softmax(scores, axis=-1)
-    probs_low = probs.astype(jnp.bfloat16)
-    attended = dealt_order(batched(probs_low, value_window, 2, 1).astype(jnp.bfloat16), count)
-    partial = dot(attended, out_weight).astype(jnp.bfloat16).reshape(count, slots, width)
-    came, branch = beside(second_columns, partial, scatter)
+    shared = (qkv_columns, out_weight, perm, rel_bias, column, row)
+    came, (qkv, attended, partial) = beside(
+        second_columns, (normed_all, *shared), lambda given: attend(*given)
+    )
     second_columns = came.reshape(count * shard, -1)
     gate_up_columns = jnp.concatenate((first_columns[:, 3 * head :], second_columns), axis=1)
-    middle = rows_in + branch
-
-    scale_two = norm_scale(middle)
-    normed_two = (middle * scale_two * gain_two).astype(jnp.bfloat16)
-    normed_two, upstream_all = lax.optimization_barrier((normed_two, upstream_all))
-    normed_two_all = gather(normed_two).reshape(-1, width)
-    gate_up = dot(normed_two_all, gate_up_columns)
-
-    def gelu_product(gate_part, up_part):
-        return jax.nn.gelu(gate_part, approximate=True) * up_part
-
-    hidden_full, gelu_pull = jax.vjp(
-        gelu_product, gate_up[:, :hidden_width], gate_up[:, hidden_width:]
-    )
-    hidden = hidden_full.astype(jnp.bfloat16)
-
-    d_gate, d_up = gelu_pull(against_rows(upstream_all, down_weight))
-    d_gate_up = jnp.concatenate((d_gate, d_up), axis=1).astype(jnp.bfloat16)
-    gate_up_grad = rows_product(d_gate_up, normed_two_all).astype(jnp.bfloat16)
-    partial = against_rows(d_gate_up, gate_up_columns).astype(jnp.bfloat16)
-    d_normed_two = scatter(partial.reshape(count, slots, width))
-    partial = dot(hidden, down_weight).astype(jnp.bfloat16)
-    partial, d_normed_two = lax.optimization_barrier((partial, d_normed_two))
-    down = scatter(partial.reshape(count, slots, width))
-    d_normed_two, down = lax.optimization_barrier((d_normed_two, down))
-    result = (middle + down).astype(jnp.bfloat16)
-    gain_two_grad = jnp.sum(d_normed_two * middle * scale_two, axis=0)
-    d_middle = upstream + norm_back(middle, scale_two, gain_two, d_normed_two)
+
+    d_branch_all, result, d_middle, gain_two_grad, gate_up_grad, down_grad = middle_part(
+        partial, rows_low, upstream_low, gain_two[None, :], gate_up_columns, down_weight
+    )
+    gate_up_grad = gate_up_grad.astype(jnp.bfloat16)
     turned = starts + (me * grain + jnp.arange(grain, dtype=jnp.int32)[:, None] - starts) % length
     back_slot = (turned // length * grain + jnp.arange(grain, dtype=jnp.int32)[:, None]).T
     spread = back_slot.reshape(-1, 1) == slot_ids[None, :]
@@ -847,33 +1470,15 @@
     sent = jnp.concatenate(
         (owners_share(gate_up_grad[head:]), select(spread, result).reshape(cut)), axis=1
     )
-    came, d_branch_all = beside(sent, d_middle.astype(jnp.bfloat16), gather)
+    came, (partial, out_grad, qkv_grad, bias_grad) = beside(
+        sent, (d_branch_all, normed_all, attended, qkv, *shared), lambda given: attend_back(*given)
+    )
     second_grad = came[:, :shard]
     layer_output = select(turn.T, came[:, shard:].reshape(length, width))[None]
-    d_branch_all = d_branch_all.reshape(-1, width)
-    d_attended = natural(
-        against_rows(d_branch_all, out_weight).astype(jnp.bfloat16), count, tiles
-    )
-    d_value = unwindow(batched(probs_low, d_attended, 1, 1))
-    d_probs = batched(d_attended, value_window, 2, 2)
-    inner = jnp.sum(probs * d_probs, axis=-1, keepdims=True)
-    d_scores = (probs * (d_probs - inner)).astype(jnp.bfloat16)
-    d_query = batched(d_scores, key_window, 2, 1)
-    d_key = unwindow(batched(d_scores, query, 1, 1))
-    d_bias = jnp.sum(d_scores.astype(jnp.float32), axis=0).reshape(1, -1)
-    table_sum = jnp.sum(jnp.where(onehot, d_bias, 0.0), axis=1)
-    d_qkv = dealt_order(
-        jnp.concatenate((d_query, d_key, d_value), axis=2).astype(jnp.bfloat16), count
-    )
-    qkv_grad = rows_product(d_qkv, normed_all).astype(jnp.bfloat16)
+    table_sum = jnp.sum(jnp.where(onehot, bias_grad.reshape(1, -1), 0.0), axis=1)
+    qkv_grad = qkv_grad.astype(jnp.bfloat16)
     sent = owners_share(jnp.concatenate((qkv_grad, gate_up_grad[:head]), axis=0))
-    partial = against_rows(d_qkv, qkv_columns).astype(jnp.bfloat16)
-    first_grad, d_normed = beside(sent, partial.reshape(count, slots, width), scatter)
-    first_grad, second_grad, attended, hidden, d_normed = lax.optimization_barrier(
-        (first_grad, second_grad, attended, hidden, d_normed)
-    )
-    out_grad = rows_product(attended, d_branch_all)
-    down_grad = rows_product(hidden, upstream_all)
+    first_grad, d_normed = beside(sent, partial, scatter)
     gain_one_grad = jnp.sum(d_normed * rows_in * scale_one, axis=0)
     d_dealt = (d_middle + norm_back(rows_in, scale_one, gain_one, d_normed)).astype(jnp.bfloat16)
 

time: 776 us -> 698 us (0.90)
  matrix products: 107 us -> 9.6 us
  Pallas kernels: 487 us -> 542 us
  local copies, waits for them, and re-layouts: 61.4 us -> 34 us
  between operations: 15.7 us -> 1.82 us
  waiting for transfers between devices: 18.1 us -> 26.7 us
    pallas_call x4, Pallas kernels: 277 us -> 461 us  [the longest x1 339 us: middle_part(): pl.pallas_call(functools.partial(middle_kernel, cuts), out_shape=[shape(a...]
    pallas_call x3 -> x1, Pallas kernels: 205 us -> 75.5 us  [gather(): pl.pallas_call(gather_kernel, out_shape=jax.ShapeDtypeStruct((32, rows, w...]
    dot_general x13 -> x0, matrix products: 61.4 us -> none  [the longest x4 27.5 us: against_rows(): lax.dot_general(left, right, (((1,), (1,)), ((), ())), preferred_element_...]
    dot_general x13 -> x9, matrix products: 40.6 us -> 9.6 us  [dot(): return jnp.dot(left, right, preferred_element_type=jnp.float32)]
    all_to_all x8, waiting for transfers between devices: 18.1 us -> 26.7 us  [exchange(): return lax.all_to_all(blocks, AXIS, split_axis=0, concat_axis=0, tiled=True)]
  transfers between devices with their start and end apart: 9 -> 8, of which waited for: 3 -> 4; matrix products, arithmetic and copies ran while one was open for 11% -> 5% of each run, Pallas kernels for 40% -> 30%
where the time goes in v3:
time: 698 us; the launch traced here: 686 us
  Pallas kernels  542 us (78%)
  starting transfers between devices  47.1 us (7%)
  local copies, waits for them, and re-layouts  34 us (5%)
  waiting for transfers between devices  26.7 us (4%)
  other arithmetic  25.7 us (4%)
  matrix products  9.6 us (1%)
    pallas_call x1, Pallas kernels, middle_part(): pl.pallas_call(functools.partial(middle_kernel, cuts), out_shape=[shape(a...  339 us
    pallas_call x1, Pallas kernels, gather(): pl.pallas_call(gather_kernel, out_shape=jax.ShapeDtypeStruct((32, rows, w...  75.5 us
    pallas_call x1, Pallas kernels, scatter(): pl.pallas_call(functools.partial(scatter_kernel, given), out_shape=[jax.S...  62.6 us
    all_to_all x8, starting transfers between devices, exchange(): return lax.all_to_all(blocks, AXIS, split_axis=0, concat_axis=0, tiled=True)  47.1 us
    pallas_call x1, Pallas kernels, attend_back(): pl.pallas_call(functools.partial(attend_back_kernel, groups), grid=(group...  36.1 us
    all_to_all x8, waiting for transfers between devices, exchange(): return lax.all_to_all(blocks, AXIS, split_axis=0, concat_axis=0, tiled=True)  26.7 us
    pallas_call x1, Pallas kernels, attend(): pl.pallas_call(functools.partial(attend_kernel, groups), grid=(groups + 1...  23.8 us
  transfers between devices with their start and end apart: 8, of which 4 were waited for; matrix products, arithmetic and copies ran while one was open for 5% of the time, Pallas kernels for 30%

profile of v3, /device:TPU:29, one launch (start us, length us, event | category | flops | bytes accessed | tf_op | source)
XLA Modules:
  0.0 686.5 jit_solution(10674930424909990447)
XLA Ops:
  4.6 6.2 all-to-all-start
  18.1 2.0 pack_columns.1
  21.5 2.5 all-to-all-done
  25.8 6.0 all-to-all-start.1
  36.4 8.0 %all-to-all-done.1 = bf16[32,4,2048]{2,1,0:T(4,128)(2,1)S(1)} async-done(((bf16[32,4,2048]{2,1,0:T(4,128)(2,1)}), bf16[32,4,2048]{2,1,0:T(4,128)(2,1)S(1)}, u32[]{:S(2)}, u32[]{:S(2)}) %all-to-all-start.1) | async-done | bytes 524320 | tf_op jit(solution)/shard_map/all_to_all | solution.py:1294
  46.3 6.1 all-to-all-start.2
  52.4 75.5 %gather_rows.1.x_ref = bf16[32,80,2048]{2,1,0:T(8,128)(2,1)} custom-call(bf16[80,2048]{1,0:T(8,128)(2,1)} %fusion.8.a_ref), custom_call_target="tpu_custom_call" | custom-call | tf_op jit(solution)/shard_map/gather_rows/pallas_call | solution.py:414
  128.0 5.1 all-to-all-start.3
  138.7 23.8 %attend.1 = (bf16[2816,192]{1,0:T(8,128)(2,1)}, bf16[32,80,64]{2,1,0:T(8,128)(2,1)}, bf16[32,80,2048]{2,1,0:T(8,128)(2,1)}) custom-call(bf16[32,80,2048]{2,1,0:T(8,128)(2,1)} %gather_rows.1.x_ref, bf16[2048,192]{1,0:T(8,128)(2,1)} %bitcast.46, bf16[64,2048]{1,0:T(8,128)(2,1)} %wo_ref.1, bf16[512,512]{1,0:T(8,128)(2,1)} %fusion.5.perm_ref, ...), custom_call_target="tpu_custom_call" | custom-call | tf_op jit(solution)/shard_map/attend/pallas_call | solution.py:683
  163.5 3.1 pad_maximum_fusion.1.refs_4_
  166.6 338.7 %middle_part.1 = (bf16[32,80,2048]{2,1,0:T(8,128)(2,1)}, bf16[80,2048]{1,0:T(8,128)(2,1)}, f32[80,2048]{1,0:T(8,128)}, f32[1,2048]{1,0:T(1,128)}, f32[320,2048]{...) custom-call(bf16[32,80,2048]{2,1,0:T(8,128)(2,1)} %get-tuple-element, ...), custom_call_target="tpu_custom_call" | custom-call | tf_op jit(solution)/shard_map/middle_part/pallas_call | solution.py:1269
  511.3 5.7 all-to-all-start.4
  518.5 36.1 %attend_back.1 = (bf16[32,80,2048]{2,1,0:T(8,128)(2,1)}, f32[64,2048]{1,0:T(8,128)}, f32[192,2048]{1,0:T(8,128)}, f32[128,384]{1,0:T(8,128)}) custom-call(bf16[32,80,2048]{2,1,0:T(8,128)(2,1)} %get-tuple-element.104.d_ref, bf16[32,80,2048]{2,1,0:T(8,128)(2,1)} %gather_rows.1.x_ref, bf16[32,80,64]{2,1,0:T(8,128)(2,1)} %get-tuple-element.106.att_ref, ...), custom_call_target="tpu_custom_call" | custom-call | tf_op jit(solution)/shard_map/attend_back/pallas_call | solution.py:764
  554.6 2.1 convert_element_type.205
  558.1 5.8 all-to-all-start.5
  568.7 62.6 %scatter_rows.1 = f32[80,2048]{1,0:T(8,128)} custom-call(bf16[32,80,2048]{2,1,0:T(8,128)(2,1)} %get-tuple-element.123.refs_0_), custom_call_target="tpu_custom_call" | custom-call | tf_op jit(solution)/shard_map/scatter_rows/pallas_call | solution.py:587
  632.7 2.5 convolution_convert_fusion.1
  637.8 5.9 all-to-all-start.6
  645.4 11.6 %all-to-all-done.6 = bf16[32,4,2176]{2,1,0:T(4,128)(2,1)} async-done(((bf16[32,4,2176]{2,1,0:T(4,128)(2,1)}), bf16[32,4,2176]{2,1,0:T(4,128)(2,1)}, u32[]{:S(2)}, u32[]{:S(2)}) %all-to-all-start.6) | async-done | bytes 557088 | tf_op jit(solution)/shard_map/all_to_all | solution.py:1294
  656.9 2.1 slice.95
  663.4 6.3 all-to-all-start.7
  672.5 2.8 unpack_columns.1
  677.5 4.6 all-to-all-done.7
  682.1 2.9 gather_fusion.2
  (173 shorter events, 56.7 us)
Async XLA Ops:
  1.7 9.1 %copy-start.7 = (s32[32]{0:T(128)S(1)}, s32[32]{0:T(128)}, u32[]{:S(2)}) copy-start(s32[32]{0:T(128)} %param.15) | copy-start | bytes 388
  4.6 19.5 %all-to-all-start = ((bf16[32,4,2176]{2,1,0:T(4,128)(2,1)}), bf16[32,4,2176]{2,1,0:T(4,128)(2,1)S(1)}, u32[]{:S(2)}, u32[]{:S(2)}) async-start(bf16[32,4,2176]{2,1,0:T(4,128)(2,1)} %pad_maximum_fusion.4), calls=%async_computation | async-start | bytes 1114112 | tf_op jit(solution)/shard_map/all_to_all | solution.py:1294
  10.7 7.3 %copy-start.2 = (bf16[64,5120]{1,0:T(8,128)(2,1)S(1)}, bf16[64,5120]{1,0:T(8,128)(2,1)}, u32[]{:S(2)}) copy-start(bf16[64,5120]{1,0:T(8,128)(2,1)} %gate_ref.1) | copy-start | bytes 1966084
  10.7 7.3 %copy-start.3 = (bf16[64,5120]{1,0:T(8,128)(2,1)S(1)}, bf16[64,5120]{1,0:T(8,128)(2,1)}, u32[]{:S(2)}) copy-start(bf16[64,5120]{1,0:T(8,128)(2,1)} %up_ref.1) | copy-start | bytes 1966084
  10.7 7.3 %copy-start.4 = (bf16[64,2048]{1,0:T(8,128)(2,1)S(1)}, bf16[64,2048]{1,0:T(8,128)(2,1)}, u32[]{:S(2)}) copy-start(bf16[64,2048]{1,0:T(8,128)(2,1)} %query_ref.1) | copy-start | bytes 786436
  10.8 7.3 %copy-start.5 = (bf16[64,2048]{1,0:T(8,128)(2,1)S(1)}, bf16[64,2048]{1,0:T(8,128)(2,1)}, u32[]{:S(2)}) copy-start(bf16[64,2048]{1,0:T(8,128)(2,1)} %key_ref.1) | copy-start | bytes 786436
  21.5 23.0 %copy-start.25 = (s32[80]{0:T(128)}, s32[80]{0:T(128)S(1)}, u32[]{:S(2)}) copy-start(s32[80]{0:T(128)S(1)} %multiply_add_fusion.1) | copy-start | bytes 964
  25.8 18.6 %all-to-all-start.1 = ((bf16[32,4,2048]{2,1,0:T(4,128)(2,1)}), bf16[32,4,2048]{2,1,0:T(4,128)(2,1)S(1)}, u32[]{:S(2)}, u32[]{:S(2)}) async-start(bf16[32,4,2048]{2,1,0:T(4,128)(2,1)} %reshape.428), calls=%async_computation.1 | async-start | bytes 1048576 | tf_op jit(solution)/shard_map/all_to_all | solution.py:1294
  46.3 81.6 %all-to-all-start.2 = ((bf16[32,96,256]{2,1,0:T(8,128)(2,1)}), bf16[32,96,256]{2,1,0:T(8,128)(2,1)S(1)}, u32[]{:S(2)}, u32[]{:S(2)}) async-start(bf16[32,96,256]{2,1,0:T(8,128)(2,1)} %pad_maximum_fusion), calls=%async_computation.2 | async-start | bytes 3145728 | tf_op jit(solution)/shard_map/all_to_all | solution.py:1294
  128.0 7.7 %copy-start.8 = (bf16[32,64,256]{2,1,0:T(8,128)(2,1)}, bf16[32,64,256]{2,1,0:T(8,128)(2,1)S(1)}, u32[]{:S(2)}) copy-start(bf16[32,64,256]{2,1,0:T(8,128)(2,1)S(1)} %slice.64) | copy-start | bytes 3145732
  128.0 35.5 %all-to-all-start.3 = ((bf16[32,64,256]{2,1,0:T(8,128)(2,1)}), bf16[32,64,256]{2,1,0:T(8,128)(2,1)}, u32[]{:S(2)}, u32[]{:S(2)}) async-start(bf16[32,64,256]{2,1,0:T(8,128)(2,1)} %get-tuple-element.85), calls=%async_computation.3 | async-start | bytes 2097152 | tf_op jit(solution)/shard_map/all_to_all | solution.py:1294
  138.7 23.8 %copy-start.26 = (s32[80]{0:T(128)S(1)}, s32[80]{0:T(128)}, u32[]{:S(2)}) copy-start(s32[80]{0:T(128)} %copy-done.25) | copy-start | bytes 964
  511.3 43.3 %all-to-all-start.4 = ((bf16[32,96,256]{2,1,0:T(8,128)(2,1)}), bf16[32,96,256]{2,1,0:T(8,128)(2,1)S(1)}, u32[]{:S(2)}, u32[]{:S(2)}) async-start(bf16[32,96,256]{2,1,0:T(8,128)(2,1)} %pad_maximum_fusion.2), calls=%async_computation.4 | async-start | bytes 3145728 | tf_op jit(solution)/shard_map/all_to_all | solution.py:1294
  554.6 115.1 %copy-start.11 = (bf16[32,96,256]{2,1,0:T(8,128)(2,1)}, bf16[32,96,256]{2,1,0:T(8,128)(2,1)S(1)}, u32[]{:S(2)}) copy-start(bf16[32,96,256]{2,1,0:T(8,128)(2,1)S(1)} %all-to-all-done.4) | copy-start | bytes 4718596
  558.1 8.0 %copy-start.20 = (f32[1,2048]{1,0:T(1,128)S(1)}, f32[1,2048]{1,0:T(1,128)}, u32[]{:S(2)}) copy-start(f32[1,2048]{1,0:T(1,128)} %get-tuple-element.125) | copy-start | bytes 24580
  558.1 73.2 %all-to-all-start.5 = ((bf16[32,64,256]{2,1,0:T(8,128)(2,1)}), bf16[32,64,256]{2,1,0:T(8,128)(2,1)S(1)}, u32[]{:S(2)}, u32[]{:S(2)}) async-start(bf16[32,64,256]{2,1,0:T(8,128)(2,1)} %bitcast.49), calls=%async_computation.5 | async-start | bytes 2097152 | tf_op jit(solution)/shard_map/all_to_all | solution.py:1294
  568.6 62.7 %copy-start.10 = (bf16[80,2048]{1,0:T(8,128)(2,1)S(1)}, bf16[80,2048]{1,0:T(8,128)(2,1)}, u32[]{:S(2)}) copy-start(bf16[80,2048]{1,0:T(8,128)(2,1)} %copy-done.9) | copy-start | bytes 983044
  568.6 62.7 %copy-start.22 = (f32[80]{0:T(128)S(1)}, f32[80]{0:T(128)}, u32[]{:S(2)}) copy-start(f32[80]{0:T(128)} %copy-done.21) | copy-start | bytes 964
  568.6 64.1 %copy-start.24 = (s32[128]{0:T(128)S(1)}, s32[128]{0:T(128)}, u32[]{:S(2)}) copy-start(s32[128]{0:T(128)} %multiply_add_fusion) | copy-start | bytes 1540
  568.6 64.1 %copy-start.27 = (f32[80]{0:T(128)S(1)}, f32[80]{0:T(128)}, u32[]{:S(2)}) copy-start(f32[80]{0:T(128)} %get-tuple-element.148) | copy-start | bytes 964
  635.2 8.5 %copy-start.30 = (s32[32]{0:T(128)S(1)}, s32[32]{0:T(128)}, u32[]{:S(2)}) copy-start(s32[32]{0:T(128)} %param.16) | copy-start | bytes 388
  637.8 19.1 %all-to-all-start.6 = ((bf16[32,4,2176]{2,1,0:T(4,128)(2,1)}), bf16[32,4,2176]{2,1,0:T(4,128)(2,1)}, u32[]{:S(2)}, u32[]{:S(2)}) async-start(bf16[32,4,2176]{2,1,0:T(4,128)(2,1)} %pad_maximum_fusion.5), calls=%async_computation.6 | async-start | bytes 1114112 | tf_op jit(solution)/shard_map/all_to_all | solution.py:1294
  663.4 18.7 %all-to-all-start.7 = ((bf16[32,4,2048]{2,1,0:T(4,128)(2,1)}), bf16[32,4,2048]{2,1,0:T(4,128)(2,1)}, u32[]{:S(2)}, u32[]{:S(2)}) async-start(bf16[32,4,2048]{2,1,0:T(4,128)(2,1)} %reshape.445), calls=%async_computation.7 | async-start | bytes 1048576 | tf_op jit(solution)/shard_map/all_to_all | solution.py:1294
  675.3 9.7 %copy-start.14 = (f32[160,2048]{1,0:T(8,128)S(1)}, f32[160,2048]{1,0:T(8,128)}, u32[]{:S(2)}) copy-start(f32[160,2048]{1,0:T(8,128)} %get-tuple-element.172) | copy-start | bytes 3932164
  (17 other events, 49.5 us)

commit v4 on v0

--- a/solution.py
+++ b/solution.py
@@ -1,6 +1,10 @@
+import functools
+
 import jax
 import jax.numpy as jnp
 from jax import lax
+from jax.experimental import pallas as pl
+from jax.experimental.pallas import tpu as pltpu
 from jax.sharding import PartitionSpec as P
 
 HEADS = 32
@@ -78,7 +82,7 @@
     )
 
 
-def body(
+def body_any(
     tokens,
     lengths,
     permutation,
@@ -284,6 +288,1101 @@
     )
 
 
+MESH = pl.DeviceIdType.MESH
+AXIS = "fsdp"
+
+
+def over(left, right, left_dim=1, right_dim=0):
+    return lax.dot_general(
+        left, right, (((left_dim,), (right_dim,)), ((), ())), preferred_element_type=jnp.float32
+    )
+
+
+def low(values):
+    return values.astype(jnp.bfloat16)
+
+
+def tile_probs(query, key, bias, same):
+    scores = jnp.where(same, over(query, key, 1, 1) + bias, masked_score)
+    grown = jnp.exp(scores - jnp.max(scores, axis=-1, keepdims=True))
+    return grown / jnp.sum(grown, axis=-1, keepdims=True)
+
+
+class Spot:
+    def __init__(self):
+        me = lax.axis_index(AXIS)
+        c, x, y, z = me % 2, (me // 2) % 2, (me // 4) % 2, me // 8
+        self.me = me
+        self.mid = (z == 1) | (z == 2)
+        self.end = jnp.logical_not(self.mid)
+        self.zs = (z, z + 1 - 2 * (z % 2), 2 - z // 2, 3 - 3 * (z // 2))
+        self.shift = [8 * (zz - z) for zz in self.zs]
+        self.core, self.x, self.y = me + 1 - 2 * c, me + 2 - 4 * x, me + 4 - 8 * y
+        self.diag = self.x + self.y - me
+        self.n1, self.n2 = me + self.shift[1], me + self.shift[2]
+
+    def greet(self):
+        bar = pltpu.get_barrier_semaphore()
+        for peer in (self.core, self.x, self.y, self.n1):
+            pl.semaphore_signal(bar, inc=1, device_id=(peer,), device_id_type=MESH)
+
+        @pl.when(self.mid)
+        def _():
+            pl.semaphore_signal(bar, inc=1, device_id=(self.n2,), device_id_type=MESH)
+
+        pl.semaphore_wait(bar, 4 + self.mid.astype(jnp.int32))
+
+    def greet_all(self, count):
+        bar = pltpu.get_barrier_semaphore()
+
+        def signal(d, _):
+            peer = (self.me + d) % count
+            pl.semaphore_signal(bar, inc=1, device_id=(peer,), device_id_type=MESH)
+            return _
+
+        lax.fori_loop(1, count, signal, 0)
+        pl.semaphore_wait(bar, count - 1)
+
+
+class Sends:
+    def __init__(self, sems):
+        self.sems, self.used, self.open = sems, 0, []
+
+    def push(self, src, dst, rsem, peer, when=None):
+        ssem = self.sems.at[self.used]
+        self.used += 1
+
+        def copy():
+            return pltpu.make_async_remote_copy(
+                src, dst, ssem, rsem, device_id=(peer,), device_id_type=MESH
+            )
+
+        if when is None:
+            copy().start()
+        else:
+            pl.when(when)(lambda: copy().start())
+        self.open.append((lambda: copy().wait_send(), when))
+
+    def finish(self):
+        for wait, when in self.open:
+            if when is None:
+                wait()
+            else:
+                pl.when(when)(wait)
+        self.open = []
+
+
+def arrive(dst, rsem, spot):
+    pltpu.make_async_remote_copy(
+        dst, dst, rsem, rsem, device_id=(spot.core,), device_id_type=MESH
+    ).wait_recv()
+
+
+def gather_steps(spot, src, dst, rows, sends, rsem, own_sem):
+    half = src.shape[1] // 2
+    cols = (pl.ds(0, half), pl.ds(half, half))
+    me, mid, shift = spot.me, spot.mid, spot.shift
+    first, last = (spot.x, spot.y), (spot.y, spot.x)
+    own = pltpu.make_async_copy(src.at[rows, :], dst.at[me, rows, :], own_sem)
+    own.start()
+
+    def push(part, block, peer, mine=False, when=None):
+        there = dst.at[block, rows, cols[part]]
+        here = src.at[rows, cols[part]] if mine else there
+        sends.push(here, there, rsem.at[part, block], peer, when)
+
+    def landed(part, block):
+        arrive(dst.at[block, rows, cols[part]], rsem.at[part, block], spot)
+
+    for part in (0, 1):
+        push(part, me, spot.n1, True)
+        push(part, me, spot.n2, True, mid)
+        push(part, me, first[part], True)
+        push(part, me, last[part], True)
+    for part in (0, 1):
+        push(part, me, spot.core, True)
+    yield
+
+    def from_z(part, j):
+        b = me + shift[j]
+        landed(part, b)
+        push(part, b, spot.n2 if j == 1 else spot.n1, when=mid)
+        push(part, b, first[part])
+        push(part, b, last[part])
+        push(part, b, spot.core)
+
+    def from_first(part, j):
+        b = first[part] + shift[j]
+        landed(part, b)
+        push(part, b, last[part])
+        push(part, b, spot.core)
+
+    def from_last(part, b):
+        landed(part, b)
+        push(part, b, spot.core)
+
+    for j in range(4):
+        if j:
+            for part in (0, 1):
+                from_z(part, j)
+                yield
+        for part in (0, 1):
+            from_first(part, j)
+            yield
+        if j:
+            for part in (0, 1):
+                from_last(part, last[part] + shift[j - 1])
+                yield
+    for part in (0, 1):
+        from_last(part, last[part] + shift[3])
+        yield
+    for j in range(4):
+        for part in (0, 1):
+            from_last(part, spot.diag + shift[j])
+            yield
+    for j in range(4):
+        for base in (me, spot.x, spot.y, spot.diag):
+            for part in (0, 1):
+                landed(part, base + spot.core - me + shift[j])
+    own.wait()
+    yield
+
+
+def scatter_steps(spot, p_refs, o_refs, rows, bufs, sems, sends):
+    ring_ref, s_ref, first_ref, second_ref, za_ref, zb_ref = bufs
+    lsem, csem, fsem, gsem, zasem, zbsem = sems
+    given = len(p_refs)
+    width = p_refs[0].shape[2]
+    half = given * width // 2
+    me, mid, end, zs = spot.me, spot.mid, spot.end, spot.zs
+    cols, short = (pl.ds(0, half), pl.ds(half, half)), pl.ds(0, half)
+    plane = (me, spot.x, spot.y, spot.diag)
+    first_peer, second_peer = (spot.y, spot.x), (spot.x, spot.y)
+    start, size = rows.start, rows.size
+
+    def mine(q, j, part):
+        return s_ref.at[q * 4 + zs[j], rows, cols[part]]
+
+    def held(ref, part, slot):
+        return ref.at[part, slot, rows, short]
+
+    def chunks(count, step):
+        lax.fori_loop(0, size // 16, lambda i, _: step(pl.ds(pl.multiple_of(start + i * 16, 16), 16)) or _, 0)
+
+    def add(q, j, part, *more):
+        def step(r):
+            v = s_ref[q * 4 + zs[j], r, cols[part]].astype(jnp.float32)
+            for ref, slot in more:
+                v = v + ref[part, slot, r, short].astype(jnp.float32)
+            s_ref[q * 4 + zs[j], r, cols[part]] = v.astype(s_ref.dtype)
+
+        chunks(size, step)
+
+    def pair_exchange(j):
+        for q in (3, 2, 1, 0):
+            b = plane[q] + spot.shift[j]
+            slot = q * 4 + zs[j]
+            for i, p_ref in enumerate(p_refs):
+                own = pl.ds(i * width, width)
+                sends.push(p_ref.at[b + spot.core - me, rows, :], s_ref.at[slot, rows, own], csem.at[i, slot], spot.core)
+                here = ring_ref.at[j % 2 * 4 + q, rows, own]
+                pltpu.make_async_copy(p_ref.at[b, rows, :], here, lsem.at[i, j % 2 * 4 + q]).start()
+
+    def joined(q, j):
+        slot, near = q * 4 + zs[j], j % 2 * 4 + q
+        for i, p_ref in enumerate(p_refs):
+            own = pl.ds(i * width, width)
+            pltpu.make_async_copy(p_ref.at[0, rows, :], ring_ref.at[near, rows, own], lsem.at[i, near]).wait()
+            arrive(s_ref.at[slot, rows, own], csem.at[i, slot], spot)
+        everything = pl.ds(0, given * width)
+
+        def step(r):
+            v = ring_ref[near, r, everything].astype(jnp.float32) + s_ref[slot, r, everything].astype(jnp.float32)
+            s_ref[slot, r, everything] = v.astype(s_ref.dtype)
+
+        chunks(size, step)
+
+    def to_first(part, q, j):
+        slot = (4 if q == 3 else 0) + zs[j]
+        sends.push(mine(q, j, part), held(first_ref, part, slot), fsem.at[part, slot], first_peer[part])
+
+    def first_stage(j):
+        joined(3, j)
+        if j:
+            pair_exchange(j - 1)
+        to_first(0, 3, j)
+        to_first(1, 3, j)
+        yield
+        joined(2, j)
+        to_first(0, 2, j)
+        yield
+        joined(1, j)
+        to_first(1, 1, j)
+        joined(0, j)
+        yield
+
+    def second_stage(j):
+        for part in (0, 1):
+            q, slot = (1, 2)[part], 4 + zs[j]
+            arrive(held(first_ref, part, slot), fsem.at[part, slot], spot)
+            add(q, j, part, (first_ref, slot))
+            sends.push(mine(q, j, part), held(second_ref, part, zs[j]), gsem.at[part, zs[j]], second_peer[part])
+            yield
+
+    def z_send(j):
+        for part in (0, 1):
+            arrive(held(first_ref, part, zs[j]), fsem.at[part, zs[j]], spot)
+            arrive(held(second_ref, part, zs[j]), gsem.at[part, zs[j]], spot)
+            add(0, j, part, (first_ref, zs[j]), (second_ref, zs[j]))
+            if j:
+                sends.push(mine(0, j, part), held(za_ref, part, 3 - j), zasem.at[part, 3 - j], spot.n1, end)
+            yield
+
+    def z_relay(j):
+        if not j:
+            return
+        for part in (0, 1):
+            came, sem, slot = (za_ref, zasem, 3 - j) if j > 1 else (zb_ref, zbsem, 0)
+
+            @pl.when(mid)
+            def _():
+                arrive(held(came, part, slot), sem.at[part, slot], spot)
+                add(0, j, part, (came, slot))
+
+            slot = 3 - j if j > 1 else 0
+            peer = spot.n2 if j > 1 else spot.n1
+            sends.push(mine(0, j, part), held(zb_ref, part, slot), zbsem.at[part, slot], peer, mid)
+            yield
+
+    pair_exchange(3)
+    yield
+    stages = (first_stage, second_stage, z_send, z_relay)
+    for step in range(4 + len(stages) - 1):
+        for stage, what in enumerate(stages):
+            j = 3 - (step - stage)
+            if 0 <= j <= 3:
+                yield from what(j)
+    for part in (0, 1):
+        o_ref, there = (o_refs[part], pl.ds(0, half)) if given == 2 else (o_refs[0], cols[part])
+
+        def total(*more):
+            def step(r):
+                v = s_ref[zs[0], r, cols[part]].astype(jnp.float32)
+                for ref, slot in more:
+                    v = v + ref[part, slot, r, short].astype(jnp.float32)
+                o_ref[r, there] = v
+
+            chunks(size, step)
+
+        @pl.when(mid)
+        def _():
+            arrive(held(za_ref, part, 2), zasem.at[part, 2], spot)
+            arrive(held(zb_ref, part, 1), zbsem.at[part, 1], spot)
+            total((za_ref, 2), (zb_ref, 1))
+
+        @pl.when(end)
+        def _():
+            arrive(held(zb_ref, part, 0), zbsem.at[part, 0], spot)
+            total((zb_ref, 0))
+
+        yield
+
+
+def gather_kernel(a_ref, o_ref, own_sem, ssem, rsem):
+    spot = Spot()
+    spot.greet()
+    sends = Sends(ssem)
+    for _ in gather_steps(spot, a_ref, o_ref, pl.ds(0, a_ref.shape[0]), sends, rsem, own_sem):
+        pass
+    sends.finish()
+
+
+def gather(block):
+    rows, width = block.shape
+    dma = pltpu.SemaphoreType.DMA
+    return pl.pallas_call(
+        gather_kernel,
+        out_shape=jax.ShapeDtypeStruct((32, rows, width), block.dtype),
+        in_specs=[pl.BlockSpec(memory_space=pl.ANY)],
+        out_specs=pl.BlockSpec(memory_space=pl.ANY),
+        scratch_shapes=[dma, dma((N_GATHER_SENDS,)), dma((2, 32))],
+        name="gather_rows",
+        compiler_params=pltpu.CompilerParams(collective_id=0, has_side_effects=True),
+    )(block)
+
+
+def weave(tasks, order):
+    names = list(tasks)
+    left = {name: steps for name, (_, steps) in tasks.items()}
+
+    def advance(name):
+        for other in tasks[name][0]:
+            if other in left:
+                advance(other)
+                assert other not in left, name
+        if name in left and next(left[name], left) is left:
+            del left[name]
+
+    for number, times in order:
+        for _ in range(times):
+            advance(names[number])
+    while left:
+        name = next(n for n in left if not any(other in left for other in tasks[n][0]))
+        while name in left:
+            advance(name)
+
+
+FRONT_ORDER = (
+    (0, 1), (2, 1), (1, 1), (2, 9), (1, 1), (2, 3), (1, 1), (2, 1), (1, 2), (3, 8), (1, 1), (3, 4), (1, 1),
+    (9, 8), (10, 1), (3, 1), (1, 1), (3, 1), (10, 1), (1, 1), (3, 1), (10, 2), (3, 1), (10, 1), (3, 1), (10,
+    2), (1, 2), (3, 4), (10, 1), (3, 4), (10, 5), (0, 1), (1, 1), (10, 2), (3, 1), (1, 3), (3, 2), (1, 1), (3,
+    1), (1, 1), (3, 4), (10, 4), (3, 1), (10, 1), (3, 1), (10, 5), (1, 4), (3, 1), (1, 2), (3, 1), (1, 6),
+    (10, 3), (4, 1), (5, 1), (10, 4), (1, 3), (10, 3), (5, 1), (10, 1), (5, 1), (10, 1), (11, 1), (5, 26),
+    (12, 1), (5, 3), (12, 1), (6, 1), (12, 3), (6, 1), (12, 4), (6, 1), (12, 2), (6, 1), (12, 6), (6, 1), (12,
+    1), (6, 1), (12, 12), (6, 1), (12, 2), (7, 12), (13, 2), (7, 2), (13, 1), (7, 6), (13, 1), (7, 3), (13,
+    1), (14, 1), (7, 4), (14, 1), (7, 1), (14, 9), (7, 9), (8, 1), (14, 26), (15, 1),
+)
+REAR_ORDER = (
+    (0, 15), (1, 1), (0, 17), (4, 1), (1, 1), (4, 1), (1, 1), (4, 1), (1, 1), (4, 2), (1, 1), (4, 1), (1, 1),
+    (4, 1), (1, 1), (4, 1), (1, 1), (4, 1), (1, 1), (4, 1), (1, 1), (4, 1), (1, 1), (4, 2), (1, 1), (4, 1),
+    (1, 1), (4, 1), (1, 2), (4, 2), (1, 1), (4, 1), (1, 1), (4, 1), (1, 1), (4, 1), (1, 1), (4, 2), (1, 2),
+    (4, 1), (1, 1), (5, 1), (6, 1), (5, 1), (1, 3), (5, 1), (1, 2), (5, 1), (1, 1), (5, 1), (6, 1), (1, 1),
+    (6, 1), (5, 1), (6, 1), (1, 1), (6, 1), (5, 1), (1, 1), (6, 1), (1, 1), (5, 1), (1, 1), (6, 1), (1, 1),
+    (5, 1), (6, 1), (1, 1), (5, 1), (1, 1), (6, 1), (5, 1), (1, 1), (5, 3), (7, 1), (5, 1), (7, 1), (5, 2),
+    (3, 1), (7, 1), (5, 7), (7, 6), (5, 1), (7, 1), (5, 1), (7, 1), (5, 1), (7, 1), (5, 1), (7, 1), (5, 1),
+    (7, 3), (5, 2), (7, 3), (5, 1), (7, 1), (2, 1), (7, 1), (5, 1), (7, 3), (5, 1), (7, 2), (5, 1), (7, 2),
+    (5, 1), (7, 1), (5, 1), (7, 8), (8, 1), (3, 1), (2, 1), (8, 2),
+)
+N_GATHER_SENDS = 66
+FEW = 16
+
+
+def gelu_pair(gate):
+    slope = 0.7978845608028654
+    squared = gate * gate
+    bent = jnp.tanh(slope * (gate + 0.044715 * gate * squared))
+    gelu = 0.5 * gate * (1.0 + bent)
+    return gelu, 0.5 * (1.0 + bent) + 0.5 * gate * (1.0 - bent * bent) * slope * (1.0 + 3.0 * 0.044715 * squared)
+
+
+def scatter_sems(halves, given):
+    dma = pltpu.SemaphoreType.DMA
+    return [
+        dma((halves, 16 * given + 36)), dma((halves, given, 8)), dma((halves, given, 16)), dma((halves, 2, 8)),
+        dma((halves, 2, 4)), dma((halves, 2, 3)), dma((halves, 2, 2)),
+    ]
+
+
+def scatter_bufs(rows, width, given):
+    half = given * width // 2
+    shapes = ((8, rows, given * width), (16, rows, given * width), (2, 8, rows, half), (2, 4, rows, half))
+    return [pltpu.VMEM(shape, jnp.bfloat16) for shape in shapes + ((2, 3, rows, half), (2, 2, rows, half))]
+
+
+class Stage:
+    def __init__(self, count, cuts, in_refs, out_refs, in_sems, out_sems):
+        self.spot = Spot()
+        self.count = count
+        self.ranges = [pl.ds(a, b - a) for a, b in zip(cuts[:-1], cuts[1:])]
+        self.cuts = cuts
+        self.sends = {}
+        self.in_refs, self.out_refs, self.in_sems, self.out_sems = in_refs, out_refs, in_sems, out_sems
+
+    def gathering(self, name, at, src, dst, rows, sems):
+        own_sem, ssem, rsem = sems
+        self.sends[name] = Sends(ssem.at[at])
+        yield from gather_steps(self.spot, src, dst, rows, self.sends[name], rsem.at[at], own_sem.at[at])
+
+    def scattering(self, name, p_refs, o_refs, rows, bufs, sems, at):
+        self.sends[name] = Sends(sems[0].at[at])
+        yield from scatter_steps(
+            self.spot, p_refs, o_refs, rows, bufs, [sem.at[at] for sem in sems[1:]], self.sends[name]
+        )
+
+    def fetch(self, group, sources, streams=None):
+        streams = range(len(sources)) if streams is None else streams
+        for i, source in zip(streams, sources):
+            there = self.in_refs[i].at[group % 2]
+            yield pltpu.make_async_copy(source.at[:, pl.ds(group * FEW, FEW), :], there, self.in_sems.at[i, group % 2])
+
+    def store(self, group, targets):
+        for i, target in enumerate(targets):
+            there = target.at[:, pl.ds(group * FEW, FEW), :]
+            yield pltpu.make_async_copy(self.out_refs[i], there, self.out_sems.at[i])
+
+    def finish(self):
+        for some in self.sends.values():
+            some.finish()
+
+
+def start_all(copies):
+    for copy in copies:
+        copy.start()
+
+
+def wait_all(copies):
+    for copy in copies:
+        copy.wait()
+
+
+def tile_inputs(qkv_ref, col_ref, row_ref, base, length, head):
+    query = qkv_ref[pl.ds(base + length, length), :head]
+    key = qkv_ref[pl.ds(base, 3 * length), head : 2 * head]
+    value = qkv_ref[pl.ds(base, 3 * length), 2 * head :]
+    return query, key, value, col_ref[pl.ds(base, length), :] == row_ref[:, pl.ds(base, 3 * length)]
+
+
+def front_kernel(cuts, *refs):
+    (nx_all_ref, rows_ref, up_ref, gain_ref, qkv_w_ref, gate_w_ref, mine_ref, wd_ref, wo_ref, perm_ref, bias_ref, col_ref,
+     row_ref) = refs[:13]
+    (qkv_ref, att_ref, middle_ref, d_mid_ref, d_ref, gain_grad_ref, near_grad_ref, far_grad_ref, wd_grad_ref,
+     forth_ref) = refs[13:23]
+    part_ref, up_all_ref, x_all_ref, back_ref = refs[23:27]
+    branch_ref, x_ref, dn_ref, w_ref = refs[27:31]
+    bufs, two_ref, in_refs, out_refs = refs[31:37], refs[37], refs[38:40], refs[40:42]
+    in_sems, out_sems, w_ssem, w_rsem, w_own = refs[42:47]
+    g_sems, one_sems, two_sems = refs[47:50], refs[50:57], refs[57:64]
+    two_bufs = (bufs[0], two_ref, *bufs[2:])
+    count = part_ref.shape[0]
+    stage = Stage(count, cuts, in_refs, out_refs, in_sems, out_sems)
+    spot, ranges = stage.spot, stage.ranges
+    spot.greet_all(count)
+    width, units, head, length = rows_ref.shape[1], wd_ref.shape[0], wo_ref.shape[0], bias_ref.shape[0]
+    size = perm_ref.shape[0]
+    groups = cuts[-1] // FEW
+    shard = mine_ref.shape[1]
+    near = units - head
+
+    def column_blocks(what):
+        def one(d, _):
+            peer = (spot.me + d) % count
+            source = (spot.me + count - d) % count
+            if what == "send":
+                pltpu.make_async_remote_copy(
+                    mine_ref.at[peer], w_ref.at[pl.ds(pl.multiple_of(spot.me * shard, shard), shard), :], w_ssem.at[peer],
+                    w_rsem.at[spot.me], device_id=(peer,), device_id_type=MESH,
+                ).start()
+            else:
+                there = w_ref.at[pl.ds(pl.multiple_of(source * shard, shard), shard), :]
+                copy = pltpu.make_async_remote_copy(
+                    there, there, w_ssem.at[peer], w_rsem.at[source], device_id=(peer,), device_id_type=MESH,
+                )
+                copy.wait_recv()
+                copy.wait_send()
+            return _
+
+        lax.fori_loop(1, count, one, 0)
+
+    def columns():
+        own = pltpu.make_async_copy(
+            mine_ref.at[spot.me], w_ref.at[pl.ds(pl.multiple_of(spot.me * shard, shard), shard), :], w_own
+        )
+        own.start()
+        column_blocks("send")
+        yield
+        column_blocks("wait")
+        own.wait()
+        yield
+
+    def attending(first, last):
+        perm = perm_ref[...]
+        if first == 0:
+            start_all(stage.fetch(0, (nx_all_ref,)))
+            qkv_ref[:length, :] = jnp.zeros((length, 3 * head), qkv_ref.dtype)
+            qkv_ref[length + groups * size :, :] = jnp.zeros((length, 3 * head), qkv_ref.dtype)
+        for step in range(first, last):
+            if step < groups:
+                if step + 1 < groups:
+                    start_all(stage.fetch(step + 1, (nx_all_ref,)))
+                wait_all(stage.fetch(step, (nx_all_ref,)))
+                rows = low(over(in_refs[0][step % 2].reshape(size, -1), qkv_w_ref[...]))
+                qkv_ref[length + step * size : length + (step + 1) * size, :] = low(over(perm, rows))
+                yield
+            if step > 0:
+                attended = []
+                for tile in range(size // length):
+                    base = (step - 1) * size + tile * length
+                    query, key, value, same = tile_inputs(qkv_ref, col_ref, row_ref, base, length, head)
+                    attended.append(low(over(low(tile_probs(query, key, bias_ref[...], same)), value)))
+                    if tile % 2:
+                        yield
+                rows = low(over(perm, jnp.concatenate(attended, axis=0), 0, 0))
+                att_ref[:, (step - 1) * FEW : step * FEW, :] = rows.reshape(count, FEW, head)
+                if step > max(first, 1):
+                    wait_all(stage.store(step - 2, (part_ref,)))
+                for i in range(2):
+                    there = pl.ds(i * count // 2, count // 2)
+                    piece = over(rows[i * size // 2 : (i + 1) * size // 2], wo_ref[...])
+                    out_refs[0][there] = low(piece).reshape(count // 2, FEW, width)
+                start_all(stage.store(step - 1, (part_ref,)))
+                yield
+        if last > max(first, 1):
+            wait_all(stage.store(last - 2, (part_ref,)))
+        yield
+
+    def rows_of(rows):
+        return [pl.ds(rows.start + i, 16) for i in range(0, rows.size, 16)]
+
+    def scale_of(v):
+        return lax.rsqrt(jnp.sum(v * v, axis=1, keepdims=True) / width + EPSILON)
+
+    def first_norm(rows):
+        for r in rows_of(rows):
+            v = rows_ref[r, :].astype(jnp.float32) + branch_ref[r, :]
+            middle_ref[r, :] = v
+            x_ref[r, :] = (v * scale_of(v) * gain_ref[...]).astype(x_ref.dtype)
+        yield
+
+    def norm_back_rows(rows):
+        for r in rows_of(rows):
+            v, d, gain = middle_ref[r, :], dn_ref[r, :], gain_ref[...]
+            scale = scale_of(v)
+            gain_grad_ref[...] += jnp.sum(d * v * scale, axis=0, keepdims=True)
+            w = gain * d
+            mean = jnp.sum(w * v, axis=1, keepdims=True) / width
+            d_mid = up_ref[r, :].astype(jnp.float32) + scale * w - v * (scale * scale * scale) * mean
+            d_mid_ref[r, :] = d_mid
+            d_ref[r, :] = d_mid.astype(d_ref.dtype)
+        yield
+
+    def feeding(first, last):
+        sources, targets = (x_all_ref, up_all_ref), (back_ref, forth_ref)
+        start_all(stage.fetch(first, sources))
+        for group in range(first, last):
+            if group + 1 < last:
+                start_all(stage.fetch(group + 1, sources))
+            wait_all(stage.fetch(group, sources))
+            for i in range(2):
+                blocks = slice(i * count // 2, (i + 1) * count // 2)
+                x = in_refs[0][group % 2, blocks].reshape(size // 2, width)
+                upstream = in_refs[1][group % 2, blocks].reshape(size // 2, width)
+                both = over(x, w_ref[...])
+                gate = jnp.concatenate((over(x, gate_w_ref[...]), both[:, :near]), axis=1)
+                up = both[:, near:]
+                d_hidden = over(upstream, wd_ref[...], 1, 1)
+                gelu, d_gelu = gelu_pair(gate)
+                hidden = low(gelu * up)
+                d_gate, d_up = low(d_hidden * up * d_gelu), low(d_hidden * gelu)
+                d_first, d_both = d_gate[:, :head], jnp.concatenate((d_gate[:, head:], d_up), axis=1)
+                if i == 0 and group > first:
+                    wait_all(stage.store(group - 1, targets))
+                shape = (count // 2, FEW, width)
+                back = over(d_both, w_ref[...], 1, 1) + over(d_first, gate_w_ref[...], 1, 1)
+                out_refs[0][blocks] = low(back).reshape(shape)
+                out_refs[1][blocks] = low(over(hidden, wd_ref[...])).reshape(shape)
+                if i:
+                    start_all(stage.store(group, targets))
+                near_grad_ref[...] += over(d_first, x, 0, 0)
+                far_grad_ref[...] += over(d_both, x, 0, 0)
+                wd_grad_ref[...] += over(hidden, upstream, 0, 0)
+                yield
+        wait_all(stage.store(last - 1, targets))
+        yield
+
+    for ref in (near_grad_ref, far_grad_ref, wd_grad_ref, gain_grad_ref):
+        ref[...] = jnp.zeros_like(ref)
+    halves = len(ranges)
+    tasks = {
+        "columns": ([], columns()),
+        "up": ([], stage.gathering("up", 0, up_ref, up_all_ref, pl.ds(0, cuts[-1]), g_sems)),
+    }
+    for i, rows in enumerate(ranges):
+        h = str(i)
+        last_step = groups + 1 if i == halves - 1 else cuts[i + 1] // FEW + 1
+        first_step = cuts[i] // FEW + 1 if i else 0
+        tasks |= {
+            "attend" + h: ([f"attend{i - 1}"] if i else [], attending(first_step, last_step)),
+            "one" + h: (
+                ["attend" + h], stage.scattering("one" + h, (part_ref,), (branch_ref,), rows, bufs, one_sems, i),
+            ),
+            "norm" + h: (["one" + h], first_norm(rows)),
+            "x" + h: (["norm" + h], stage.gathering("x" + h, 1 + i, x_ref, x_all_ref, rows, g_sems)),
+            "feed" + h: (
+                ["x" + h, "up", "columns", f"feed{i - 1}" if i else f"attend{halves - 1}"],
+                feeding(cuts[i] // FEW, cuts[i + 1] // FEW),
+            ),
+            "two" + h: (
+                ["feed" + h],
+                stage.scattering("two" + h, (back_ref,), (dn_ref,), rows, two_bufs, two_sems, i),
+            ),
+            "back" + h: (["two" + h], norm_back_rows(rows)),
+        }
+    weave(tasks, FRONT_ORDER)
+    stage.finish()
+
+
+def halves_of(rows):
+    return (0, 48, 80) if rows == 80 else (0, rows)
+
+
+def front(normed_all, rows_low, upstream_low, gain, qkv_w, gate_w, mine, wd, wo, perm, bias, col, row):
+    count, rows, width = normed_all.shape
+    cuts = halves_of(rows)
+    halves = len(cuts) - 1
+    head, length, size = wo.shape[0], bias.shape[0], perm.shape[0]
+    low_rows, all_rows, group = (rows, width), (count, rows, width), (count, FEW, width)
+    bf, wide, dma = jnp.bfloat16, jnp.float32, pltpu.SemaphoreType.DMA
+    vmem, hbm = pl.BlockSpec(memory_space=pltpu.VMEM), pl.BlockSpec(memory_space=pl.ANY)
+    shape = jax.ShapeDtypeStruct
+    outs = pl.pallas_call(
+        functools.partial(front_kernel, cuts),
+        out_shape=[
+            shape((rows // FEW * size + 2 * length, 3 * head), bf), shape((count, rows, head), bf), shape(low_rows, wide),
+            shape(low_rows, wide), shape(low_rows, bf), shape((1, width), wide), shape((head, width), wide),
+            shape((mine.shape[2], width), wide), shape(wd.shape, wide),
+        ] + [shape(all_rows, bf)] * 5,
+        in_specs=[hbm] + [vmem] * 5 + [hbm] + [vmem] * 6,
+        out_specs=[vmem] * 9 + [hbm] * 5,
+        scratch_shapes=[
+            pltpu.VMEM(low_rows, wide), pltpu.VMEM(low_rows, bf), pltpu.VMEM(low_rows, wide),
+            pltpu.VMEM((width, mine.shape[2]), bf),
+        ] + scatter_bufs(rows, width, 1) + [
+            pltpu.VMEM((16, rows, width), bf),
+            pltpu.VMEM((2,) + group, bf), pltpu.VMEM((2,) + group, bf), pltpu.VMEM(group, bf), pltpu.VMEM(group, bf),
+            dma((2, 2)), dma((2,)), dma((count,)), dma((count,)), dma,
+            dma((1 + halves,)), dma((1 + halves, N_GATHER_SENDS)), dma((1 + halves, 2, 32)),
+        ] + scatter_sems(halves, 1) * 2,
+        name="front",
+        compiler_params=pltpu.CompilerParams(collective_id=3, has_side_effects=True, vmem_limit_bytes=63 * 2**20),
+    )(normed_all, rows_low, upstream_low, gain, qkv_w, gate_w, mine, wd, wo, perm, bias, col, row)
+    return outs[:10]
+
+
+def swap(spot, count, src, dst, sems, what):
+    send_sem, recv_sem, own_sem = sems
+    share = src.shape[0] // count
+
+    def part(ref, index):
+        return ref.at[pl.ds(pl.multiple_of(index * share, share), share), :]
+
+    own = pltpu.make_async_copy(part(src, spot.me), part(dst, spot.me), own_sem)
+
+    def one(d, _):
+        peer, source = (spot.me + d) % count, (spot.me + count - d) % count
+        if what == "send":
+            pltpu.make_async_remote_copy(
+                part(src, peer), part(dst, spot.me), send_sem.at[peer], recv_sem.at[spot.me], device_id=(peer,),
+                device_id_type=MESH,
+            ).start()
+        else:
+            copy = pltpu.make_async_remote_copy(
+                part(src, peer), part(dst, source), send_sem.at[peer], recv_sem.at[source], device_id=(peer,),
+                device_id_type=MESH,
+            )
+            copy.wait_recv()
+            copy.wait_send()
+        return _
+
+    if what == "send":
+        own.start()
+    lax.fori_loop(1, count, one, 0)
+    if what == "wait":
+        own.wait()
+
+
+def rear_kernel(cuts, *refs):
+    (d_ref, x_all_ref, att_ref, qkv_ref, w_ref, wo_ref, perm_ref, bias_ref, col_ref, row_ref, near_ref, forth_ref, middle_ref,
+     rows_ref, d_mid_ref, gain_ref, spread_ref, turn_ref, bucket_ref) = refs[:19]
+    wo_grad_ref, owned_ref, out_rows_ref, sums_ref, token_rows_ref = refs[19:24]
+    d_all_ref, part_ref = refs[24:26]
+    dn_ref, down_ref, bias_grad_ref, dq_ref, dkv_ref, w_grad_ref, turned_ref, result_ref, going_ref, came_ref, last_ref = refs[26:37]
+    bufs, other_bufs, in_refs, out_refs = refs[37:43], refs[43:49], refs[49:51], refs[51:52]
+    in_sems, out_sems = refs[52:54]
+    w_sems, r_sems, t_sems, l_sems = refs[54:57], refs[57:60], refs[60:63], refs[63:66]
+    g_sems, one_sems, down_sems = refs[66:69], refs[69:76], refs[76:83]
+    count, width = part_ref.shape[0], part_ref.shape[2]
+    stage = Stage(count, cuts, in_refs, out_refs, in_sems, out_sems)
+    spot, ranges = stage.spot, stage.ranges
+    spot.greet_all(count)
+    head, length, size = wo_ref.shape[0], bias_ref.shape[0], perm_ref.shape[0]
+    groups = cuts[-1] // FEW
+    folds, piece = spread_ref.shape[0], result_ref.shape[1]
+
+    def owners():
+        merged = jnp.concatenate((low(w_grad_ref[...]), low(near_ref[...])), axis=0)
+        for i in range(0, width, 512):
+            turned_ref[i : i + 512, :] = merged[:, i : i + 512].T
+        swap(spot, count, turned_ref, owned_ref, w_sems, "send")
+        yield
+        swap(spot, count, turned_ref, owned_ref, w_sems, "wait")
+        yield
+
+    def dealt_out(rows):
+        return sum(
+            over(spread_ref[i], rows[:, i * piece : (i + 1) * piece]) for i in range(folds)
+        )
+
+    def output():
+        rows = low(middle_ref[...] + down_ref[...])
+        result_ref[...] = low(dealt_out(rows))
+        swap(spot, count, result_ref, out_rows_ref, r_sems, "send")
+        yield
+        swap(spot, count, result_ref, out_rows_ref, r_sems, "wait")
+        yield
+
+    def scale_of(v):
+        return lax.rsqrt(jnp.sum(v * v, axis=1, keepdims=True) / width + EPSILON)
+
+    def shares(v):
+        shape = (going_ref.shape[0], width)
+        at, to = lax.broadcasted_iota(jnp.int32, shape, 0), lax.broadcasted_iota(jnp.int32, shape, 1)
+        spread = jnp.where(at == to // (width // count) * 16, v, 0.0)
+        fold = lax.broadcasted_iota(jnp.int32, (width, width // count), 0) % (width // count)
+        fold = fold == lax.broadcasted_iota(jnp.int32, (width, width // count), 1)
+        high = low(spread)
+        rest = low(spread - high.astype(jnp.float32))
+        return jnp.concatenate([over(p, low(fold.astype(jnp.float32))) for p in (high, rest)], axis=1)
+
+    def finals():
+        v, d, gain = rows_ref[...].astype(jnp.float32), dn_ref[...], gain_ref[...]
+        scale = scale_of(v)
+        w = gain * d
+        mean = jnp.sum(w * v, axis=1, keepdims=True) / width
+        rows = low(d_mid_ref[...] + scale * w - v * (scale * scale * scale) * mean)
+        going_ref[:, :piece] = low(dealt_out(rows))
+        sums = shares(jnp.sum(d * v * scale, axis=0, keepdims=True))
+        at, to = lax.broadcasted_iota(jnp.int32, sums.shape, 0), lax.broadcasted_iota(jnp.int32, sums.shape, 1)
+        for b in range(BUCKETS):
+            total = jnp.sum(jnp.where(bucket_ref[...] == b, bias_grad_ref[...], 0.0), axis=(0, 1), keepdims=True)
+            high = low(total).astype(jnp.float32)
+            sums = sums + jnp.where((at == 16 * b + 1) & (to == 0), high, 0.0)
+            sums = sums + jnp.where((at == 16 * b + 1) & (to == 1), total - high, 0.0)
+        going_ref[:, piece:] = low(sums)
+        swap(spot, count, going_ref, came_ref, t_sems, "send")
+        yield
+        swap(spot, count, going_ref, came_ref, t_sems, "wait")
+        sums_ref[...] = came_ref[:, piece:]
+        last_ref[...] = low(over(turn_ref[...], came_ref[:, :piece]))
+        swap(spot, count, last_ref, token_rows_ref, l_sems, "send")
+        yield
+        swap(spot, count, last_ref, token_rows_ref, l_sems, "wait")
+        yield
+
+    def backing(first, last):
+        perm = perm_ref[...]
+        for step in range(first, last):
+            if step < groups:
+                start_all(stage.fetch(step, (d_all_ref,)))
+                start_all(stage.fetch(step, (x_all_ref,), (1,)))
+                wait_all(stage.fetch(step, (d_all_ref,)))
+                d_branch = in_refs[0][step % 2].reshape(size, width)
+                attended = att_ref[:, step * FEW : (step + 1) * FEW, :].reshape(size, head)
+                wo_grad_ref[...] += over(attended, d_branch, 0, 0)
+                yield
+                d_attended = low(over(perm, low(over(d_branch, wo_ref[...], 1, 1))))
+                yield
+                for tile in range(size // length):
+                    base = step * size + tile * length
+                    query, key, value, same = tile_inputs(qkv_ref, col_ref, row_ref, base, length, head)
+                    probs = tile_probs(query, key, bias_ref[...], same)
+                    d_out = d_attended[tile * length : (tile + 1) * length, :]
+                    d_probs = over(d_out, value, 1, 1)
+                    inner = jnp.sum(probs * d_probs, axis=-1, keepdims=True)
+                    d_scores = low(probs * (d_probs - inner))
+                    bias_grad_ref[...] += d_scores.astype(jnp.float32)
+                    dq_ref[base + length : base + 2 * length, :] = low(over(d_scores, key))
+                    both = jnp.concatenate((over(d_scores, query, 0, 0), over(low(probs), d_out, 0, 0)), axis=1)
+                    dkv_ref[base : base + 3 * length, :] += both
+                    if tile % 2:
+                        yield
+            if step > 0:
+                at = slice(length + (step - 1) * size, length + step * size)
+                rows = low(over(perm, jnp.concatenate((dq_ref[at, :], low(dkv_ref[at, :])), axis=1), 0, 0))
+                wait_all(stage.fetch(step - 1, (x_all_ref,), (1,)))
+                w_grad_ref[...] += over(rows, in_refs[1][(step - 1) % 2].reshape(size, width), 0, 0)
+                yield
+                if step > max(first, 1):
+                    wait_all(stage.store(step - 2, (part_ref,)))
+                for i in range(2):
+                    there = pl.ds(i * count // 2, count // 2)
+                    block = over(rows[i * size // 2 : (i + 1) * size // 2], w_ref[...], 1, 1)
+                    out_refs[0][there] = low(block).reshape(count // 2, FEW, width)
+                start_all(stage.store(step - 1, (part_ref,)))
+                yield
+        if last > max(first, 1):
+            wait_all(stage.store(last - 2, (part_ref,)))
+        yield
+
+    for ref in (wo_grad_ref, bias_grad_ref, dkv_ref, w_grad_ref):
+        ref[...] = jnp.zeros_like(ref)
+    halves = len(ranges)
+    everything = pl.ds(0, cuts[-1])
+    tasks = {
+        "d": ([], stage.gathering("d", 0, d_ref, d_all_ref, everything, g_sems)),
+        "down": ([], stage.scattering("down", (forth_ref,), (down_ref,), everything, other_bufs, down_sems, 0)),
+        "output": (["down"], output()),
+        "owners": ([f"back{halves - 1}"], owners()),
+    }
+    for i, rows in enumerate(ranges):
+        h = str(i)
+        first_step = cuts[i] // FEW + 1 if i else 0
+        tasks |= {
+            "back" + h: ([f"back{i - 1}"] if i else ["d"], backing(first_step, cuts[i + 1] // FEW + 1)),
+            "one" + h: (["back" + h], stage.scattering("one" + h, (part_ref,), (dn_ref,), rows, bufs, one_sems, i)),
+        }
+    tasks["finals"] = ([f"one{i}" for i in range(halves)], finals())
+    weave(tasks, REAR_ORDER)
+    stage.finish()
+
+
+def rear(d_rows, normed_all, attended, qkv, qkv_w, wo, perm, bias, col, row, near_grad, forth, middle, rows_low, d_mid, gain,
+         spread, turn, buckets):
+    count, rows, width = normed_all.shape
+    cuts = halves_of(rows)
+    halves = len(cuts) - 1
+    head = wo.shape[0]
+    columns = 4 * head
+    size, piece = perm.shape[0], width // spread.shape[0]
+    all_rows, group = (count, rows, width), (count, FEW, width)
+    bf, wide, dma = jnp.bfloat16, jnp.float32, pltpu.SemaphoreType.DMA
+    vmem, hbm = pl.BlockSpec(memory_space=pltpu.VMEM), pl.BlockSpec(memory_space=pl.ANY)
+    shape = jax.ShapeDtypeStruct
+    outs = pl.pallas_call(
+        functools.partial(rear_kernel, cuts),
+        out_shape=[
+            shape((head, width), wide), shape((width, columns), bf), shape((size, piece), bf), shape((size, 128), bf),
+            shape((size, piece), bf),
+        ] + [shape(all_rows, bf)] * 2,
+        in_specs=[vmem, hbm] + [vmem] * 9 + [hbm] + [vmem] * 7,
+        out_specs=[vmem, hbm, hbm, vmem, hbm] + [hbm] * 2,
+        scratch_shapes=[
+            pltpu.VMEM((rows, width), wide), pltpu.VMEM((rows, width), wide), pltpu.VMEM(bias.shape, wide),
+            pltpu.VMEM((qkv.shape[0], head), bf), pltpu.VMEM((qkv.shape[0], 2 * head), wide),
+            pltpu.VMEM((3 * head, width), wide), pltpu.VMEM((width, columns), bf),
+            pltpu.VMEM((size, piece), bf), pltpu.VMEM((size, piece + 128), bf), pltpu.VMEM((size, piece + 128), bf),
+            pltpu.VMEM((size, piece), bf),
+        ] + scatter_bufs(rows, width, 1) * 2 + [
+            pltpu.VMEM((2,) + group, bf), pltpu.VMEM((2,) + group, bf), pltpu.VMEM(group, bf),
+            dma((2, 2)), dma((1,)),
+        ] + [dma((count,)), dma((count,)), dma] * 4 + [
+            dma((1,)), dma((1, N_GATHER_SENDS)), dma((1, 2, 32)),
+        ] + scatter_sems(halves, 1) + scatter_sems(1, 1),
+        name="rear",
+        compiler_params=pltpu.CompilerParams(collective_id=4, has_side_effects=True, vmem_limit_bytes=63 * 2**20),
+    )(d_rows, normed_all, attended, qkv, qkv_w, wo, perm, bias, col, row, near_grad, forth, middle, rows_low, d_mid, gain,
+      spread, turn, buckets)
+    return outs[:5]
+
+
+def exchange(blocks):
+    return lax.all_to_all(blocks, AXIS, split_axis=0, concat_axis=0, tiled=True)
+
+
+def dot(left, right):
+    return jnp.dot(left, right, preferred_element_type=jnp.float32)
+
+
+def select(mask, rows):
+    return dot(mask.astype(jnp.bfloat16), rows).astype(jnp.bfloat16)
+
+
+def beside(sent, chain, kernel):
+    sent, chain = lax.optimization_barrier((sent, chain))
+    return lax.optimization_barrier((exchange(sent), kernel(chain)))
+
+
+def pack_kernel(query_ref, key_ref, value_ref, gate_ref, up_ref, first_ref, second_ref):
+    count = first_ref.shape[0]
+    head = query_ref.shape[1] // count
+    units = gate_ref.shape[1] // count
+    for j in range(count):
+        for i, ref in enumerate((query_ref, key_ref, value_ref)):
+            first_ref[j, :, i * head : (i + 1) * head] = ref[:, j * head : (j + 1) * head]
+        first_ref[j, :, 3 * head :] = gate_ref[:, j * units : j * units + head]
+        second_ref[j, :, : units - head] = gate_ref[:, j * units + head : (j + 1) * units]
+        second_ref[j, :, units - head :] = up_ref[:, j * units : (j + 1) * units]
+
+
+def pack(shards, count):
+    rows, width = shards[0].shape
+    head, units = width // count, shards[3].shape[1] // count
+    return pl.pallas_call(
+        pack_kernel,
+        out_shape=[
+            jax.ShapeDtypeStruct((count, rows, 4 * head), jnp.bfloat16),
+            jax.ShapeDtypeStruct((count, rows, 2 * units - head), jnp.bfloat16),
+        ],
+        in_specs=[pl.BlockSpec(memory_space=pltpu.VMEM)] * 5,
+        out_specs=[pl.BlockSpec(memory_space=pltpu.VMEM)] * 2,
+        name="pack_columns",
+        compiler_params=pltpu.CompilerParams(vmem_limit_bytes=32 * 2**20),
+    )(*shards)
+
+
+def unpack_kernel(first_ref, second_ref, query_ref, key_ref, value_ref, gate_ref, up_ref):
+    count = first_ref.shape[0]
+    head = query_ref.shape[1] // count
+    units = gate_ref.shape[1] // count
+    wide = jnp.float32
+    for j in range(count):
+        for i, ref in enumerate((query_ref, key_ref, value_ref)):
+            ref[:, j * head : (j + 1) * head] = first_ref[j, :, i * head : (i + 1) * head].astype(wide)
+        gate_ref[:, j * units : j * units + head] = first_ref[j, :, 3 * head :].astype(wide)
+        gate_ref[:, j * units + head : (j + 1) * units] = second_ref[j, :, : units - head].astype(wide)
+        up_ref[:, j * units : (j + 1) * units] = second_ref[j, :, units - head :].astype(wide)
+
+
+def unpack(first, second, width, hidden):
+    rows = first.shape[1]
+    widths = (width, width, width, hidden, hidden)
+    return pl.pallas_call(
+        unpack_kernel,
+        out_shape=[jax.ShapeDtypeStruct((rows, columns), jnp.float32) for columns in widths],
+        in_specs=[pl.BlockSpec(memory_space=pltpu.VMEM)] * 2,
+        out_specs=[pl.BlockSpec(memory_space=pltpu.VMEM)] * 5,
+        name="unpack_columns",
+        compiler_params=pltpu.CompilerParams(vmem_limit_bytes=32 * 2**20),
+    )(first, second)
+
+
+def body(
+    tokens,
+    lengths,
+    permutation,
+    query_weight,
+    key_weight,
+    value_weight,
+    out_weight,
+    gate_weight,
+    up_weight,
+    down_weight,
+    gain_attention,
+    gain_feedforward,
+    bias_table,
+    cotangent,
+):
+    me = lax.axis_index(AXIS)
+    count = tokens.shape[0]
+    grain = tokens.shape[1]
+    length = cotangent.shape[1]
+    width = tokens.shape[2]
+    shard = query_weight.shape[0]
+    hidden_width = gate_weight.shape[1] // count
+    head = HEAD_DIM
+    total = 3 * count * length // 5
+    tiles = -(-total // length)
+    slots = tiles * grain
+
+    small = jnp.concatenate((gain_attention, gain_feedforward, bias_table))
+    small = jnp.pad(small, (0, grain * 128 - small.shape[0])).reshape(1, grain, 128)
+    small = jnp.broadcast_to(small, (count, grain, 128))
+    came = exchange(jnp.concatenate((tokens[permutation], small), axis=2))
+    dealt = came[:, :, :width].reshape(length, width)
+    small = came[:, :, width:].reshape(count, -1)
+    gain_one = small[:, :shard].reshape(-1).astype(jnp.float32)
+    gain_two = small[:, shard : 2 * shard].reshape(-1).astype(jnp.float32)
+    table = small[:, 2 * shard : 2 * shard + HEADS]
+
+    dealt_lengths = lengths[permutation]
+    ends = jnp.cumsum(dealt_lengths)
+    starts = ends - dealt_lengths
+    my_start, my_length = starts[me], dealt_lengths[me]
+    place_in = jnp.arange(length, dtype=jnp.int32)
+    turn = (
+        (place_in[:, None] - my_start) % length == place_in[None, :]
+    ) & (place_in[None, :] < my_length)
+    slot_ids = jnp.arange(slots, dtype=jnp.int32)
+    packed_ids = slot_ids // grain * length + me * grain + slot_ids % grain
+    source_seq = jnp.sum((packed_ids[:, None] >= ends[None, :]).astype(jnp.int32), axis=1)
+    pick = (source_seq * grain + slot_ids % grain)[:, None] == place_in[None, :]
+
+    def spread_out(rows):
+        return select(turn, rows).reshape(count, grain, width)
+
+    def packed_block(came):
+        return select(pick, came.reshape(length, width))
+
+    rows_low = packed_block(exchange(spread_out(dealt)))
+    rows_in = rows_low.astype(jnp.float32)
+    first_columns, second_columns = pack(
+        (query_weight, key_weight, value_weight, gate_weight, up_weight), count
+    )
+
+    all_ids = jnp.arange(tiles * length, dtype=jnp.int32)
+    segment = jnp.sum((all_ids[:, None] >= ends[None, :]).astype(jnp.int32), axis=1) + 1
+    column, row = segment[:, None], jnp.pad(segment, (length, length))[None, :]
+    relative = (
+        jnp.arange(3 * length, dtype=jnp.int32)[None, :] - length - place_in[:, None]
+    ).reshape(-1)
+    onehot = bucket_index(relative)[None, :] == jnp.arange(BUCKETS, dtype=jnp.int32)[:, None]
+    head_table = lax.dynamic_slice_in_dim(table, me, 1, axis=1)
+    rel_bias = dot(head_table.T, onehot.astype(jnp.bfloat16)).reshape(length, 3 * length)
+    few = 16
+    ids = jnp.arange(few * count, dtype=jnp.int32)
+    ids = ids % length // grain * few + ids // length * grain + ids % grain
+    perm = (ids[:, None] == jnp.arange(few * count, dtype=jnp.int32)[None, :]).astype(jnp.bfloat16)
+
+    scale_one = norm_scale(rows_in)
+    normed = (rows_in * scale_one * gain_one).astype(jnp.bfloat16)
+    cut = (count, -1, 4 * head)
+    sent = jnp.concatenate((first_columns, spread_out(cotangent[0]).reshape(cut)), axis=1)
+    normed, perm, rel_bias, column, row = lax.optimization_barrier(
+        (normed, perm, rel_bias, column, row)
+    )
+    came, normed_all = beside(sent, normed, gather)
+    first_columns = came[:, :shard].reshape(-1, 4 * head)
+    upstream_low = packed_block(came[:, shard:])
+    qkv_columns, gate_columns = first_columns[:, : 3 * head], first_columns[:, 3 * head :]
+    shared = (out_weight, perm, rel_bias, column, row)
+    (qkv, attended, middle, d_middle, d_low, gain_two_grad, near_grad, far_grad, down_grad, forth) = front(
+        normed_all, rows_low, upstream_low, gain_two[None, :], qkv_columns, gate_columns, second_columns, down_weight, *shared
+    )
+
+    folds = few // grain
+    piece = width // folds
+    share = jnp.arange(few * count, dtype=jnp.int32)
+    share_row, share_fold = share // few * grain + share % grain, share % few // grain
+    turned = (starts[None, :] + (me * grain + jnp.arange(grain, dtype=jnp.int32)[:, None] - starts[None, :]) % length).T
+    back_slot = (turned // length * grain + jnp.arange(grain, dtype=jnp.int32)[None, :]).reshape(-1)
+    spread = (back_slot[share_row][:, None] == slot_ids[None, :])[None] & (
+        share_fold[None, :, None] == jnp.arange(folds, dtype=jnp.int32)[:, None, None]
+    )
+    back_turn = (
+        ((share_row[None, :] - my_start) % length == share_row[:, None])
+        & (share_row[:, None] < my_length)
+        & (share_fold[:, None] == share_fold[None, :])
+    )
+
+    high = lax.reduce_precision(gain_two_grad, 8, 7)
+    sums = jnp.stack((high, gain_two_grad - high)).astype(jnp.bfloat16).reshape(2, count, shard)
+    sums = jnp.pad(sums.transpose(1, 0, 2).reshape(count, 1, -1), ((0, 0), (0, few - 1), (0, 4 * head - 2 * shard)))
+    sent = jnp.concatenate((far_grad.astype(jnp.bfloat16).T.reshape(count, shard, -1), sums), axis=1)
+    given = (
+        d_low, normed_all, attended, qkv, qkv_columns, *shared, near_grad, forth, middle, rows_low, d_middle, gain_one[None, :],
+        spread.astype(jnp.bfloat16), back_turn.astype(jnp.bfloat16), bucket_index(relative).reshape(length, -1),
+    )
+    came, (out_grad, first_grad, out_rows, other_sums, token_rows) = beside(sent, given, lambda given: rear(*given))
+    second_grad, sums = came[:, :shard], came[:, shard].astype(jnp.float32)
+    first_grad = first_grad.reshape(count, shard, -1)
+    other_sums = other_sums.reshape(count, few, -1).astype(jnp.float32)
+    gain_attention_grad = jnp.sum(other_sums[:, 0, :shard] + other_sums[:, 0, shard : 2 * shard], axis=0)
+    gain_feedforward_grad = jnp.sum(sums[:, :shard] + sums[:, shard : 2 * shard], axis=0)
+    table_grad = other_sums[:, 1, 0] + other_sums[:, 1, 1]
+
+    def whole_rows(shares):
+        return shares.reshape(count, folds, grain, piece).transpose(0, 2, 1, 3).reshape(count, grain, width)
+
+    layer_output = select(turn.T, whole_rows(out_rows).reshape(length, width))[None]
+    tokens_grad = whole_rows(token_rows)[jnp.argsort(permutation)]
+    query_grad, key_grad, value_grad, gate_grad, up_grad = unpack(
+        first_grad, second_grad, width, hidden_width * count
+    )
+    return (
+        layer_output,
+        tokens_grad,
+        query_grad,
+        key_grad,
+        value_grad,
+        out_grad,
+        gate_grad,
+        up_grad,
+        down_grad,
+        gain_attention_grad,
+        gain_feedforward_grad,
+        table_grad,
+    )
+
+
 def solution(mesh):
     placed = (
         P(None, "fsdp", None),
@@ -302,7 +1401,7 @@
         P("fsdp", None, None),
     )
     return jax.shard_map(
-        body,
+        body if mesh.shape[AXIS] == 32 else body_any,
         mesh=mesh,
         in_specs=placed,
         out_specs=(

time: 2500 us -> 621 us (0.25)
  waiting for transfers between devices: 2020 us -> 13.2 us
  Pallas kernels: 0 us -> 524 us
  matrix products: 201 us -> 5.58 us
  other arithmetic: 111 us -> 19.8 us
  blocking collectives: 82.3 us -> 0 us
    reduce_scatter x2 -> x0, waiting for transfers between devices: 1580 us -> none  [the longest x1 1140 us: body(): lax.psum_scatter(jnp.concatenate((rows_product(normed, d_qkv), jnp.concat...]
    pallas_call x0 -> x5, Pallas kernels: none -> 524 us  [the longest x1 238 us: front(): pl.pallas_call(functools.partial(front_kernel, cuts), out_shape=[shape((r...]
    all_gather x2 -> x0, waiting for transfers between devices: 440 us -> none  [the longest x1 343 us: body(): lax.all_gather(shards[0], 'fsdp', axis=0, tiled=True)]
    dot_general x20 -> x6, matrix products: 201 us -> 5.58 us  [dot(): return jnp.dot(left, right, preferred_element_type=jnp.float32)]
    concatenate x1 -> x3, other arithmetic: 98.5 us -> 3.6 us  [the longest x1 1.37 us: body(): jnp.concatenate((first_columns, spread_out(cotangent[0]).reshape(cut)), a...]
    unnamed x2 -> x0, blocking collectives: 82.3 us -> none
  transfers between devices with their start and end apart: 6 -> 4, of which waited for: 4 -> 2; matrix products, arithmetic and copies ran while one was open for 5% -> 4% of each run, Pallas kernels for 0% -> 46%
where the time goes in v4:
time: 621 us; the launch traced here: 614 us
  Pallas kernels  524 us (84%)
  starting transfers between devices  27.1 us (4%)
  local copies, waits for them, and re-layouts  23.5 us (4%)
  other arithmetic  19.8 us (3%)
  waiting for transfers between devices  13.2 us (2%)
    pallas_call x1, Pallas kernels, front(): pl.pallas_call(functools.partial(front_kernel, cuts), out_shape=[shape((r...  238 us
    pallas_call x1, Pallas kernels, rear(): pl.pallas_call(functools.partial(rear_kernel, cuts), out_shape=[shape((he...  216 us
    pallas_call x1, Pallas kernels, gather(): pl.pallas_call(gather_kernel, out_shape=jax.ShapeDtypeStruct((32, rows, w...  66.5 us
    all_to_all x4, starting transfers between devices, exchange(): return lax.all_to_all(blocks, AXIS, split_axis=0, concat_axis=0, tiled=True)  27.1 us
    all_to_all x4, waiting for transfers between devices, exchange(): return lax.all_to_all(blocks, AXIS, split_axis=0, concat_axis=0, tiled=True)  13.2 us
  transfers between devices with their start and end apart: 4, of which 2 were waited for; matrix products, arithmetic and copies ran while one was open for 4% of the time, Pallas kernels for 46%

profile of v4, /device:TPU:29, one launch (start us, length us, event | category | flops | bytes accessed | tf_op | source)
XLA Modules:
  0.0 614.4 jit_solution(7896012738832094043)
XLA Ops:
  4.6 6.2 %all-to-all-start = ((bf16[32,4,2176]{2,1,0:T(4,128)(2,1)}), bf16[32,4,2176]{2,1,0:T(4,128)(2,1)S(1)}, u32[]{:S(2)}, u32[]{:S(2)}) async-start(bf16[32,4,2176]{2,1,0:T(4,128)(2,1)} %pad_maximum_fusion.1), calls=%async_computation | async-start | bytes 1114112 | tf_op jit(solution)/shard_map/all_to_all | solution.py:1168
  15.0 1.4 convolution_convert_fusion.2
  18.7 1.4 pad_maximum_fusion
  20.1 3.9 all-to-all-done
  25.8 6.0 all-to-all-start.1
  33.2 1.2 fusion.1
  35.1 9.3 %all-to-all-done.1 = bf16[32,4,2048]{2,1,0:T(4,128)(2,1)S(1)} async-done(((bf16[32,4,2048]{2,1,0:T(4,128)(2,1)}), bf16[32,4,2048]{2,1,0:T(4,128)(2,1)S(1)}, u32[]{:S(2)}, u32[]{:S(2)}) %all-to-all-start.1) | async-done | bytes 524320 | tf_op jit(solution)/shard_map/all_to_all | solution.py:1168
  45.8 6.1 all-to-all-start.2
  52.3 3.3 gather_fusion.2
  57.2 1.1 and_convert_fusion.refs_17_
  58.3 1.1 and_convert_fusion.1.refs_16_
  60.8 66.5 %gather_rows.1.refs_0_.refs_1_ = bf16[32,80,2048]{2,1,0:T(8,128)(2,1)} custom-call(bf16[80,2048]{1,0:T(8,128)(2,1)} %fusion.10.a_ref), custom_call_target="tpu_custom_call" | custom-call | tf_op jit(solution)/shard_map/gather_rows/pallas_call | solution.py:603
  127.3 1.5 copy.46.refs_11_
  131.3 237.8 %front.1 = (bf16[2816,192]{1,0:T(8,128)(2,1)}, bf16[32,80,64]{2,1,0:T(8,128)(2,1)}, f32[80,2048]{1,0:T(8,128)}, f32[80,2048]{1,0:T(8,128)}, bf16[80,2048]{1,0:T(...) custom-call(bf16[32,80,2048]{2,1,0:T(8,128)(2,1)} %gather_rows.1.ref, ...), custom_call_target="tpu_custom_call" | custom-call | tf_op jit(solution)/shard_map/front/pallas_call | solution.py:927
  369.1 1.7 convert_bitcast_fusion
  371.9 1.2 fusion.6
  373.1 8.8 %all-to-all-start.3 = ((bf16[32,80,256]{2,1,0:T(8,128)(2,1)}), bf16[32,80,256]{2,1,0:T(8,128)(2,1)}, u32[]{:S(2)}, u32[]{:S(2)}) async-start(bf16[32,80,256]{2,1,0:T(8,128)(2,1)} %fusion.6), calls=%async_computation.3 | async-start | bytes 2621440 | tf_op jit(solution)/shard_map/all_to_all | solution.py:1168
  382.0 1.6 sort.17
  383.6 1.5 copy.51.refs_8_
  385.1 215.6 %rear.1 = (f32[64,2048]{1,0:T(8,128)}, bf16[2048,256]{1,0:T(8,128)(2,1)}, bf16[512,512]{1,0:T(8,128)(2,1)}, bf16[512,128]{1,0:T(8,128)(2,1)}, bf16[512,512]{1,0:...) custom-call(bf16[80,2048]{1,0:T(8,128)(2,1)} %get-tuple-element.91.refs_0_, ...), custom_call_target="tpu_custom_call" | custom-call | tf_op jit(solution)/shard_map/rear/pallas_call | solution.py:1140
  602.4 1.3 slice.60.second_ref
  605.3 1.2 fusion.5
  607.8 2.8 unpack_columns.1
  610.6 1.8 gather_fusion.3
  (131 shorter events, 28.6 us)
Async XLA Ops:
  0.6 1.1 copy-start
  1.7 9.1 %copy-start.9 = (s32[32]{0:T(128)S(1)}, s32[32]{0:T(128)}, u32[]{:S(2)}) copy-start(s32[32]{0:T(128)} %param.15) | copy-start | bytes 388
  4.6 19.5 %all-to-all-start = ((bf16[32,4,2176]{2,1,0:T(4,128)(2,1)}), bf16[32,4,2176]{2,1,0:T(4,128)(2,1)S(1)}, u32[]{:S(2)}, u32[]{:S(2)}) async-start(bf16[32,4,2176]{2,1,0:T(4,128)(2,1)} %pad_maximum_fusion.1), calls=%async_computation | async-start | bytes 1114112 | tf_op jit(solution)/shard_map/all_to_all | solution.py:1168
  10.7 6.7 %copy-start.4 = (bf16[64,5120]{1,0:T(8,128)(2,1)S(1)}, bf16[64,5120]{1,0:T(8,128)(2,1)}, u32[]{:S(2)}) copy-start(bf16[64,5120]{1,0:T(8,128)(2,1)} %gate_ref.1) | copy-start | bytes 1966084
  10.7 6.7 %copy-start.5 = (bf16[64,5120]{1,0:T(8,128)(2,1)S(1)}, bf16[64,5120]{1,0:T(8,128)(2,1)}, u32[]{:S(2)}) copy-start(bf16[64,5120]{1,0:T(8,128)(2,1)} %up_ref.1) | copy-start | bytes 1966084
  10.7 6.7 %copy-start.6 = (bf16[64,2048]{1,0:T(8,128)(2,1)S(1)}, bf16[64,2048]{1,0:T(8,128)(2,1)}, u32[]{:S(2)}) copy-start(bf16[64,2048]{1,0:T(8,128)(2,1)} %query_ref.1) | copy-start | bytes 786436
  10.8 6.7 %copy-start.7 = (bf16[64,2048]{1,0:T(8,128)(2,1)S(1)}, bf16[64,2048]{1,0:T(8,128)(2,1)}, u32[]{:S(2)}) copy-start(bf16[64,2048]{1,0:T(8,128)(2,1)} %key_ref.1) | copy-start | bytes 786436
  10.8 6.7 %copy-start.8 = (bf16[64,2048]{1,0:T(8,128)(2,1)S(1)}, bf16[64,2048]{1,0:T(8,128)(2,1)}, u32[]{:S(2)}) copy-start(bf16[64,2048]{1,0:T(8,128)(2,1)} %value_ref.1) | copy-start | bytes 786436
  17.5 1.2 copy-start.12
  18.6 1.5 copy-start.3
  25.8 18.6 %all-to-all-start.1 = ((bf16[32,4,2048]{2,1,0:T(4,128)(2,1)}), bf16[32,4,2048]{2,1,0:T(4,128)(2,1)S(1)}, u32[]{:S(2)}, u32[]{:S(2)}) async-start(bf16[32,4,2048]{2,1,0:T(4,128)(2,1)} %reshape.568), calls=%async_computation.1 | async-start | bytes 1048576 | tf_op jit(solution)/shard_map/all_to_all | solution.py:1168
  32.0 12.4 %copy-start.14 = (s32[128,384]{1,0:T(8,128)}, s32[128,384]{1,0:T(8,128)S(1)}, u32[]{:S(2)}) copy-start(s32[128,384]{1,0:T(8,128)S(1)} %fusion.12.refs_18_) | copy-start | bytes 589828
  44.9 0.9 copy-start.11
  45.8 83.1 %all-to-all-start.2 = ((bf16[32,96,256]{2,1,0:T(8,128)(2,1)}), bf16[32,96,256]{2,1,0:T(8,128)(2,1)S(1)}, u32[]{:S(2)}, u32[]{:S(2)}) async-start(bf16[32,96,256]{2,1,0:T(8,128)(2,1)} %pad_maximum_fusion), calls=%async_computation.2 | async-start | bytes 3145728 | tf_op jit(solution)/shard_map/all_to_all | solution.py:1168
  128.9 1.4 copy-start.10
  370.9 0.7 copy-start.18
  373.1 8.9 %copy-start.19 = (s32[32]{0:T(128)S(1)}, s32[32]{0:T(128)}, u32[]{:S(2)}) copy-start(s32[32]{0:T(128)} %param.16) | copy-start | bytes 388
  373.1 227.6 %all-to-all-start.3 = ((bf16[32,80,256]{2,1,0:T(8,128)(2,1)}), bf16[32,80,256]{2,1,0:T(8,128)(2,1)}, u32[]{:S(2)}, u32[]{:S(2)}) async-start(bf16[32,80,256]{2,1,0:T(8,128)(2,1)} %fusion.6), calls=%async_computation.3 | async-start | bytes 2621440 | tf_op jit(solution)/shard_map/all_to_all | solution.py:1168
  600.7 4.1 copy-start.17
  604.9 1.6 copy-start.16
  605.2 2.6 copy-start.2
  607.8 4.5 copy-start.15
  610.6 2.6 copy-start.13
  612.3 1.9 copy-start.1

commit v5 on v4

--- a/solution.py
+++ b/solution.py
@@ -588,27 +588,52 @@
         yield
 
 
-def gather_kernel(a_ref, o_ref, own_sem, ssem, rsem):
-    spot = Spot()
-    spot.greet()
-    sends = Sends(ssem)
-    for _ in gather_steps(spot, a_ref, o_ref, pl.ds(0, a_ref.shape[0]), sends, rsem, own_sem):
-        pass
-    sends.finish()
-
-
-def gather(block):
-    rows, width = block.shape
-    dma = pltpu.SemaphoreType.DMA
-    return pl.pallas_call(
-        gather_kernel,
-        out_shape=jax.ShapeDtypeStruct((32, rows, width), block.dtype),
-        in_specs=[pl.BlockSpec(memory_space=pl.ANY)],
-        out_specs=pl.BlockSpec(memory_space=pl.ANY),
-        scratch_shapes=[dma, dma((N_GATHER_SENDS,)), dma((2, 32))],
-        name="gather_rows",
-        compiler_params=pltpu.CompilerParams(collective_id=0, has_side_effects=True),
-    )(block)
+def swap(spot, count, src, dst, sems, what, some=None):
+    begin, end = some or (1, count)
+    send_sem, recv_sem, own_sem = sems
+    share = src.shape[0] // count
+
+    def part(ref, index):
+        return ref.at[pl.ds(pl.multiple_of(index * share, share), share), :]
+
+    def own():
+        return pltpu.make_async_copy(part(src, spot.me), part(dst, spot.me), own_sem)
+
+    def one(d, _):
+        peer, source = (spot.me + d) % count, (spot.me + count - d) % count
+        if what == "send":
+            pltpu.make_async_remote_copy(
+                part(src, peer), part(dst, spot.me), send_sem.at[peer], recv_sem.at[spot.me], device_id=(peer,),
+                device_id_type=MESH,
+            ).start()
+        else:
+            copy = pltpu.make_async_remote_copy(
+                part(src, peer), part(dst, source), send_sem.at[peer], recv_sem.at[source], device_id=(peer,),
+                device_id_type=MESH,
+            )
+            copy.wait_recv()
+            copy.wait_send()
+        return _
+
+    if what == "send" and begin == 1:
+        own().start()
+    lax.fori_loop(begin, end, one, 0)
+    if what == "wait" and end == count:
+        own().wait()
+
+
+def pack(weights, first_ref, second_ref):
+    query_ref, key_ref, value_ref, gate_ref, up_ref = weights
+    rows = query_ref.shape[0]
+    count = first_ref.shape[0] // rows
+    head, units = query_ref.shape[1] // count, gate_ref.shape[1] // count
+    for j in range(count):
+        there = pl.ds(j * rows, rows)
+        for i, ref in enumerate((query_ref, key_ref, value_ref)):
+            first_ref[there, i * head : (i + 1) * head] = ref[:, j * head : (j + 1) * head]
+        first_ref[there, 3 * head :] = gate_ref[:, j * units : j * units + head]
+        second_ref[there, : units - head] = gate_ref[:, j * units + head : (j + 1) * units]
+        second_ref[there, units - head :] = up_ref[:, j * units : (j + 1) * units]
 
 
 def weave(tasks, order):
@@ -633,25 +658,27 @@
 
 
 FRONT_ORDER = (
-    (0, 1), (2, 1), (1, 1), (2, 9), (1, 1), (2, 3), (1, 1), (2, 1), (1, 2), (3, 8), (1, 1), (3, 4), (1, 1),
-    (9, 8), (10, 1), (3, 1), (1, 1), (3, 1), (10, 1), (1, 1), (3, 1), (10, 2), (3, 1), (10, 1), (3, 1), (10,
-    2), (1, 2), (3, 4), (10, 1), (3, 4), (10, 5), (0, 1), (1, 1), (10, 2), (3, 1), (1, 3), (3, 2), (1, 1), (3,
-    1), (1, 1), (3, 4), (10, 4), (3, 1), (10, 1), (3, 1), (10, 5), (1, 4), (3, 1), (1, 2), (3, 1), (1, 6),
-    (10, 3), (4, 1), (5, 1), (10, 4), (1, 3), (10, 3), (5, 1), (10, 1), (5, 1), (10, 1), (11, 1), (5, 26),
-    (12, 1), (5, 3), (12, 1), (6, 1), (12, 3), (6, 1), (12, 4), (6, 1), (12, 2), (6, 1), (12, 6), (6, 1), (12,
-    1), (6, 1), (12, 12), (6, 1), (12, 2), (7, 12), (13, 2), (7, 2), (13, 1), (7, 6), (13, 1), (7, 3), (13,
-    1), (14, 1), (7, 4), (14, 1), (7, 1), (14, 9), (7, 9), (8, 1), (14, 26), (15, 1),
+    (0, 1), (2, 1), (0, 1), (2, 4), (0, 2), (4, 5), (2, 1), (3, 1), (4, 16), (1, 1), (4, 11), (6, 1), (1, 1),
+    (5, 1), (6, 8), (5, 1), (6, 2), (5, 1), (6, 2), (5, 1), (6, 1), (5, 1), (7, 5), (13, 1), (7, 1), (13, 1),
+    (7, 2), (13, 1), (5, 1), (13, 2), (7, 4), (5, 1), (13, 3), (14, 1), (7, 1), (5, 1), (7, 1), (14, 1), (3,
+    1), (5, 1), (7, 1), (14, 2), (7, 1), (14, 1), (7, 1), (14, 7), (5, 1), (14, 1), (5, 1), (7, 2), (14, 1),
+    (7, 6), (5, 1), (14, 1), (7, 1), (5, 5), (14, 4), (7, 4), (14, 1), (7, 2), (14, 1), (7, 1), (14, 4), (5,
+    1), (7, 1), (5, 2), (7, 1), (5, 6), (7, 1), (5, 2), (14, 1), (5, 1), (14, 1), (7, 1), (14, 1), (8, 1), (9,
+    1), (14, 2), (5, 1), (14, 1), (3, 1), (5, 2), (14, 1), (3, 1), (14, 3), (9, 1), (14, 1), (9, 1), (14, 1),
+    (15, 1), (9, 18), (3, 1), (9, 8), (16, 1), (9, 3), (16, 1), (10, 1), (16, 3), (10, 1), (16, 4), (10, 1),
+    (16, 2), (10, 1), (16, 5), (10, 1), (16, 1), (10, 1), (16, 11), (10, 1), (16, 2), (11, 1), (16, 1), (11,
+    1), (16, 1), (11, 6), (17, 1), (11, 1), (17, 1), (11, 3), (17, 1), (11, 9), (17, 1), (11, 2), (17, 1),
+    (18, 1), (11, 4), (18, 1), (11, 1), (18, 8), (11, 1), (18, 1), (11, 8), (12, 1), (18, 26), (19, 1),
 )
 REAR_ORDER = (
-    (0, 15), (1, 1), (0, 17), (4, 1), (1, 1), (4, 1), (1, 1), (4, 1), (1, 1), (4, 2), (1, 1), (4, 1), (1, 1),
+    (0, 4), (1, 1), (0, 28), (4, 1), (1, 1), (4, 1), (1, 1), (4, 1), (1, 1), (4, 2), (1, 1), (4, 1), (1, 1),
     (4, 1), (1, 1), (4, 1), (1, 1), (4, 1), (1, 1), (4, 1), (1, 1), (4, 1), (1, 1), (4, 2), (1, 1), (4, 1),
-    (1, 1), (4, 1), (1, 2), (4, 2), (1, 1), (4, 1), (1, 1), (4, 1), (1, 1), (4, 1), (1, 1), (4, 2), (1, 2),
-    (4, 1), (1, 1), (5, 1), (6, 1), (5, 1), (1, 3), (5, 1), (1, 2), (5, 1), (1, 1), (5, 1), (6, 1), (1, 1),
-    (6, 1), (5, 1), (6, 1), (1, 1), (6, 1), (5, 1), (1, 1), (6, 1), (1, 1), (5, 1), (1, 1), (6, 1), (1, 1),
-    (5, 1), (6, 1), (1, 1), (5, 1), (1, 1), (6, 1), (5, 1), (1, 1), (5, 3), (7, 1), (5, 1), (7, 1), (5, 2),
-    (3, 1), (7, 1), (5, 7), (7, 6), (5, 1), (7, 1), (5, 1), (7, 1), (5, 1), (7, 1), (5, 1), (7, 1), (5, 1),
-    (7, 3), (5, 2), (7, 3), (5, 1), (7, 1), (2, 1), (7, 1), (5, 1), (7, 3), (5, 1), (7, 2), (5, 1), (7, 2),
-    (5, 1), (7, 1), (5, 1), (7, 8), (8, 1), (3, 1), (2, 1), (8, 2),
+    (1, 1), (4, 1), (1, 2), (4, 2), (1, 1), (4, 1), (1, 1), (4, 1), (1, 1), (4, 1), (1, 1), (4, 2), (1, 3),
+    (4, 1), (5, 1), (6, 1), (5, 1), (1, 3), (5, 1), (1, 2), (5, 1), (1, 1), (5, 1), (6, 1), (1, 1), (5, 1),
+    (1, 1), (5, 1), (6, 3), (1, 1), (5, 1), (1, 1), (6, 1), (1, 1), (5, 1), (1, 1), (6, 1), (5, 1), (1, 1),
+    (6, 2), (3, 1), (1, 1), (5, 1), (1, 1), (5, 12), (7, 1), (5, 1), (7, 2), (5, 4), (7, 2), (5, 1), (3, 1),
+    (7, 4), (5, 2), (7, 2), (5, 1), (7, 1), (2, 1), (7, 1), (5, 1), (7, 3), (5, 1), (7, 2), (5, 1), (7, 2),
+    (5, 1), (7, 1), (5, 1), (7, 4), (2, 1), (7, 12), (8, 3),
 )
 N_GATHER_SENDS = 66
 FEW = 16
@@ -733,55 +760,106 @@
 
 
 def front_kernel(cuts, *refs):
-    (nx_all_ref, rows_ref, up_ref, gain_ref, qkv_w_ref, gate_w_ref, mine_ref, wd_ref, wo_ref, perm_ref, bias_ref, col_ref,
-     row_ref) = refs[:13]
-    (qkv_ref, att_ref, middle_ref, d_mid_ref, d_ref, gain_grad_ref, near_grad_ref, far_grad_ref, wd_grad_ref,
-     forth_ref) = refs[13:23]
-    part_ref, up_all_ref, x_all_ref, back_ref = refs[23:27]
-    branch_ref, x_ref, dn_ref, w_ref = refs[27:31]
-    bufs, two_ref, in_refs, out_refs = refs[31:37], refs[37], refs[38:40], refs[40:42]
-    in_sems, out_sems, w_ssem, w_rsem, w_own = refs[42:47]
-    g_sems, one_sems, two_sems = refs[47:50], refs[50:57], refs[57:64]
-    two_bufs = (bufs[0], two_ref, *bufs[2:])
-    count = part_ref.shape[0]
+    tok_ref, cot_ref, index_ref, small_ref = refs[:4]
+    weights = refs[4:9]
+    wd_ref, wo_ref, perm_ref, bucket_ref, col_ref, row_ref = refs[9:15]
+    (rows_ref, gain_one_ref, bias_ref, first_w_ref, qkv_ref, att_ref, middle_ref, d_mid_ref, d_ref, gain_grad_ref, near_grad_ref,
+     far_grad_ref, wd_grad_ref, nx_all_ref, forth_ref) = refs[15:30]
+    part_ref, up_all_ref, x_all_ref, back_ref = refs[30:34]
+    branch_ref, x_ref, dn_ref, w_ref, nx_ref, up_ref, gain_ref, gate_w_ref = refs[34:42]
+    one_ref, two_ref, cot_out_ref, one_in_ref, two_in_ref, cot_in_ref = refs[42:48]
+    small_out_ref, all_small_ref, first_ref, second_ref = refs[48:52]
+    bufs, two_total_ref, in_refs, out_refs = refs[52:58], refs[58], refs[59:61], refs[61:63]
+    in_sems, out_sems = refs[63:65]
+    exchanges = refs[65:83]
+    one_x, two_x, cot_x, small_x, first_x, second_x = [exchanges[i : i + 3] for i in range(0, 18, 3)]
+    g_sems, one_sems, two_sems = refs[83:86], refs[86:93], refs[93:100]
+    two_bufs = (bufs[0], two_total_ref, *bufs[2:])
+    count, slots, width = x_all_ref.shape
     stage = Stage(count, cuts, in_refs, out_refs, in_sems, out_sems)
     spot, ranges = stage.spot, stage.ranges
+    units, head, length = wd_ref.shape[0], wo_ref.shape[0], bias_ref.shape[0]
+    size, piece = one_ref.shape
+    folds, share = width // piece, size // count
+    grain = share // folds
+    groups = cuts[-1] // FEW
+    near = units - head
     spot.greet_all(count)
-    width, units, head, length = rows_ref.shape[1], wd_ref.shape[0], wo_ref.shape[0], bias_ref.shape[0]
-    size = perm_ref.shape[0]
-    groups = cuts[-1] // FEW
-    shard = mine_ref.shape[1]
-    near = units - head
-
-    def column_blocks(what):
-        def one(d, _):
-            peer = (spot.me + d) % count
-            source = (spot.me + count - d) % count
-            if what == "send":
-                pltpu.make_async_remote_copy(
-                    mine_ref.at[peer], w_ref.at[pl.ds(pl.multiple_of(spot.me * shard, shard), shard), :], w_ssem.at[peer],
-                    w_rsem.at[spot.me], device_id=(peer,), device_id_type=MESH,
-                ).start()
-            else:
-                there = w_ref.at[pl.ds(pl.multiple_of(source * shard, shard), shard), :]
-                copy = pltpu.make_async_remote_copy(
-                    there, there, w_ssem.at[peer], w_rsem.at[source], device_id=(peer,), device_id_type=MESH,
+
+    def at(shape, axis):
+        return lax.broadcasted_iota(jnp.int32, shape, axis)
+
+    def marked(mask):
+        return low(jnp.where(mask, 1.0, 0.0))
+
+    def folded(rows, sources):
+        shape = (length, size)
+        return low(
+            sum(
+                over(
+                    marked((at(shape, 0) == sources) & (at(shape, 1) % share // grain == i)),
+                    rows[:, i * piece : (i + 1) * piece], 0, 0,
                 )
-                copy.wait_recv()
-                copy.wait_send()
-            return _
-
-        lax.fori_loop(1, count, one, 0)
-
-    def columns():
-        own = pltpu.make_async_copy(
-            mine_ref.at[spot.me], w_ref.at[pl.ds(pl.multiple_of(spot.me * shard, shard), shard), :], w_own
+                for i in range(folds)
+            )
         )
-        own.start()
-        column_blocks("send")
-        yield
-        column_blocks("wait")
-        own.wait()
+
+    def pick(shares, to_ref):
+        source = index_ref[2:3, :slots]
+        for i in range(folds):
+            mask = at((size, slots), 0) == source + i * grain
+            to_ref[:, i * piece : (i + 1) * piece] = low(over(marked(mask), shares, 0, 0))
+
+    def tokens():
+        for i in range(count):
+            small_out_ref[i * share : (i + 1) * share, :] = small_ref[...]
+        one_ref[...] = folded(tok_ref[...], index_ref[0:1, :])
+        swap(spot, count, one_ref, one_in_ref, one_x, "send")
+        swap(spot, count, small_out_ref, all_small_ref, small_x, "send")
+        yield
+        swap(spot, count, one_ref, one_in_ref, one_x, "wait")
+        place = index_ref[1:2, :]
+        place = jnp.where(place < 0, -1, place // grain * share + place % grain + at((1, size), 1) % share // grain * grain)
+        two_ref[...] = low(over(marked(at((size, size), 0) == place), one_in_ref[...], 0, 0))
+        swap(spot, count, two_ref, two_in_ref, two_x, "send")
+        yield
+        swap(spot, count, small_out_ref, all_small_ref, small_x, "wait")
+        each = width // count
+        shape = (2 * each, width)
+        mine = at((size, width), 0) == at((size, width), 1) // each * share
+        for i, ref in enumerate((gain_one_ref, gain_ref)):
+            fold = marked(at(shape, 0) == at(shape, 1) % each + i * each)
+            ref[...] = jnp.sum(jnp.where(mine, over(all_small_ref[...], fold), 0.0), axis=0, keepdims=True)
+        table = jnp.where(at(all_small_ref.shape, 1) == spot.me, all_small_ref[...].astype(jnp.float32), 0.0)
+        table = jnp.sum(table, axis=1, keepdims=True)
+        bias_ref[...] = sum(
+            jnp.where(bucket_ref[...] == b, table[b * share + 1 : b * share + 2, :], 0.0) for b in range(BUCKETS)
+        )
+        yield
+        swap(spot, count, two_ref, two_in_ref, two_x, "wait")
+        pick(two_in_ref[...], rows_ref)
+        v = rows_ref[...].astype(jnp.float32)
+        nx_ref[...] = (v * scale_of(v) * gain_one_ref[...]).astype(nx_ref.dtype)
+        yield
+
+    def cotangent():
+        cot_out_ref[...] = folded(cot_ref[...], index_ref[1:2, :])
+        swap(spot, count, cot_out_ref, cot_in_ref, cot_x, "send")
+        yield
+        swap(spot, count, cot_out_ref, cot_in_ref, cot_x, "wait")
+        pick(cot_in_ref[...], up_ref)
+        yield
+
+    def columns(src, dst, sems, packs):
+        if packs:
+            pack(weights, first_ref, second_ref)
+            yield
+        for i in range(0, count, 8):
+            swap(spot, count, src, dst, sems, "send", (max(i, 1), i + 8))
+            yield
+        swap(spot, count, src, dst, sems, "wait")
+        if packs:
+            gate_w_ref[...] = dst[:, 3 * head :]
         yield
 
     def attending(first, last):
@@ -795,7 +873,7 @@
                 if step + 1 < groups:
                     start_all(stage.fetch(step + 1, (nx_all_ref,)))
                 wait_all(stage.fetch(step, (nx_all_ref,)))
-                rows = low(over(in_refs[0][step % 2].reshape(size, -1), qkv_w_ref[...]))
+                rows = low(over(in_refs[0][step % 2].reshape(size, -1), first_w_ref[:, : 3 * head]))
                 qkv_ref[length + step * size : length + (step + 1) * size, :] = low(over(perm, rows))
                 yield
             if step > 0:
@@ -882,23 +960,28 @@
     for ref in (near_grad_ref, far_grad_ref, wd_grad_ref, gain_grad_ref):
         ref[...] = jnp.zeros_like(ref)
     halves = len(ranges)
+    everything = pl.ds(0, slots)
     tasks = {
-        "columns": ([], columns()),
-        "up": ([], stage.gathering("up", 0, up_ref, up_all_ref, pl.ds(0, cuts[-1]), g_sems)),
+        "tokens": ([], tokens()),
+        "cot": ([], cotangent()),
+        "first": ([], columns(first_ref, first_w_ref, first_x, True)),
+        "second": (["first"], columns(second_ref, w_ref, second_x, False)),
+        "gather": (["tokens"], stage.gathering("gather", 0, nx_ref, nx_all_ref, everything, g_sems)),
+        "up": (["cot"], stage.gathering("up", 1, up_ref, up_all_ref, everything, g_sems)),
     }
     for i, rows in enumerate(ranges):
         h = str(i)
         last_step = groups + 1 if i == halves - 1 else cuts[i + 1] // FEW + 1
         first_step = cuts[i] // FEW + 1 if i else 0
         tasks |= {
-            "attend" + h: ([f"attend{i - 1}"] if i else [], attending(first_step, last_step)),
+            "attend" + h: ([f"attend{i - 1}"] if i else ["gather", "first"], attending(first_step, last_step)),
             "one" + h: (
                 ["attend" + h], stage.scattering("one" + h, (part_ref,), (branch_ref,), rows, bufs, one_sems, i),
             ),
             "norm" + h: (["one" + h], first_norm(rows)),
-            "x" + h: (["norm" + h], stage.gathering("x" + h, 1 + i, x_ref, x_all_ref, rows, g_sems)),
+            "x" + h: (["norm" + h], stage.gathering("x" + h, 2 + i, x_ref, x_all_ref, rows, g_sems)),
             "feed" + h: (
-                ["x" + h, "up", "columns", f"feed{i - 1}" if i else f"attend{halves - 1}"],
+                ["x" + h, "up", "second", f"feed{i - 1}" if i else f"attend{halves - 1}"],
                 feeding(cuts[i] // FEW, cuts[i + 1] // FEW),
             ),
             "two" + h: (
@@ -915,69 +998,44 @@
     return (0, 48, 80) if rows == 80 else (0, rows)
 
 
-def front(normed_all, rows_low, upstream_low, gain, qkv_w, gate_w, mine, wd, wo, perm, bias, col, row):
-    count, rows, width = normed_all.shape
-    cuts = halves_of(rows)
+def front(tok, cot, index, small, weights, wd, wo, perm, buckets, col, row, slots):
+    size, (length, width) = index.shape[1], tok.shape
+    shard = weights[0].shape[0]
+    count, piece = width // shard, length * width // size
+    cuts = halves_of(slots)
     halves = len(cuts) - 1
-    head, length, size = wo.shape[0], bias.shape[0], perm.shape[0]
-    low_rows, all_rows, group = (rows, width), (count, rows, width), (count, FEW, width)
+    head, units = wo.shape[0], wd.shape[0]
+    low_rows, all_rows, group, share = (slots, width), (count, slots, width), (count, FEW, width), (size, piece)
+    first, second = (width, 4 * head), (width, 2 * units - head)
     bf, wide, dma = jnp.bfloat16, jnp.float32, pltpu.SemaphoreType.DMA
     vmem, hbm = pl.BlockSpec(memory_space=pltpu.VMEM), pl.BlockSpec(memory_space=pl.ANY)
     shape = jax.ShapeDtypeStruct
     outs = pl.pallas_call(
         functools.partial(front_kernel, cuts),
         out_shape=[
-            shape((rows // FEW * size + 2 * length, 3 * head), bf), shape((count, rows, head), bf), shape(low_rows, wide),
+            shape(low_rows, bf), shape((1, width), wide), shape(buckets.shape, wide), shape(first, bf),
+            shape((slots // FEW * size + 2 * length, 3 * head), bf), shape((count, slots, head), bf), shape(low_rows, wide),
             shape(low_rows, wide), shape(low_rows, bf), shape((1, width), wide), shape((head, width), wide),
-            shape((mine.shape[2], width), wide), shape(wd.shape, wide),
-        ] + [shape(all_rows, bf)] * 5,
-        in_specs=[hbm] + [vmem] * 5 + [hbm] + [vmem] * 6,
-        out_specs=[vmem] * 9 + [hbm] * 5,
+            shape((second[1], width), wide), shape(wd.shape, wide),
+        ] + [shape(all_rows, bf)] * 6,
+        in_specs=[vmem] * 15,
+        out_specs=[vmem] * 13 + [hbm] * 6,
         scratch_shapes=[
-            pltpu.VMEM(low_rows, wide), pltpu.VMEM(low_rows, bf), pltpu.VMEM(low_rows, wide),
-            pltpu.VMEM((width, mine.shape[2]), bf),
-        ] + scatter_bufs(rows, width, 1) + [
-            pltpu.VMEM((16, rows, width), bf),
+            pltpu.VMEM(low_rows, wide), pltpu.VMEM(low_rows, bf), pltpu.VMEM(low_rows, wide), pltpu.VMEM(second, bf),
+            pltpu.VMEM(low_rows, bf), pltpu.VMEM(low_rows, bf), pltpu.VMEM((1, width), wide), pltpu.VMEM((width, head), bf),
+        ] + [pltpu.VMEM(share, bf)] * 6 + [
+            pltpu.VMEM((size, 128), bf), pltpu.VMEM((size, 128), bf), pltpu.VMEM(first, bf), pltpu.VMEM(second, bf),
+        ] + scatter_bufs(slots, width, 1) + [
+            pltpu.VMEM((16, slots, width), bf),
             pltpu.VMEM((2,) + group, bf), pltpu.VMEM((2,) + group, bf), pltpu.VMEM(group, bf), pltpu.VMEM(group, bf),
-            dma((2, 2)), dma((2,)), dma((count,)), dma((count,)), dma,
-            dma((1 + halves,)), dma((1 + halves, N_GATHER_SENDS)), dma((1 + halves, 2, 32)),
+            dma((2, 2)), dma((2,)),
+        ] + [dma((count,)), dma((count,)), dma] * 6 + [
+            dma((2 + halves,)), dma((2 + halves, N_GATHER_SENDS)), dma((2 + halves, 2, 32)),
         ] + scatter_sems(halves, 1) * 2,
         name="front",
         compiler_params=pltpu.CompilerParams(collective_id=3, has_side_effects=True, vmem_limit_bytes=63 * 2**20),
-    )(normed_all, rows_low, upstream_low, gain, qkv_w, gate_w, mine, wd, wo, perm, bias, col, row)
-    return outs[:10]
-
-
-def swap(spot, count, src, dst, sems, what):
-    send_sem, recv_sem, own_sem = sems
-    share = src.shape[0] // count
-
-    def part(ref, index):
-        return ref.at[pl.ds(pl.multiple_of(index * share, share), share), :]
-
-    own = pltpu.make_async_copy(part(src, spot.me), part(dst, spot.me), own_sem)
-
-    def one(d, _):
-        peer, source = (spot.me + d) % count, (spot.me + count - d) % count
-        if what == "send":
-            pltpu.make_async_remote_copy(
-                part(src, peer), part(dst, spot.me), send_sem.at[peer], recv_sem.at[spot.me], device_id=(peer,),
-                device_id_type=MESH,
-            ).start()
-        else:
-            copy = pltpu.make_async_remote_copy(
-                part(src, peer), part(dst, source), send_sem.at[peer], recv_sem.at[source], device_id=(peer,),
-                device_id_type=MESH,
-            )
-            copy.wait_recv()
-            copy.wait_send()
-        return _
-
-    if what == "send":
-        own.start()
-    lax.fori_loop(1, count, one, 0)
-    if what == "wait":
-        own.wait()
+    )(tok, cot, index, small, *weights, wd, wo, perm, buckets, col, row)
+    return outs[:15]
 
 
 def rear_kernel(cuts, *refs):
@@ -1095,7 +1153,7 @@
                     wait_all(stage.store(step - 2, (part_ref,)))
                 for i in range(2):
                     there = pl.ds(i * count // 2, count // 2)
-                    block = over(rows[i * size // 2 : (i + 1) * size // 2], w_ref[...], 1, 1)
+                    block = over(rows[i * size // 2 : (i + 1) * size // 2], w_ref[:, : 3 * head], 1, 1)
                     out_refs[0][there] = low(block).reshape(count // 2, FEW, width)
                 start_all(stage.store(step - 1, (part_ref,)))
                 yield
@@ -1181,34 +1239,6 @@
     return lax.optimization_barrier((exchange(sent), kernel(chain)))
 
 
-def pack_kernel(query_ref, key_ref, value_ref, gate_ref, up_ref, first_ref, second_ref):
-    count = first_ref.shape[0]
-    head = query_ref.shape[1] // count
-    units = gate_ref.shape[1] // count
-    for j in range(count):
-        for i, ref in enumerate((query_ref, key_ref, value_ref)):
-            first_ref[j, :, i * head : (i + 1) * head] = ref[:, j * head : (j + 1) * head]
-        first_ref[j, :, 3 * head :] = gate_ref[:, j * units : j * units + head]
-        second_ref[j, :, : units - head] = gate_ref[:, j * units + head : (j + 1) * units]
-        second_ref[j, :, units - head :] = up_ref[:, j * units : (j + 1) * units]
-
-
-def pack(shards, count):
-    rows, width = shards[0].shape
-    head, units = width // count, shards[3].shape[1] // count
-    return pl.pallas_call(
-        pack_kernel,
-        out_shape=[
-            jax.ShapeDtypeStruct((count, rows, 4 * head), jnp.bfloat16),
-            jax.ShapeDtypeStruct((count, rows, 2 * units - head), jnp.bfloat16),
-        ],
-        in_specs=[pl.BlockSpec(memory_space=pltpu.VMEM)] * 5,
-        out_specs=[pl.BlockSpec(memory_space=pltpu.VMEM)] * 2,
-        name="pack_columns",
-        compiler_params=pltpu.CompilerParams(vmem_limit_bytes=32 * 2**20),
-    )(*shards)
-
-
 def unpack_kernel(first_ref, second_ref, query_ref, key_ref, value_ref, gate_ref, up_ref):
     count = first_ref.shape[0]
     head = query_ref.shape[1] // count
@@ -1263,41 +1293,32 @@
     tiles = -(-total // length)
     slots = tiles * grain
 
-    small = jnp.concatenate((gain_attention, gain_feedforward, bias_table))
-    small = jnp.pad(small, (0, grain * 128 - small.shape[0])).reshape(1, grain, 128)
-    small = jnp.broadcast_to(small, (count, grain, 128))
-    came = exchange(jnp.concatenate((tokens[permutation], small), axis=2))
-    dealt = came[:, :, :width].reshape(length, width)
-    small = came[:, :, width:].reshape(count, -1)
-    gain_one = small[:, :shard].reshape(-1).astype(jnp.float32)
-    gain_two = small[:, shard : 2 * shard].reshape(-1).astype(jnp.float32)
-    table = small[:, 2 * shard : 2 * shard + HEADS]
-
     dealt_lengths = lengths[permutation]
     ends = jnp.cumsum(dealt_lengths)
     starts = ends - dealt_lengths
     my_start, my_length = starts[me], dealt_lengths[me]
     place_in = jnp.arange(length, dtype=jnp.int32)
-    turn = (
-        (place_in[:, None] - my_start) % length == place_in[None, :]
-    ) & (place_in[None, :] < my_length)
     slot_ids = jnp.arange(slots, dtype=jnp.int32)
     packed_ids = slot_ids // grain * length + me * grain + slot_ids % grain
     source_seq = jnp.sum((packed_ids[:, None] >= ends[None, :]).astype(jnp.int32), axis=1)
-    pick = (source_seq * grain + slot_ids % grain)[:, None] == place_in[None, :]
-
-    def spread_out(rows):
-        return select(turn, rows).reshape(count, grain, width)
-
-    def packed_block(came):
-        return select(pick, came.reshape(length, width))
-
-    rows_low = packed_block(exchange(spread_out(dealt)))
-    rows_in = rows_low.astype(jnp.float32)
-    first_columns, second_columns = pack(
-        (query_weight, key_weight, value_weight, gate_weight, up_weight), count
-    )
-
+
+    few = 16
+    folds = few // grain
+    piece = width // folds
+    share = jnp.arange(few * count, dtype=jnp.int32)
+    share_row, share_fold = share // few * grain + share % grain, share % few // grain
+    position = share_row - my_start % length
+    position = jnp.where(position < 0, position + length, position)
+    in_share = jnp.arange(few, dtype=jnp.int32)[None, :] % grain
+    index = jnp.stack(
+        (
+            (permutation[:, None] * grain + in_share).reshape(-1),
+            jnp.where(position < my_length, position, -1),
+            jnp.pad(jnp.where(source_seq < count, source_seq * few + slot_ids % grain, -few), (0, few * count - slots)),
+        )
+    )
+    small = jnp.concatenate((gain_attention, gain_feedforward, bias_table))
+    small = jnp.pad(small, (0, few * 128 - small.shape[0])).reshape(few, 128)
     all_ids = jnp.arange(tiles * length, dtype=jnp.int32)
     segment = jnp.sum((all_ids[:, None] >= ends[None, :]).astype(jnp.int32), axis=1) + 1
     column, row = segment[:, None], jnp.pad(segment, (length, length))[None, :]
@@ -1305,40 +1326,27 @@
         jnp.arange(3 * length, dtype=jnp.int32)[None, :] - length - place_in[:, None]
     ).reshape(-1)
     onehot = bucket_index(relative)[None, :] == jnp.arange(BUCKETS, dtype=jnp.int32)[:, None]
-    head_table = lax.dynamic_slice_in_dim(table, me, 1, axis=1)
-    rel_bias = dot(head_table.T, onehot.astype(jnp.bfloat16)).reshape(length, 3 * length)
-    few = 16
     ids = jnp.arange(few * count, dtype=jnp.int32)
     ids = ids % length // grain * few + ids // length * grain + ids % grain
     perm = (ids[:, None] == jnp.arange(few * count, dtype=jnp.int32)[None, :]).astype(jnp.bfloat16)
 
-    scale_one = norm_scale(rows_in)
-    normed = (rows_in * scale_one * gain_one).astype(jnp.bfloat16)
-    cut = (count, -1, 4 * head)
-    sent = jnp.concatenate((first_columns, spread_out(cotangent[0]).reshape(cut)), axis=1)
-    normed, perm, rel_bias, column, row = lax.optimization_barrier(
-        (normed, perm, rel_bias, column, row)
-    )
-    came, normed_all = beside(sent, normed, gather)
-    first_columns = came[:, :shard].reshape(-1, 4 * head)
-    upstream_low = packed_block(came[:, shard:])
-    qkv_columns, gate_columns = first_columns[:, : 3 * head], first_columns[:, 3 * head :]
+    buckets = bucket_index(relative).reshape(length, -1)
+    (rows_low, gain_one, rel_bias, first_columns, qkv, attended, middle, d_middle, d_low, gain_two_grad, near_grad, far_grad,
+     down_grad, normed_all, forth) = front(
+        tokens.reshape(length, width), cotangent[0], index, small,
+        (query_weight, key_weight, value_weight, gate_weight, up_weight), down_weight, out_weight, perm, buckets, column, row,
+        slots,
+    )
     shared = (out_weight, perm, rel_bias, column, row)
-    (qkv, attended, middle, d_middle, d_low, gain_two_grad, near_grad, far_grad, down_grad, forth) = front(
-        normed_all, rows_low, upstream_low, gain_two[None, :], qkv_columns, gate_columns, second_columns, down_weight, *shared
-    )
-
-    folds = few // grain
-    piece = width // folds
-    share = jnp.arange(few * count, dtype=jnp.int32)
-    share_row, share_fold = share // few * grain + share % grain, share % few // grain
-    turned = (starts[None, :] + (me * grain + jnp.arange(grain, dtype=jnp.int32)[:, None] - starts[None, :]) % length).T
-    back_slot = (turned // length * grain + jnp.arange(grain, dtype=jnp.int32)[None, :]).reshape(-1)
-    spread = (back_slot[share_row][:, None] == slot_ids[None, :])[None] & (
+
+    turned = me * grain + in_share - starts[:, None] % length
+    turned = starts[:, None] + jnp.where(turned < 0, turned + length, turned)
+    back_slot = (turned // length * grain + in_share).reshape(-1)
+    spread = (back_slot[:, None] == slot_ids[None, :])[None] & (
         share_fold[None, :, None] == jnp.arange(folds, dtype=jnp.int32)[:, None, None]
     )
     back_turn = (
-        ((share_row[None, :] - my_start) % length == share_row[:, None])
+        (position[None, :] == share_row[:, None])
         & (share_row[:, None] < my_length)
         & (share_fold[:, None] == share_fold[None, :])
     )
@@ -1348,8 +1356,8 @@
     sums = jnp.pad(sums.transpose(1, 0, 2).reshape(count, 1, -1), ((0, 0), (0, few - 1), (0, 4 * head - 2 * shard)))
     sent = jnp.concatenate((far_grad.astype(jnp.bfloat16).T.reshape(count, shard, -1), sums), axis=1)
     given = (
-        d_low, normed_all, attended, qkv, qkv_columns, *shared, near_grad, forth, middle, rows_low, d_middle, gain_one[None, :],
-        spread.astype(jnp.bfloat16), back_turn.astype(jnp.bfloat16), bucket_index(relative).reshape(length, -1),
+        d_low, normed_all, attended, qkv, first_columns, *shared, near_grad, forth, middle, rows_low, d_middle, gain_one,
+        spread.astype(jnp.bfloat16), back_turn.astype(jnp.bfloat16), buckets,
     )
     came, (out_grad, first_grad, out_rows, other_sums, token_rows) = beside(sent, given, lambda given: rear(*given))
     second_grad, sums = came[:, :shard], came[:, shard].astype(jnp.float32)
@@ -1362,7 +1370,10 @@
     def whole_rows(shares):
         return shares.reshape(count, folds, grain, piece).transpose(0, 2, 1, 3).reshape(count, grain, width)
 
-    layer_output = select(turn.T, whole_rows(out_rows).reshape(length, width))[None]
+    place = place_in - my_start % length
+    place = jnp.where(place < 0, place + length, place)
+    turned_back = (place[None, :] == place_in[:, None]) & (place_in[:, None] < my_length)
+    layer_output = select(turned_back, whole_rows(out_rows).reshape(length, width))[None]
     tokens_grad = whole_rows(token_rows)[jnp.argsort(permutation)]
     query_grad, key_grad, value_grad, gate_grad, up_grad = unpack(
         first_grad, second_grad, width, hidden_width * count

time: 621 us -> 608 us (0.979)
  Pallas kernels: 524 us -> 556 us
  starting transfers between devices: 27.1 us -> 8.99 us
  waiting for transfers between devices: 13.2 us -> 0.01 us
  local copies, waits for them, and re-layouts: 23.5 us -> 14.6 us
    pallas_call x3 -> x1, Pallas kernels: 305 us -> 338 us  [front(): pl.pallas_call(functools.partial(front_kernel, cuts), out_shape=[shape(lo...]
    all_to_all x4 -> x1, starting transfers between devices: 27.1 us -> 8.99 us  [exchange(): return lax.all_to_all(blocks, AXIS, split_axis=0, concat_axis=0, tiled=True)]
    all_to_all x4 -> x1, waiting for transfers between devices: 13.2 us -> 0.01 us  [exchange(): return lax.all_to_all(blocks, AXIS, split_axis=0, concat_axis=0, tiled=True)]
  transfers between devices with their start and end apart: 4 -> 1, of which waited for: 2 -> 0; matrix products, arithmetic and copies ran while one was open for 4% -> 1% of each run, Pallas kernels for 46% -> 36%
where the time goes in v5:
time: 608 us; the launch traced here: 601 us
  Pallas kernels  556 us (91%)
  other arithmetic  17.1 us (3%)
  local copies, waits for them, and re-layouts  14.6 us (2%)
  starting transfers between devices  8.99 us (1%)
    pallas_call x1, Pallas kernels, front(): pl.pallas_call(functools.partial(front_kernel, cuts), out_shape=[shape(lo...  338 us
    pallas_call x1, Pallas kernels, rear(): pl.pallas_call(functools.partial(rear_kernel, cuts), out_shape=[shape((he...  215 us
  transfers between devices with their start and end apart: 1, of which 0 were waited for; matrix products, arithmetic and copies ran while one was open for 1% of the time, Pallas kernels for 36%

profile of v5, /device:TPU:29, one launch (start us, length us, event | category | flops | bytes accessed | tf_op | source)
XLA Modules:
  0.0 601.2 jit_solution(15933523019320499699)
XLA Ops:
  0.7 0.7 broadcast_multiply_fusion
  7.4 1.5 copy.43.refs_13_
  9.5 0.9 fusion.3.refs_11_.refs_6_
  10.5 0.9 fusion.4.refs_12_.refs_18_
  11.3 0.9 reshape.519.refs_0_
  13.5 338.0 %front.1 = (bf16[80,2048]{1,0:T(8,128)(2,1)}, f32[1,2048]{1,0:T(1,128)}, f32[128,384]{1,0:T(8,128)}, bf16[2048,256]{1,0:T(8,128)(2,1)}, bf16[2816,192]{1,0:T(8,1...) custom-call(bf16[128,2048]{1,0:T(8,128)(2,1)} %reshape.519.refs_0_, ...), custom_call_target="tpu_custom_call" | custom-call | tf_op jit(solution)/shard_map/front/pallas_call | solution.py:1013
  351.5 1.7 convert_bitcast_fusion
  354.8 1.2 fusion.2
  355.9 1.1 and_convert_fusion.1.refs_16_
  357.1 1.1 and_convert_fusion.refs_17_
  358.2 9.0 %all-to-all-start = ((bf16[32,80,256]{2,1,0:T(8,128)(2,1)}), bf16[32,80,256]{2,1,0:T(8,128)(2,1)}, u32[]{:S(2)}, u32[]{:S(2)}) async-start(bf16[32,80,256]{2,1,0:T(8,128)(2,1)} %fusion.2), calls=%async_computation | async-start | bytes 2621440 | tf_op jit(solution)/shard_map/all_to_all | solution.py:1226
  367.2 1.5 copy.48.refs_8_
  368.7 1.6 sort.17
  370.3 215.3 %rear.1 = (f32[64,2048]{1,0:T(8,128)}, bf16[2048,256]{1,0:T(8,128)(2,1)}, bf16[512,512]{1,0:T(8,128)(2,1)}, bf16[512,128]{1,0:T(8,128)(2,1)}, bf16[512,512]{1,0:...) custom-call(bf16[80,2048]{1,0:T(8,128)(2,1)} %get-tuple-element.79.refs_0_, ...), custom_call_target="tpu_custom_call" | custom-call | tf_op jit(solution)/shard_map/rear/pallas_call | solution.py:1198
  585.6 0.7 iota_compare_fusion.7
  586.4 0.9 bitcast_convert_fusion
  588.0 1.3 slice.24.second_ref
  589.3 0.9 slice_convert_fusion
  590.9 1.2 reshape.524
  593.2 2.8 unpack_columns.1
  596.0 1.8 gather_fusion.1
  597.8 1.1 fusion.1
  598.9 0.8 copy.60
  599.7 1.1 copy.61
  (83 shorter events, 9.8 us)
Async XLA Ops:
  0.6 0.8 copy-start
  0.7 10.7 %copy-start.4 = (bf16[32,4,2048]{2,1,0:T(4,128)(2,1)S(1)}, bf16[32,4,2048]{2,1,0:T(4,128)(2,1)}, u32[]{:S(2)}) copy-start(bf16[32,4,2048]{2,1,0:T(4,128)(2,1)} %param.14) | copy-start | bytes 1572868
  0.7 12.2 %copy-start.10 = (bf16[64]{0:T(256)(128)(2,1)S(1)}, bf16[64]{0:T(256)(128)(2,1)}, u32[]{:S(2)}) copy-start(bf16[64]{0:T(256)(128)(2,1)} %param.24) | copy-start | bytes 388
  0.7 12.2 %copy-start.9 = (bf16[64]{0:T(256)(128)(2,1)S(1)}, bf16[64]{0:T(256)(128)(2,1)}, u32[]{:S(2)}) copy-start(bf16[64]{0:T(256)(128)(2,1)} %param.25) | copy-start | bytes 388
  0.7 12.2 %copy-start.8 = (bf16[32]{0:T(256)(128)(2,1)S(1)}, bf16[32]{0:T(256)(128)(2,1)}, u32[]{:S(2)}) copy-start(bf16[32]{0:T(256)(128)(2,1)} %param.26) | copy-start | bytes 196
  351.5 2.3 copy-start.7
  358.2 10.5 %copy-start.11 = (s32[32]{0:T(128)S(1)}, s32[32]{0:T(128)}, u32[]{:S(2)}) copy-start(s32[32]{0:T(128)} %param.16) | copy-start | bytes 388
  358.2 228.2 %all-to-all-start = ((bf16[32,80,256]{2,1,0:T(8,128)(2,1)}), bf16[32,80,256]{2,1,0:T(8,128)(2,1)}, u32[]{:S(2)}, u32[]{:S(2)}) async-start(bf16[32,80,256]{2,1,0:T(8,128)(2,1)} %fusion.2), calls=%async_computation | async-start | bytes 2621440 | tf_op jit(solution)/shard_map/all_to_all | solution.py:1226
  585.6 4.8 copy-start.6
  590.4 2.8 copy-start.2
  596.0 2.9 copy-start.5
  596.0 3.7 copy-start.3
  597.8 3.0 copy-start.1

commit v6 on v5

--- a/solution.py
+++ b/solution.py
@@ -378,7 +378,7 @@
     ).wait_recv()
 
 
-def gather_steps(spot, src, dst, rows, sends, rsem, own_sem):
+def gather_steps(spot, src, dst, rows, sends, rsem, own_sem, between=False):
     half = src.shape[1] // 2
     cols = (pl.ds(0, half), pl.ds(half, half))
     me, mid, shift = spot.me, spot.mid, spot.shift
@@ -421,25 +421,57 @@
         landed(part, b)
         push(part, b, spot.core)
 
-    for j in range(4):
-        if j:
-            for part in (0, 1):
-                from_z(part, j)
-                yield
+    def from_side(part):
+        b = first[part]
+        landed(part, b)
+        push(part, b, spot.n1)
+        push(part, b, spot.n2, when=mid)
+        push(part, b, last[part])
+        push(part, b, spot.core)
+
+    def along_z(part, base, j):
+        b = base + shift[j]
+        landed(part, b)
+        push(part, b, spot.n2 if j == 1 else spot.n1, when=mid)
+        push(part, b, last[part])
+        push(part, b, spot.core)
+
+    if between:
         for part in (0, 1):
-            from_first(part, j)
+            from_side(part)
             yield
-        if j:
+        for j in range(1, 5):
+            if j < 4:
+                for part in (0, 1):
+                    along_z(part, me, j)
+                    yield
+                for part in (0, 1):
+                    along_z(part, first[part], j)
+                    yield
             for part in (0, 1):
                 from_last(part, last[part] + shift[j - 1])
+                from_last(part, spot.diag + shift[j - 1])
                 yield
-    for part in (0, 1):
-        from_last(part, last[part] + shift[3])
-        yield
-    for j in range(4):
+    else:
+        for j in range(4):
+            if j:
+                for part in (0, 1):
+                    from_z(part, j)
+                    yield
+            for part in (0, 1):
+                from_first(part, j)
+                yield
+            if j:
+                for part in (0, 1):
+                    from_last(part, last[part] + shift[j - 1])
+                    yield
         for part in (0, 1):
-            from_last(part, spot.diag + shift[j])
+            from_last(part, last[part] + shift[3])
             yield
+        for j in range(4):
+            for part in (0, 1):
+                from_last(part, spot.diag + shift[j])
+                yield
     for j in range(4):
         for base in (me, spot.x, spot.y, spot.diag):
             for part in (0, 1):
@@ -658,29 +690,29 @@
 
 
 FRONT_ORDER = (
-    (0, 1), (2, 1), (0, 1), (2, 4), (0, 2), (4, 5), (2, 1), (3, 1), (4, 16), (1, 1), (4, 11), (6, 1), (1, 1),
-    (5, 1), (6, 8), (5, 1), (6, 2), (5, 1), (6, 2), (5, 1), (6, 1), (5, 1), (7, 5), (13, 1), (7, 1), (13, 1),
-    (7, 2), (13, 1), (5, 1), (13, 2), (7, 4), (5, 1), (13, 3), (14, 1), (7, 1), (5, 1), (7, 1), (14, 1), (3,
-    1), (5, 1), (7, 1), (14, 2), (7, 1), (14, 1), (7, 1), (14, 7), (5, 1), (14, 1), (5, 1), (7, 2), (14, 1),
-    (7, 6), (5, 1), (14, 1), (7, 1), (5, 5), (14, 4), (7, 4), (14, 1), (7, 2), (14, 1), (7, 1), (14, 4), (5,
-    1), (7, 1), (5, 2), (7, 1), (5, 6), (7, 1), (5, 2), (14, 1), (5, 1), (14, 1), (7, 1), (14, 1), (8, 1), (9,
-    1), (14, 2), (5, 1), (14, 1), (3, 1), (5, 2), (14, 1), (3, 1), (14, 3), (9, 1), (14, 1), (9, 1), (14, 1),
-    (15, 1), (9, 18), (3, 1), (9, 8), (16, 1), (9, 3), (16, 1), (10, 1), (16, 3), (10, 1), (16, 4), (10, 1),
-    (16, 2), (10, 1), (16, 5), (10, 1), (16, 1), (10, 1), (16, 11), (10, 1), (16, 2), (11, 1), (16, 1), (11,
-    1), (16, 1), (11, 6), (17, 1), (11, 1), (17, 1), (11, 3), (17, 1), (11, 9), (17, 1), (11, 2), (17, 1),
-    (18, 1), (11, 4), (18, 1), (11, 1), (18, 8), (11, 1), (18, 1), (11, 8), (12, 1), (18, 26), (19, 1),
+    (0, 2), (2, 3), (0, 1), (2, 2), (0, 1), (4, 12), (2, 1), (4, 15), (1, 1), (4, 5), (6, 1), (3, 1), (6, 8),
+    (1, 1), (5, 1), (6, 5), (5, 2), (7, 6), (13, 1), (7, 1), (13, 1), (7, 1), (13, 1), (5, 1), (13, 2), (7,
+    4), (13, 3), (5, 1), (14, 1), (7, 1), (5, 2), (7, 1), (14, 6), (5, 1), (7, 1), (5, 1), (7, 2), (5, 1),
+    (14, 1), (5, 1), (14, 1), (5, 1), (14, 3), (5, 1), (14, 1), (3, 1), (7, 1), (14, 1), (7, 4), (5, 1), (7,
+    1), (5, 1), (7, 2), (5, 1), (14, 1), (5, 3), (7, 1), (5, 2), (14, 2), (5, 1), (14, 2), (5, 1), (7, 2),
+    (14, 1), (7, 2), (5, 1), (14, 1), (7, 2), (14, 2), (7, 1), (14, 2), (7, 2), (14, 1), (7, 1), (14, 2), (7,
+    1), (8, 1), (9, 1), (14, 6), (9, 1), (14, 1), (9, 6), (14, 1), (9, 2), (14, 1), (9, 2), (3, 1), (9, 1),
+    (15, 1), (9, 15), (3, 1), (9, 4), (16, 2), (3, 1), (10, 1), (16, 3), (10, 1), (16, 4), (10, 1), (16, 2),
+    (10, 1), (16, 5), (10, 1), (16, 1), (10, 1), (16, 11), (10, 1), (16, 2), (11, 1), (16, 1), (11, 1), (16,
+    1), (11, 6), (17, 1), (11, 1), (17, 1), (11, 3), (17, 1), (11, 9), (17, 1), (11, 2), (17, 1), (11, 1),
+    (18, 1), (11, 3), (18, 1), (11, 1), (18, 9), (11, 9), (12, 1), (18, 26), (19, 1),
 )
 REAR_ORDER = (
-    (0, 4), (1, 1), (0, 28), (4, 1), (1, 1), (4, 1), (1, 1), (4, 1), (1, 1), (4, 2), (1, 1), (4, 1), (1, 1),
-    (4, 1), (1, 1), (4, 1), (1, 1), (4, 1), (1, 1), (4, 1), (1, 1), (4, 1), (1, 1), (4, 2), (1, 1), (4, 1),
-    (1, 1), (4, 1), (1, 2), (4, 2), (1, 1), (4, 1), (1, 1), (4, 1), (1, 1), (4, 1), (1, 1), (4, 2), (1, 3),
-    (4, 1), (5, 1), (6, 1), (5, 1), (1, 3), (5, 1), (1, 2), (5, 1), (1, 1), (5, 1), (6, 1), (1, 1), (5, 1),
-    (1, 1), (5, 1), (6, 3), (1, 1), (5, 1), (1, 1), (6, 1), (1, 1), (5, 1), (1, 1), (6, 1), (5, 1), (1, 1),
-    (6, 2), (3, 1), (1, 1), (5, 1), (1, 1), (5, 12), (7, 1), (5, 1), (7, 2), (5, 4), (7, 2), (5, 1), (3, 1),
-    (7, 4), (5, 2), (7, 2), (5, 1), (7, 1), (2, 1), (7, 1), (5, 1), (7, 3), (5, 1), (7, 2), (5, 1), (7, 2),
-    (5, 1), (7, 1), (5, 1), (7, 4), (2, 1), (7, 12), (8, 3),
+    (0, 4), (1, 1), (0, 28), (4, 1), (5, 1), (1, 1), (5, 1), (1, 1), (5, 1), (1, 1), (5, 2), (1, 1), (5, 1),
+    (1, 1), (5, 1), (1, 1), (5, 1), (1, 1), (5, 1), (1, 1), (5, 1), (1, 1), (5, 1), (1, 1), (5, 2), (1, 1),
+    (5, 1), (1, 1), (5, 1), (1, 2), (5, 2), (1, 1), (5, 1), (1, 1), (5, 1), (1, 1), (5, 1), (1, 1), (5, 2),
+    (1, 3), (5, 1), (6, 1), (7, 1), (6, 1), (1, 3), (6, 1), (1, 2), (6, 1), (1, 1), (6, 1), (7, 1), (1, 1),
+    (6, 1), (1, 1), (6, 1), (7, 3), (1, 1), (6, 1), (1, 1), (7, 1), (1, 1), (6, 1), (1, 1), (7, 1), (6, 1),
+    (1, 1), (7, 2), (3, 1), (1, 1), (6, 1), (1, 1), (6, 12), (8, 1), (6, 1), (8, 2), (6, 4), (8, 2), (6, 1),
+    (3, 1), (8, 4), (6, 2), (8, 2), (6, 1), (8, 1), (2, 1), (8, 1), (6, 1), (8, 3), (6, 1), (8, 2), (6, 1),
+    (8, 2), (6, 1), (8, 1), (6, 1), (8, 4), (2, 1), (8, 12), (9, 3),
 )
-N_GATHER_SENDS = 66
+N_GATHER_SENDS = 70
 FEW = 16
 
 
@@ -715,10 +747,10 @@
         self.sends = {}
         self.in_refs, self.out_refs, self.in_sems, self.out_sems = in_refs, out_refs, in_sems, out_sems
 
-    def gathering(self, name, at, src, dst, rows, sems):
+    def gathering(self, name, at, src, dst, rows, sems, between=False):
         own_sem, ssem, rsem = sems
         self.sends[name] = Sends(ssem.at[at])
-        yield from gather_steps(self.spot, src, dst, rows, self.sends[name], rsem.at[at], own_sem.at[at])
+        yield from gather_steps(self.spot, src, dst, rows, self.sends[name], rsem.at[at], own_sem.at[at], between)
 
     def scattering(self, name, p_refs, o_refs, rows, bufs, sems, at):
         self.sends[name] = Sends(sems[0].at[at])
@@ -756,13 +788,29 @@
     query = qkv_ref[pl.ds(base + length, length), :head]
     key = qkv_ref[pl.ds(base, 3 * length), head : 2 * head]
     value = qkv_ref[pl.ds(base, 3 * length), 2 * head :]
-    return query, key, value, col_ref[pl.ds(base, length), :] == row_ref[:, pl.ds(base, 3 * length)]
+    tile = base // length
+    return query, key, value, col_ref[:, tile : tile + 1] == row_ref[:, pl.ds(base, 3 * length)]
+
+
+def at(shape, axis):
+    return lax.broadcasted_iota(jnp.int32, shape, axis)
+
+
+def marked(mask):
+    return low(jnp.where(mask, 1.0, 0.0))
+
+
+def packed_order(size, length, grain):
+    shape = (size, size)
+    row = at((size, 1), 0)
+    return marked(at(shape, 1) == row % length // grain * FEW + row // length * grain + row % grain)
 
 
 def front_kernel(cuts, *refs):
     tok_ref, cot_ref, index_ref, small_ref = refs[:4]
     weights = refs[4:9]
-    wd_ref, wo_ref, perm_ref, bucket_ref, col_ref, row_ref = refs[9:15]
+    wd_ref, wo_ref, bucket_ref, col_ref, row_ref, perm_ref = refs[9:14] + refs[-1:]
+    refs = (None,) + refs[:-1]
     (rows_ref, gain_one_ref, bias_ref, first_w_ref, qkv_ref, att_ref, middle_ref, d_mid_ref, d_ref, gain_grad_ref, near_grad_ref,
      far_grad_ref, wd_grad_ref, nx_all_ref, forth_ref) = refs[15:30]
     part_ref, up_all_ref, x_all_ref, back_ref = refs[30:34]
@@ -785,12 +833,7 @@
     groups = cuts[-1] // FEW
     near = units - head
     spot.greet_all(count)
-
-    def at(shape, axis):
-        return lax.broadcasted_iota(jnp.int32, shape, axis)
-
-    def marked(mask):
-        return low(jnp.where(mask, 1.0, 0.0))
+    perm_ref[...] = packed_order(size, length, grain)
 
     def folded(rows, sources):
         shape = (length, size)
@@ -967,7 +1010,7 @@
         "first": ([], columns(first_ref, first_w_ref, first_x, True)),
         "second": (["first"], columns(second_ref, w_ref, second_x, False)),
         "gather": (["tokens"], stage.gathering("gather", 0, nx_ref, nx_all_ref, everything, g_sems)),
-        "up": (["cot"], stage.gathering("up", 1, up_ref, up_all_ref, everything, g_sems)),
+        "up": (["cot"], stage.gathering("up", 1, up_ref, up_all_ref, everything, g_sems, True)),
     }
     for i, rows in enumerate(ranges):
         h = str(i)
@@ -998,7 +1041,7 @@
     return (0, 48, 80) if rows == 80 else (0, rows)
 
 
-def front(tok, cot, index, small, weights, wd, wo, perm, buckets, col, row, slots):
+def front(tok, cot, index, small, weights, wd, wo, buckets, col, row, slots):
     size, (length, width) = index.shape[1], tok.shape
     shard = weights[0].shape[0]
     count, piece = width // shard, length * width // size
@@ -1018,7 +1061,7 @@
             shape(low_rows, wide), shape(low_rows, bf), shape((1, width), wide), shape((head, width), wide),
             shape((second[1], width), wide), shape(wd.shape, wide),
         ] + [shape(all_rows, bf)] * 6,
-        in_specs=[vmem] * 15,
+        in_specs=[vmem] * 14,
         out_specs=[vmem] * 13 + [hbm] * 6,
         scratch_shapes=[
             pltpu.VMEM(low_rows, wide), pltpu.VMEM(low_rows, bf), pltpu.VMEM(low_rows, wide), pltpu.VMEM(second, bf),
@@ -1031,43 +1074,52 @@
             dma((2, 2)), dma((2,)),
         ] + [dma((count,)), dma((count,)), dma] * 6 + [
             dma((2 + halves,)), dma((2 + halves, N_GATHER_SENDS)), dma((2 + halves, 2, 32)),
-        ] + scatter_sems(halves, 1) * 2,
+        ] + scatter_sems(halves, 1) * 2 + [pltpu.VMEM((size, size), bf)],
         name="front",
         compiler_params=pltpu.CompilerParams(collective_id=3, has_side_effects=True, vmem_limit_bytes=63 * 2**20),
-    )(tok, cot, index, small, *weights, wd, wo, perm, buckets, col, row)
+    )(tok, cot, index, small, *weights, wd, wo, buckets, col, row)
     return outs[:15]
 
 
 def rear_kernel(cuts, *refs):
-    (d_ref, x_all_ref, att_ref, qkv_ref, w_ref, wo_ref, perm_ref, bias_ref, col_ref, row_ref, near_ref, forth_ref, middle_ref,
-     rows_ref, d_mid_ref, gain_ref, spread_ref, turn_ref, bucket_ref) = refs[:19]
-    wo_grad_ref, owned_ref, out_rows_ref, sums_ref, token_rows_ref = refs[19:24]
-    d_all_ref, part_ref = refs[24:26]
-    dn_ref, down_ref, bias_grad_ref, dq_ref, dkv_ref, w_grad_ref, turned_ref, result_ref, going_ref, came_ref, last_ref = refs[26:37]
-    bufs, other_bufs, in_refs, out_refs = refs[37:43], refs[43:49], refs[49:51], refs[51:52]
-    in_sems, out_sems = refs[52:54]
-    w_sems, r_sems, t_sems, l_sems = refs[54:57], refs[57:60], refs[60:63], refs[63:66]
-    g_sems, one_sems, down_sems = refs[66:69], refs[69:76], refs[76:83]
+    (d_ref, x_all_ref, att_ref, qkv_ref, w_ref, wo_ref, bias_ref, col_ref, row_ref, near_ref, far_ref, forth_ref, middle_ref,
+     rows_ref, d_mid_ref, gain_ref, gain_two_ref, index_ref, bucket_ref) = refs[:19]
+    wo_grad_ref, owned_ref, far_owned_ref, out_rows_ref, sums_ref, token_rows_ref = refs[19:25]
+    d_all_ref, part_ref = refs[25:27]
+    dn_ref, down_ref, bias_grad_ref, dq_ref, dkv_ref, w_grad_ref, turned_ref, far_turned_ref = refs[27:35]
+    result_ref, going_ref, came_ref, last_ref, perm_ref = refs[35:40]
+    bufs, other_bufs, in_refs, out_refs = refs[40:46], refs[46:52], refs[52:54], refs[54:55]
+    in_sems, out_sems = refs[55:57]
+    w_sems, f_sems, r_sems, t_sems, l_sems = [refs[i : i + 3] for i in range(57, 72, 3)]
+    g_sems, one_sems, down_sems = refs[72:75], refs[75:82], refs[82:89]
     count, width = part_ref.shape[0], part_ref.shape[2]
     stage = Stage(count, cuts, in_refs, out_refs, in_sems, out_sems)
     spot, ranges = stage.spot, stage.ranges
     spot.greet_all(count)
     head, length, size = wo_ref.shape[0], bias_ref.shape[0], perm_ref.shape[0]
     groups = cuts[-1] // FEW
-    folds, piece = spread_ref.shape[0], result_ref.shape[1]
-
-    def owners():
-        merged = jnp.concatenate((low(w_grad_ref[...]), low(near_ref[...])), axis=0)
+    piece, share = result_ref.shape[1], size // count
+    folds = width // piece
+    grain = share // folds
+    perm_ref[...] = packed_order(size, length, grain)
+
+    def owners(sources, to_ref, owner_ref, sems):
+        merged = jnp.concatenate([low(ref[...]) for ref in sources], axis=0)
         for i in range(0, width, 512):
-            turned_ref[i : i + 512, :] = merged[:, i : i + 512].T
-        swap(spot, count, turned_ref, owned_ref, w_sems, "send")
-        yield
-        swap(spot, count, turned_ref, owned_ref, w_sems, "wait")
+            to_ref[i : i + 512, :] = merged[:, i : i + 512].T
+        swap(spot, count, to_ref, owner_ref, sems, "send")
+        yield
+        swap(spot, count, to_ref, owner_ref, sems, "wait")
         yield
 
     def dealt_out(rows):
+        shape = (rows.shape[0], size)
         return sum(
-            over(spread_ref[i], rows[:, i * piece : (i + 1) * piece]) for i in range(folds)
+            over(
+                marked((at(shape, 0) == index_ref[0:1, :]) & (at(shape, 1) % share // grain == i)),
+                rows[:, i * piece : (i + 1) * piece], 0, 0,
+            )
+            for i in range(folds)
         )
 
     def output():
@@ -1081,15 +1133,15 @@
     def scale_of(v):
         return lax.rsqrt(jnp.sum(v * v, axis=1, keepdims=True) / width + EPSILON)
 
-    def shares(v):
-        shape = (going_ref.shape[0], width)
-        at, to = lax.broadcasted_iota(jnp.int32, shape, 0), lax.broadcasted_iota(jnp.int32, shape, 1)
-        spread = jnp.where(at == to // (width // count) * 16, v, 0.0)
-        fold = lax.broadcasted_iota(jnp.int32, (width, width // count), 0) % (width // count)
-        fold = fold == lax.broadcasted_iota(jnp.int32, (width, width // count), 1)
+    def shares(*values):
+        shape, each = (size, width), width // count
+        spread = 0.0
+        for i, v in enumerate(values):
+            spread += jnp.where(at(shape, 0) == at(shape, 1) // each * share + 2 * i, v, 0.0)
+        fold = marked(at((width, each), 0) % each == at((width, each), 1))
         high = low(spread)
         rest = low(spread - high.astype(jnp.float32))
-        return jnp.concatenate([over(p, low(fold.astype(jnp.float32))) for p in (high, rest)], axis=1)
+        return jnp.concatenate([over(p, fold) for p in (high, rest)], axis=1)
 
     def finals():
         v, d, gain = rows_ref[...].astype(jnp.float32), dn_ref[...], gain_ref[...]
@@ -1098,19 +1150,21 @@
         mean = jnp.sum(w * v, axis=1, keepdims=True) / width
         rows = low(d_mid_ref[...] + scale * w - v * (scale * scale * scale) * mean)
         going_ref[:, :piece] = low(dealt_out(rows))
-        sums = shares(jnp.sum(d * v * scale, axis=0, keepdims=True))
-        at, to = lax.broadcasted_iota(jnp.int32, sums.shape, 0), lax.broadcasted_iota(jnp.int32, sums.shape, 1)
+        sums = shares(jnp.sum(d * v * scale, axis=0, keepdims=True), gain_two_ref[...])
+        row, lane = at(sums.shape, 0), at(sums.shape, 1)
         for b in range(BUCKETS):
             total = jnp.sum(jnp.where(bucket_ref[...] == b, bias_grad_ref[...], 0.0), axis=(0, 1), keepdims=True)
             high = low(total).astype(jnp.float32)
-            sums = sums + jnp.where((at == 16 * b + 1) & (to == 0), high, 0.0)
-            sums = sums + jnp.where((at == 16 * b + 1) & (to == 1), total - high, 0.0)
+            sums = sums + jnp.where((row == share * b + 1) & (lane == 0), high, 0.0)
+            sums = sums + jnp.where((row == share * b + 1) & (lane == 1), total - high, 0.0)
         going_ref[:, piece:] = low(sums)
         swap(spot, count, going_ref, came_ref, t_sems, "send")
         yield
         swap(spot, count, going_ref, came_ref, t_sems, "wait")
         sums_ref[...] = came_ref[:, piece:]
-        last_ref[...] = low(over(turn_ref[...], came_ref[:, :piece]))
+        shape, row, lane = (size, size), at((size, 1), 0), at((1, size), 1)
+        turn = (index_ref[1:2, :] == row // share * grain + row % grain) & (row % share // grain == lane % share // grain)
+        last_ref[...] = low(over(marked(turn), came_ref[:, :piece]))
         swap(spot, count, last_ref, token_rows_ref, l_sems, "send")
         yield
         swap(spot, count, last_ref, token_rows_ref, l_sems, "wait")
@@ -1169,7 +1223,8 @@
         "d": ([], stage.gathering("d", 0, d_ref, d_all_ref, everything, g_sems)),
         "down": ([], stage.scattering("down", (forth_ref,), (down_ref,), everything, other_bufs, down_sems, 0)),
         "output": (["down"], output()),
-        "owners": ([f"back{halves - 1}"], owners()),
+        "owners": ([f"back{halves - 1}"], owners((w_grad_ref, near_ref), turned_ref, owned_ref, w_sems)),
+        "far": ([], owners((far_ref,), far_turned_ref, far_owned_ref, f_sems)),
     }
     for i, rows in enumerate(ranges):
         h = str(i)
@@ -1183,47 +1238,42 @@
     stage.finish()
 
 
-def rear(d_rows, normed_all, attended, qkv, qkv_w, wo, perm, bias, col, row, near_grad, forth, middle, rows_low, d_mid, gain,
-         spread, turn, buckets):
+def rear(d_rows, normed_all, attended, qkv, w, wo, bias, col, row, near_grad, far_grad, forth, middle, rows_low, d_mid, gain,
+         gain_two_grad, index, buckets):
     count, rows, width = normed_all.shape
     cuts = halves_of(rows)
     halves = len(cuts) - 1
-    head = wo.shape[0]
-    columns = 4 * head
-    size, piece = perm.shape[0], width // spread.shape[0]
-    all_rows, group = (count, rows, width), (count, FEW, width)
+    head, size = wo.shape[0], index.shape[1]
+    piece, owned, far = bias.shape[0] * width // size, (width, w.shape[1]), (width, far_grad.shape[0])
+    all_rows, group, share = (count, rows, width), (count, FEW, width), (size, piece)
     bf, wide, dma = jnp.bfloat16, jnp.float32, pltpu.SemaphoreType.DMA
     vmem, hbm = pl.BlockSpec(memory_space=pltpu.VMEM), pl.BlockSpec(memory_space=pl.ANY)
     shape = jax.ShapeDtypeStruct
     outs = pl.pallas_call(
         functools.partial(rear_kernel, cuts),
         out_shape=[
-            shape((head, width), wide), shape((width, columns), bf), shape((size, piece), bf), shape((size, 128), bf),
-            shape((size, piece), bf),
+            shape((head, width), wide), shape(owned, bf), shape(far, bf), shape(share, bf), shape((size, 128), bf),
+            shape(share, bf),
         ] + [shape(all_rows, bf)] * 2,
         in_specs=[vmem, hbm] + [vmem] * 9 + [hbm] + [vmem] * 7,
-        out_specs=[vmem, hbm, hbm, vmem, hbm] + [hbm] * 2,
+        out_specs=[vmem, hbm, hbm, hbm, vmem, hbm] + [hbm] * 2,
         scratch_shapes=[
             pltpu.VMEM((rows, width), wide), pltpu.VMEM((rows, width), wide), pltpu.VMEM(bias.shape, wide),
             pltpu.VMEM((qkv.shape[0], head), bf), pltpu.VMEM((qkv.shape[0], 2 * head), wide),
-            pltpu.VMEM((3 * head, width), wide), pltpu.VMEM((width, columns), bf),
-            pltpu.VMEM((size, piece), bf), pltpu.VMEM((size, piece + 128), bf), pltpu.VMEM((size, piece + 128), bf),
-            pltpu.VMEM((size, piece), bf),
+            pltpu.VMEM((3 * head, width), wide), pltpu.VMEM(owned, bf), pltpu.VMEM(far, bf),
+            pltpu.VMEM(share, bf), pltpu.VMEM((size, piece + 128), bf), pltpu.VMEM((size, piece + 128), bf),
+            pltpu.VMEM(share, bf), pltpu.VMEM((size, size), bf),
         ] + scatter_bufs(rows, width, 1) * 2 + [
             pltpu.VMEM((2,) + group, bf), pltpu.VMEM((2,) + group, bf), pltpu.VMEM(group, bf),
             dma((2, 2)), dma((1,)),
-        ] + [dma((count,)), dma((count,)), dma] * 4 + [
+        ] + [dma((count,)), dma((count,)), dma] * 5 + [
             dma((1,)), dma((1, N_GATHER_SENDS)), dma((1, 2, 32)),
         ] + scatter_sems(halves, 1) + scatter_sems(1, 1),
         name="rear",
         compiler_params=pltpu.CompilerParams(collective_id=4, has_side_effects=True, vmem_limit_bytes=63 * 2**20),
-    )(d_rows, normed_all, attended, qkv, qkv_w, wo, perm, bias, col, row, near_grad, forth, middle, rows_low, d_mid, gain,
-      spread, turn, buckets)
-    return outs[:5]
-
-
-def exchange(blocks):
-    return lax.all_to_all(blocks, AXIS, split_axis=0, concat_axis=0, tiled=True)
+    )(d_rows, normed_all, attended, qkv, w, wo, bias, col, row, near_grad, far_grad, forth, middle, rows_low, d_mid, gain,
+      gain_two_grad, index, buckets)
+    return outs[:6]
 
 
 def dot(left, right):
@@ -1232,11 +1282,6 @@
 
 def select(mask, rows):
     return dot(mask.astype(jnp.bfloat16), rows).astype(jnp.bfloat16)
-
-
-def beside(sent, chain, kernel):
-    sent, chain = lax.optimization_barrier((sent, chain))
-    return lax.optimization_barrier((exchange(sent), kernel(chain)))
 
 
 def unpack_kernel(first_ref, second_ref, query_ref, key_ref, value_ref, gate_ref, up_ref):
@@ -1296,7 +1341,8 @@
     dealt_lengths = lengths[permutation]
     ends = jnp.cumsum(dealt_lengths)
     starts = ends - dealt_lengths
-    my_start, my_length = starts[me], dealt_lengths[me]
+    this = jnp.arange(count, dtype=jnp.int32) == me
+    my_start, my_length = jnp.sum(jnp.where(this, starts, 0)), jnp.sum(jnp.where(this, dealt_lengths, 0))
     place_in = jnp.arange(length, dtype=jnp.int32)
     slot_ids = jnp.arange(slots, dtype=jnp.int32)
     packed_ids = slot_ids // grain * length + me * grain + slot_ids % grain
@@ -1321,51 +1367,31 @@
     small = jnp.pad(small, (0, few * 128 - small.shape[0])).reshape(few, 128)
     all_ids = jnp.arange(tiles * length, dtype=jnp.int32)
     segment = jnp.sum((all_ids[:, None] >= ends[None, :]).astype(jnp.int32), axis=1) + 1
-    column, row = segment[:, None], jnp.pad(segment, (length, length))[None, :]
+    column, row = segment.reshape(tiles, length).T, jnp.pad(segment, (length, length))[None, :]
     relative = (
         jnp.arange(3 * length, dtype=jnp.int32)[None, :] - length - place_in[:, None]
     ).reshape(-1)
     onehot = bucket_index(relative)[None, :] == jnp.arange(BUCKETS, dtype=jnp.int32)[:, None]
-    ids = jnp.arange(few * count, dtype=jnp.int32)
-    ids = ids % length // grain * few + ids // length * grain + ids % grain
-    perm = (ids[:, None] == jnp.arange(few * count, dtype=jnp.int32)[None, :]).astype(jnp.bfloat16)
-
     buckets = bucket_index(relative).reshape(length, -1)
     (rows_low, gain_one, rel_bias, first_columns, qkv, attended, middle, d_middle, d_low, gain_two_grad, near_grad, far_grad,
      down_grad, normed_all, forth) = front(
         tokens.reshape(length, width), cotangent[0], index, small,
-        (query_weight, key_weight, value_weight, gate_weight, up_weight), down_weight, out_weight, perm, buckets, column, row,
-        slots,
-    )
-    shared = (out_weight, perm, rel_bias, column, row)
-
+        (query_weight, key_weight, value_weight, gate_weight, up_weight), down_weight, out_weight, buckets, column, row, slots,
+    )
     turned = me * grain + in_share - starts[:, None] % length
     turned = starts[:, None] + jnp.where(turned < 0, turned + length, turned)
     back_slot = (turned // length * grain + in_share).reshape(-1)
-    spread = (back_slot[:, None] == slot_ids[None, :])[None] & (
-        share_fold[None, :, None] == jnp.arange(folds, dtype=jnp.int32)[:, None, None]
-    )
-    back_turn = (
-        (position[None, :] == share_row[:, None])
-        & (share_row[:, None] < my_length)
-        & (share_fold[:, None] == share_fold[None, :])
-    )
-
-    high = lax.reduce_precision(gain_two_grad, 8, 7)
-    sums = jnp.stack((high, gain_two_grad - high)).astype(jnp.bfloat16).reshape(2, count, shard)
-    sums = jnp.pad(sums.transpose(1, 0, 2).reshape(count, 1, -1), ((0, 0), (0, few - 1), (0, 4 * head - 2 * shard)))
-    sent = jnp.concatenate((far_grad.astype(jnp.bfloat16).T.reshape(count, shard, -1), sums), axis=1)
-    given = (
-        d_low, normed_all, attended, qkv, first_columns, *shared, near_grad, forth, middle, rows_low, d_middle, gain_one,
-        spread.astype(jnp.bfloat16), back_turn.astype(jnp.bfloat16), buckets,
-    )
-    came, (out_grad, first_grad, out_rows, other_sums, token_rows) = beside(sent, given, lambda given: rear(*given))
-    second_grad, sums = came[:, :shard], came[:, shard].astype(jnp.float32)
-    first_grad = first_grad.reshape(count, shard, -1)
-    other_sums = other_sums.reshape(count, few, -1).astype(jnp.float32)
-    gain_attention_grad = jnp.sum(other_sums[:, 0, :shard] + other_sums[:, 0, shard : 2 * shard], axis=0)
-    gain_feedforward_grad = jnp.sum(sums[:, :shard] + sums[:, shard : 2 * shard], axis=0)
-    table_grad = other_sums[:, 1, 0] + other_sums[:, 1, 1]
+
+    out_grad, first_grad, second_grad, out_rows, sums, token_rows = rear(
+        d_low, normed_all, attended, qkv, first_columns, out_weight, rel_bias, column, row, near_grad, far_grad, forth, middle,
+        rows_low, d_middle, gain_one, gain_two_grad, jnp.stack((back_slot, index[1])), buckets,
+    )
+    first_grad, second_grad = first_grad.reshape(count, shard, -1), second_grad.reshape(count, shard, -1)
+    sums = sums.reshape(count, few, -1).astype(jnp.float32)
+    gain_sums = jnp.sum(sums, axis=0)
+    gain_attention_grad = gain_sums[0, :shard] + gain_sums[0, shard : 2 * shard]
+    gain_feedforward_grad = gain_sums[2, :shard] + gain_sums[2, shard : 2 * shard]
+    table_grad = sums[:, 1, 0] + sums[:, 1, 1]
 
     def whole_rows(shares):
         return shares.reshape(count, folds, grain, piece).transpose(0, 2, 1, 3).reshape(count, grain, width)
@@ -1374,7 +1400,9 @@
     place = jnp.where(place < 0, place + length, place)
     turned_back = (place[None, :] == place_in[:, None]) & (place_in[:, None] < my_length)
     layer_output = select(turned_back, whole_rows(out_rows).reshape(length, width))[None]
-    tokens_grad = whole_rows(token_rows)[jnp.argsort(permutation)]
+    ids = jnp.arange(count, dtype=jnp.int32)
+    dealt_slot = jnp.sum(jnp.where(permutation[None, :] == ids[:, None], ids[None, :], 0), axis=1)
+    tokens_grad = whole_rows(token_rows)[dealt_slot]
     query_grad, key_grad, value_grad, gate_grad, up_grad = unpack(
         first_grad, second_grad, width, hidden_width * count
     )

time: 608 us -> 596 us (0.980)
  starting transfers between devices: 8.99 us -> 0 us
  other arithmetic: 17.1 us -> 9.42 us
    all_to_all x1 -> x0, starting transfers between devices: 8.99 us -> none  [exchange(): return lax.all_to_all(blocks, AXIS, split_axis=0, concat_axis=0, tiled=True)]
    pallas_call x1, Pallas kernels: 215 us -> 223 us  [rear(): pl.pallas_call(functools.partial(rear_kernel, cuts), out_shape=[shape((he...]
  transfers between devices with their start and end apart: 1 -> 0, of which waited for: 0 -> 0; matrix products, arithmetic and copies ran while one was open for 1% -> 0% of each run, Pallas kernels for 36% -> 0%
where the time goes in v6:
time: 596 us; the launch traced here: 589 us
  Pallas kernels  561 us (94%)
  local copies, waits for them, and re-layouts  14.7 us (2%)
  other arithmetic  9.42 us (2%)
    pallas_call x1, Pallas kernels, front(): pl.pallas_call(functools.partial(front_kernel, cuts), out_shape=[shape(lo...  335 us
    pallas_call x1, Pallas kernels, rear(): pl.pallas_call(functools.partial(rear_kernel, cuts), out_shape=[shape((he...  223 us

profile of v6, /device:TPU:29, one launch (start us, length us, event | category | flops | bytes accessed | tf_op | source)
XLA Modules:
  0.0 588.8 jit_solution(13942975501661183675)
XLA Ops:
  0.7 0.7 broadcast_multiply_fusion
  1.3 0.7 gather_fusion
  2.3 0.6 and_select_fusion.3
  2.9 0.6 fusion.28
  6.1 0.7 multiply_add_fusion
  6.9 0.6 pad_add_fusion.refs_2_
  7.7 0.7 copy.35
  8.4 0.6 broadcast_in_dim.32.refs_13_.refs_8_
  9.0 0.9 fusion.1.refs_11_.refs_18_
  9.9 2.0 reshape.381.refs_0_
  11.9 1.4 fusion.20.refs_3_
  13.2 335.0 %front.1 = (bf16[80,2048]{1,0:T(8,128)(2,1)}, f32[1,2048]{1,0:T(1,128)}, f32[128,384]{1,0:T(8,128)}, bf16[2048,256]{1,0:T(8,128)(2,1)}, bf16[2816,192]{1,0:T(8,1...) custom-call(bf16[128,2048]{1,0:T(8,128)(2,1)} %reshape.381.refs_0_, ...), custom_call_target="tpu_custom_call" | custom-call | tf_op jit(solution)/shard_map/front/pallas_call | solution.py:1056
  348.8 222.9 %rear.1 = (f32[64,2048]{1,0:T(8,128)}, bf16[2048,256]{1,0:T(8,128)(2,1)}, bf16[2048,256]{1,0:T(8,128)(2,1)}, bf16[512,512]{1,0:T(8,128)(2,1)}, bf16[512,128]{1,0...) custom-call(bf16[80,2048]{1,0:T(8,128)(2,1)} %get-tuple-element.38.refs_0_, ...), custom_call_target="tpu_custom_call" | custom-call | tf_op jit(solution)/shard_map/rear/pallas_call | solution.py:1252
  571.7 0.9 bitcast_convert_fusion
  573.4 1.2 copy-done.2
  574.6 1.2 copy-done.3
  575.8 2.8 unpack_columns.1
  578.6 1.2 reshape.383
  580.2 0.7 iota_compare_fusion.4
  580.8 1.1 fusion
  582.0 1.2 reshape.384
  583.3 1.8 gather_fusion.1
  585.6 1.9 copy.44
  587.5 1.1 copy.45
  (45 shorter events, 3.6 us)
Async XLA Ops:
  0.6 0.7 copy-start
  348.8 234.3 %copy-start.5 = (s32[32]{0:T(128)S(1)}, s32[32]{0:T(128)}, u32[]{:S(2)}) copy-start(s32[32]{0:T(128)} %param.16) | copy-start | bytes 388
  348.8 239.8 %copy-start.1 = (s32[32]{0:T(128)S(1)}, s32[32]{0:T(128)}, u32[]{:S(2)}) copy-start(s32[32]{0:T(128)} %param.15) | copy-start | bytes 388
  573.4 1.2 copy-start.2
  574.6 1.2 copy-start.3
  575.8 11.7 %copy-start.4 = (f32[160,2048]{1,0:T(8,128)S(1)}, f32[160,2048]{1,0:T(8,128)}, u32[]{:S(2)}) copy-start(f32[160,2048]{1,0:T(8,128)} %get-tuple-element.98) | copy-start | bytes 3932164

commit v7 on v6

--- a/solution.py
+++ b/solution.py
@@ -690,7 +690,7 @@
 
 
 FRONT_ORDER = (
-    (0, 2), (2, 3), (0, 1), (2, 2), (0, 1), (4, 12), (2, 1), (4, 15), (1, 1), (4, 5), (6, 1), (3, 1), (6, 8),
+    (0, 2), (2, 3), (0, 1), (2, 2), (0, 1), (4, 5), (2, 1), (4, 20), (1, 1), (4, 7), (6, 1), (3, 1), (6, 8),
     (1, 1), (5, 1), (6, 5), (5, 2), (7, 6), (13, 1), (7, 1), (13, 1), (7, 1), (13, 1), (5, 1), (13, 2), (7,
     4), (13, 3), (5, 1), (14, 1), (7, 1), (5, 2), (7, 1), (14, 6), (5, 1), (7, 1), (5, 1), (7, 2), (5, 1),
     (14, 1), (5, 1), (14, 1), (5, 1), (14, 3), (5, 1), (14, 1), (3, 1), (7, 1), (14, 1), (7, 4), (5, 1), (7,
@@ -700,17 +700,18 @@
     (15, 1), (9, 15), (3, 1), (9, 4), (16, 2), (3, 1), (10, 1), (16, 3), (10, 1), (16, 4), (10, 1), (16, 2),
     (10, 1), (16, 5), (10, 1), (16, 1), (10, 1), (16, 11), (10, 1), (16, 2), (11, 1), (16, 1), (11, 1), (16,
     1), (11, 6), (17, 1), (11, 1), (17, 1), (11, 3), (17, 1), (11, 9), (17, 1), (11, 2), (17, 1), (11, 1),
-    (18, 1), (11, 3), (18, 1), (11, 1), (18, 9), (11, 9), (12, 1), (18, 26), (19, 1),
+    (18, 1), (11, 3), (18, 1), (11, 1), (18, 9), (11, 8), (18, 3), (11, 1), (18, 13), (12, 1), (18, 10), (19,
+    1),
 )
 REAR_ORDER = (
-    (0, 4), (1, 1), (0, 28), (4, 1), (5, 1), (1, 1), (5, 1), (1, 1), (5, 1), (1, 1), (5, 2), (1, 1), (5, 1),
-    (1, 1), (5, 1), (1, 1), (5, 1), (1, 1), (5, 1), (1, 1), (5, 1), (1, 1), (5, 1), (1, 1), (5, 2), (1, 1),
-    (5, 1), (1, 1), (5, 1), (1, 2), (5, 2), (1, 1), (5, 1), (1, 1), (5, 1), (1, 1), (5, 1), (1, 1), (5, 2),
-    (1, 3), (5, 1), (6, 1), (7, 1), (6, 1), (1, 3), (6, 1), (1, 2), (6, 1), (1, 1), (6, 1), (7, 1), (1, 1),
-    (6, 1), (1, 1), (6, 1), (7, 3), (1, 1), (6, 1), (1, 1), (7, 1), (1, 1), (6, 1), (1, 1), (7, 1), (6, 1),
-    (1, 1), (7, 2), (3, 1), (1, 1), (6, 1), (1, 1), (6, 12), (8, 1), (6, 1), (8, 2), (6, 4), (8, 2), (6, 1),
-    (3, 1), (8, 4), (6, 2), (8, 2), (6, 1), (8, 1), (2, 1), (8, 1), (6, 1), (8, 3), (6, 1), (8, 2), (6, 1),
-    (8, 2), (6, 1), (8, 1), (6, 1), (8, 4), (2, 1), (8, 12), (9, 3),
+    (0, 3), (1, 1), (0, 23), (4, 1), (0, 1), (1, 1), (0, 1), (1, 1), (0, 4), (5, 1), (1, 1), (5, 2), (1, 1),
+    (5, 1), (1, 1), (5, 1), (1, 1), (5, 1), (1, 1), (5, 1), (1, 1), (5, 1), (1, 1), (5, 1), (1, 1), (5, 2),
+    (1, 1), (5, 1), (1, 1), (5, 1), (1, 1), (5, 1), (1, 1), (5, 1), (1, 1), (5, 1), (1, 1), (5, 1), (1, 1),
+    (5, 1), (1, 1), (5, 5), (1, 3), (6, 1), (7, 1), (6, 1), (1, 1), (4, 1), (1, 2), (6, 1), (1, 2), (6, 1),
+    (1, 1), (6, 3), (7, 1), (6, 1), (1, 2), (6, 1), (7, 3), (1, 2), (7, 1), (1, 2), (7, 1), (1, 1), (7, 2),
+    (3, 1), (1, 2), (6, 18), (8, 1), (6, 1), (8, 1), (6, 1), (8, 1), (2, 1), (8, 1), (6, 2), (8, 1), (3, 1),
+    (6, 1), (8, 5), (6, 1), (8, 2), (6, 1), (8, 2), (6, 1), (8, 2), (6, 1), (2, 1), (8, 3), (6, 1), (8, 18),
+    (9, 3),
 )
 N_GATHER_SENDS = 70
 FEW = 16
@@ -810,7 +811,8 @@
     tok_ref, cot_ref, index_ref, small_ref = refs[:4]
     weights = refs[4:9]
     wd_ref, wo_ref, bucket_ref, col_ref, row_ref, perm_ref = refs[9:14] + refs[-1:]
-    refs = (None,) + refs[:-1]
+    *kept, keep_sems = refs[-17:-1]
+    refs = (None,) + refs[:-17]
     (rows_ref, gain_one_ref, bias_ref, first_w_ref, qkv_ref, att_ref, middle_ref, d_mid_ref, d_ref, gain_grad_ref, near_grad_ref,
      far_grad_ref, wd_grad_ref, nx_all_ref, forth_ref) = refs[15:30]
     part_ref, up_all_ref, x_all_ref, back_ref = refs[30:34]
@@ -822,6 +824,15 @@
     exchanges = refs[65:83]
     one_x, two_x, cot_x, small_x, first_x, second_x = [exchanges[i : i + 3] for i in range(0, 18, 3)]
     g_sems, one_sems, two_sems = refs[83:86], refs[86:93], refs[93:100]
+    loads = [
+        pltpu.make_async_copy(of, to, keep_sems.at[i])
+        for i, (of, to) in enumerate(zip((*weights, cot_ref, wd_ref, wo_ref), kept[:8]))
+    ]
+    start_all(loads)
+    weights, cot_ref, wd_ref, wo_ref = kept[:5], kept[5], kept[6], kept[7]
+    results = (first_w_ref, qkv_ref, att_ref, middle_ref, near_grad_ref, far_grad_ref, wd_grad_ref)
+    first_w_ref, qkv_ref, att_ref, middle_ref, near_grad_ref, far_grad_ref, wd_grad_ref = kept[8:15]
+    saves = [pltpu.make_async_copy(of, to, keep_sems.at[8 + i]) for i, (of, to) in enumerate(zip(kept[8:15], results))]
     two_bufs = (bufs[0], two_total_ref, *bufs[2:])
     count, slots, width = x_all_ref.shape
     stage = Stage(count, cuts, in_refs, out_refs, in_sems, out_sems)
@@ -886,6 +897,7 @@
         yield
 
     def cotangent():
+        loads[5].wait()
         cot_out_ref[...] = folded(cot_ref[...], index_ref[1:2, :])
         swap(spot, count, cot_out_ref, cot_in_ref, cot_x, "send")
         yield
@@ -895,6 +907,7 @@
 
     def columns(src, dst, sems, packs):
         if packs:
+            wait_all(loads[:5])
             pack(weights, first_ref, second_ref)
             yield
         for i in range(0, count, 8):
@@ -903,6 +916,8 @@
         swap(spot, count, src, dst, sems, "wait")
         if packs:
             gate_w_ref[...] = dst[:, 3 * head :]
+            saves[0].start()
+            wait_all(loads[6:])
         yield
 
     def attending(first, last):
@@ -939,6 +954,8 @@
                 yield
         if last > max(first, 1):
             wait_all(stage.store(last - 2, (part_ref,)))
+        if last > groups:
+            start_all(saves[1:3])
         yield
 
     def rows_of(rows):
@@ -952,6 +969,8 @@
             v = rows_ref[r, :].astype(jnp.float32) + branch_ref[r, :]
             middle_ref[r, :] = v
             x_ref[r, :] = (v * scale_of(v) * gain_ref[...]).astype(x_ref.dtype)
+        if rows.start + rows.size == slots:
+            saves[3].start()
         yield
 
     def norm_back_rows(rows):
@@ -998,6 +1017,8 @@
                 wd_grad_ref[...] += over(hidden, upstream, 0, 0)
                 yield
         wait_all(stage.store(last - 1, targets))
+        if last == groups:
+            start_all(saves[4:])
         yield
 
     for ref in (near_grad_ref, far_grad_ref, wd_grad_ref, gain_grad_ref):
@@ -1034,6 +1055,7 @@
             "back" + h: (["two" + h], norm_back_rows(rows)),
         }
     weave(tasks, FRONT_ORDER)
+    wait_all(saves)
     stage.finish()
 
 
@@ -1053,16 +1075,20 @@
     bf, wide, dma = jnp.bfloat16, jnp.float32, pltpu.SemaphoreType.DMA
     vmem, hbm = pl.BlockSpec(memory_space=pltpu.VMEM), pl.BlockSpec(memory_space=pl.ANY)
     shape = jax.ShapeDtypeStruct
+    qkv, attended = (slots // FEW * size + 2 * length, 3 * head), (count, slots, head)
+    kept = [pltpu.VMEM(array.shape, bf) for array in (*weights, cot, wd, wo)]
+    kept += [pltpu.VMEM(first, bf), pltpu.VMEM(qkv, bf), pltpu.VMEM(attended, bf), pltpu.VMEM(low_rows, wide)]
+    kept += [pltpu.VMEM((n, width), wide) for n in (head, second[1], units)]
     outs = pl.pallas_call(
         functools.partial(front_kernel, cuts),
         out_shape=[
             shape(low_rows, bf), shape((1, width), wide), shape(buckets.shape, wide), shape(first, bf),
-            shape((slots // FEW * size + 2 * length, 3 * head), bf), shape((count, slots, head), bf), shape(low_rows, wide),
+            shape(qkv, bf), shape(attended, bf), shape(low_rows, wide),
             shape(low_rows, wide), shape(low_rows, bf), shape((1, width), wide), shape((head, width), wide),
             shape((second[1], width), wide), shape(wd.shape, wide),
         ] + [shape(all_rows, bf)] * 6,
-        in_specs=[vmem] * 14,
-        out_specs=[vmem] * 13 + [hbm] * 6,
+        in_specs=[vmem, hbm, vmem, vmem] + [hbm] * 7 + [vmem] * 3,
+        out_specs=[vmem] * 3 + [hbm] * 4 + [vmem] * 3 + [hbm] * 9,
         scratch_shapes=[
             pltpu.VMEM(low_rows, wide), pltpu.VMEM(low_rows, bf), pltpu.VMEM(low_rows, wide), pltpu.VMEM(second, bf),
             pltpu.VMEM(low_rows, bf), pltpu.VMEM(low_rows, bf), pltpu.VMEM((1, width), wide), pltpu.VMEM((width, head), bf),
@@ -1074,7 +1100,7 @@
             dma((2, 2)), dma((2,)),
         ] + [dma((count,)), dma((count,)), dma] * 6 + [
             dma((2 + halves,)), dma((2 + halves, N_GATHER_SENDS)), dma((2 + halves, 2, 32)),
-        ] + scatter_sems(halves, 1) * 2 + [pltpu.VMEM((size, size), bf)],
+        ] + scatter_sems(halves, 1) * 2 + kept + [dma((15,)), pltpu.VMEM((size, size), bf)],
         name="front",
         compiler_params=pltpu.CompilerParams(collective_id=3, has_side_effects=True, vmem_limit_bytes=63 * 2**20),
     )(tok, cot, index, small, *weights, wd, wo, buckets, col, row)
@@ -1088,6 +1114,13 @@
     d_all_ref, part_ref = refs[25:27]
     dn_ref, down_ref, bias_grad_ref, dq_ref, dkv_ref, w_grad_ref, turned_ref, far_turned_ref = refs[27:35]
     result_ref, going_ref, came_ref, last_ref, perm_ref = refs[35:40]
+    sums_out_ref, *s_sems = refs[-14:-10]
+    refs = refs[:-14] + refs[-10:]
+    *kept, keep_sems = refs[-10:]
+    large = (att_ref, qkv_ref, w_ref, wo_ref, near_ref, far_ref, middle_ref, rows_ref, d_mid_ref)
+    loads = [pltpu.make_async_copy(of, to, keep_sems.at[i]) for i, (of, to) in enumerate(zip(large, kept))]
+    start_all(loads)
+    att_ref, qkv_ref, w_ref, wo_ref, near_ref, far_ref, middle_ref, rows_ref, d_mid_ref = kept
     bufs, other_bufs, in_refs, out_refs = refs[40:46], refs[46:52], refs[52:54], refs[54:55]
     in_sems, out_sems = refs[55:57]
     w_sems, f_sems, r_sems, t_sems, l_sems = [refs[i : i + 3] for i in range(57, 72, 3)]
@@ -1103,7 +1136,8 @@
     grain = share // folds
     perm_ref[...] = packed_order(size, length, grain)
 
-    def owners(sources, to_ref, owner_ref, sems):
+    def owners(sources, to_ref, owner_ref, sems, load):
+        load.wait()
         merged = jnp.concatenate([low(ref[...]) for ref in sources], axis=0)
         for i in range(0, width, 512):
             to_ref[i : i + 512, :] = merged[:, i : i + 512].T
@@ -1123,6 +1157,7 @@
         )
 
     def output():
+        loads[6].wait()
         rows = low(middle_ref[...] + down_ref[...])
         result_ref[...] = low(dealt_out(rows))
         swap(spot, count, result_ref, out_rows_ref, r_sems, "send")
@@ -1144,34 +1179,38 @@
         return jnp.concatenate([over(p, fold) for p in (high, rest)], axis=1)
 
     def finals():
+        wait_all(loads[7:])
         v, d, gain = rows_ref[...].astype(jnp.float32), dn_ref[...], gain_ref[...]
         scale = scale_of(v)
         w = gain * d
         mean = jnp.sum(w * v, axis=1, keepdims=True) / width
         rows = low(d_mid_ref[...] + scale * w - v * (scale * scale * scale) * mean)
-        going_ref[:, :piece] = low(dealt_out(rows))
+        going_ref[...] = low(dealt_out(rows))
+        swap(spot, count, going_ref, came_ref, t_sems, "send")
         sums = shares(jnp.sum(d * v * scale, axis=0, keepdims=True), gain_two_ref[...])
         row, lane = at(sums.shape, 0), at(sums.shape, 1)
         for b in range(BUCKETS):
             total = jnp.sum(jnp.where(bucket_ref[...] == b, bias_grad_ref[...], 0.0), axis=(0, 1), keepdims=True)
             high = low(total).astype(jnp.float32)
-            sums = sums + jnp.where((row == share * b + 1) & (lane == 0), high, 0.0)
-            sums = sums + jnp.where((row == share * b + 1) & (lane == 1), total - high, 0.0)
-        going_ref[:, piece:] = low(sums)
-        swap(spot, count, going_ref, came_ref, t_sems, "send")
-        yield
-        swap(spot, count, going_ref, came_ref, t_sems, "wait")
-        sums_ref[...] = came_ref[:, piece:]
+            sums = sums + jnp.where((row == share * b + 1) & (lane < 2), jnp.where(lane == 0, high, total - high), 0.0)
+        sums_out_ref[...] = low(sums)
+        swap(spot, count, sums_out_ref, sums_ref, s_sems, "send")
         shape, row, lane = (size, size), at((size, 1), 0), at((1, size), 1)
         turn = (index_ref[1:2, :] == row // share * grain + row % grain) & (row % share // grain == lane % share // grain)
-        last_ref[...] = low(over(marked(turn), came_ref[:, :piece]))
+        turn = marked(turn)
+        yield
+        swap(spot, count, going_ref, came_ref, t_sems, "wait")
+        last_ref[...] = low(over(turn, came_ref[...]))
         swap(spot, count, last_ref, token_rows_ref, l_sems, "send")
         yield
+        swap(spot, count, sums_out_ref, sums_ref, s_sems, "wait")
         swap(spot, count, last_ref, token_rows_ref, l_sems, "wait")
         yield
 
     def backing(first, last):
         perm = perm_ref[...]
+        if not first:
+            wait_all(loads[:4])
         for step in range(first, last):
             if step < groups:
                 start_all(stage.fetch(step, (d_all_ref,)))
@@ -1223,8 +1262,8 @@
         "d": ([], stage.gathering("d", 0, d_ref, d_all_ref, everything, g_sems)),
         "down": ([], stage.scattering("down", (forth_ref,), (down_ref,), everything, other_bufs, down_sems, 0)),
         "output": (["down"], output()),
-        "owners": ([f"back{halves - 1}"], owners((w_grad_ref, near_ref), turned_ref, owned_ref, w_sems)),
-        "far": ([], owners((far_ref,), far_turned_ref, far_owned_ref, f_sems)),
+        "owners": ([f"back{halves - 1}"], owners((w_grad_ref, near_ref), turned_ref, owned_ref, w_sems, loads[4])),
+        "far": ([], owners((far_ref,), far_turned_ref, far_owned_ref, f_sems, loads[5])),
     }
     for i, rows in enumerate(ranges):
         h = str(i)
@@ -1255,20 +1294,25 @@
             shape((head, width), wide), shape(owned, bf), shape(far, bf), shape(share, bf), shape((size, 128), bf),
             shape(share, bf),
         ] + [shape(all_rows, bf)] * 2,
-        in_specs=[vmem, hbm] + [vmem] * 9 + [hbm] + [vmem] * 7,
-        out_specs=[vmem, hbm, hbm, hbm, vmem, hbm] + [hbm] * 2,
+        in_specs=[vmem] + [hbm] * 5 + [vmem] * 3 + [hbm] * 6 + [vmem] * 4,
+        out_specs=[vmem] + [hbm] * 7,
         scratch_shapes=[
             pltpu.VMEM((rows, width), wide), pltpu.VMEM((rows, width), wide), pltpu.VMEM(bias.shape, wide),
             pltpu.VMEM((qkv.shape[0], head), bf), pltpu.VMEM((qkv.shape[0], 2 * head), wide),
             pltpu.VMEM((3 * head, width), wide), pltpu.VMEM(owned, bf), pltpu.VMEM(far, bf),
-            pltpu.VMEM(share, bf), pltpu.VMEM((size, piece + 128), bf), pltpu.VMEM((size, piece + 128), bf),
-            pltpu.VMEM(share, bf), pltpu.VMEM((size, size), bf),
+            pltpu.VMEM(share, bf), pltpu.VMEM(share, bf), pltpu.VMEM(share, bf), pltpu.VMEM(share, bf),
+            pltpu.VMEM((size, size), bf),
         ] + scatter_bufs(rows, width, 1) * 2 + [
             pltpu.VMEM((2,) + group, bf), pltpu.VMEM((2,) + group, bf), pltpu.VMEM(group, bf),
             dma((2, 2)), dma((1,)),
         ] + [dma((count,)), dma((count,)), dma] * 5 + [
             dma((1,)), dma((1, N_GATHER_SENDS)), dma((1, 2, 32)),
-        ] + scatter_sems(halves, 1) + scatter_sems(1, 1),
+        ] + scatter_sems(halves, 1) + scatter_sems(1, 1) + [
+            pltpu.VMEM((size, 128), bf), dma((count,)), dma((count,)), dma,
+        ] + [
+            pltpu.VMEM(array.shape, array.dtype)
+            for array in (attended, qkv, w, wo, near_grad, far_grad, middle, rows_low, d_mid)
+        ] + [dma((9,))],
         name="rear",
         compiler_params=pltpu.CompilerParams(collective_id=4, has_side_effects=True, vmem_limit_bytes=63 * 2**20),
     )(d_rows, normed_all, attended, qkv, w, wo, bias, col, row, near_grad, far_grad, forth, middle, rows_low, d_mid, gain,
@@ -1342,7 +1386,8 @@
     ends = jnp.cumsum(dealt_lengths)
     starts = ends - dealt_lengths
     this = jnp.arange(count, dtype=jnp.int32) == me
-    my_start, my_length = jnp.sum(jnp.where(this, starts, 0)), jnp.sum(jnp.where(this, dealt_lengths, 0))
+    my_start = jnp.sum(jnp.where(this, starts, 0), keepdims=True)
+    my_length = jnp.sum(jnp.where(this, dealt_lengths, 0), keepdims=True)
     place_in = jnp.arange(length, dtype=jnp.int32)
     slot_ids = jnp.arange(slots, dtype=jnp.int32)
     packed_ids = slot_ids // grain * length + me * grain + slot_ids % grain

time: 596 us -> 585 us (0.982)
  Pallas kernels: 561 us -> 550 us
    pallas_call x1, Pallas kernels: 223 us -> 216 us  [rear(): pl.pallas_call(functools.partial(rear_kernel, cuts), out_shape=[shape((he...]
where the time goes in v7:
time: 585 us; the launch traced here: 578 us
  Pallas kernels  550 us (94%)
  local copies, waits for them, and re-layouts  14.7 us (3%)
  other arithmetic  9.42 us (2%)
    pallas_call x1, Pallas kernels, front(): pl.pallas_call(functools.partial(front_kernel, cuts), out_shape=[shape(lo...  331 us
    pallas_call x1, Pallas kernels, rear(): pl.pallas_call(functools.partial(rear_kernel, cuts), out_shape=[shape((he...  216 us

profile of v7, /device:TPU:29, one launch (start us, length us, event | category | flops | bytes accessed | tf_op | source)
XLA Modules:
  0.0 578.1 jit_solution(12578560770085452135)
XLA Ops:
  0.7 0.7 broadcast_multiply_fusion
  1.3 0.7 gather_fusion
  2.3 0.6 and_select_fusion.3
  2.9 0.6 fusion.28
  6.1 0.7 multiply_add_fusion
  6.9 0.6 pad_add_fusion.refs_2_
  7.7 0.7 copy.35
  8.4 0.6 broadcast_in_dim.39.refs_13_.refs_8_
  9.0 0.9 fusion.1.refs_11_.refs_18_
  9.9 2.0 reshape.387.refs_0_
  11.9 1.4 fusion.20.refs_3_
  13.2 331.0 %front.1 = (bf16[80,2048]{1,0:T(8,128)(2,1)}, f32[1,2048]{1,0:T(1,128)}, f32[128,384]{1,0:T(8,128)}, bf16[2048,256]{1,0:T(8,128)(2,1)}, bf16[2816,192]{1,0:T(8,1...) custom-call(bf16[128,2048]{1,0:T(8,128)(2,1)} %reshape.387.refs_0_, ...), custom_call_target="tpu_custom_call" | custom-call | tf_op jit(solution)/shard_map/front/pallas_call | solution.py:1082
  344.8 216.1 %rear.1 = (f32[64,2048]{1,0:T(8,128)}, bf16[2048,256]{1,0:T(8,128)(2,1)}, bf16[2048,256]{1,0:T(8,128)(2,1)}, bf16[512,512]{1,0:T(8,128)(2,1)}, bf16[512,128]{1,0...) custom-call(bf16[80,2048]{1,0:T(8,128)(2,1)} %get-tuple-element.38.refs_0_, ...), custom_call_target="tpu_custom_call" | custom-call | tf_op jit(solution)/shard_map/rear/pallas_call | solution.py:1291
  560.9 0.9 bitcast_convert_fusion
  562.7 1.2 copy-done.2
  563.9 1.2 copy-done.3
  565.1 2.8 unpack_columns.1
  567.9 1.2 reshape.389
  569.4 0.7 iota_compare_fusion.4
  570.1 1.1 fusion
  571.2 1.2 reshape.390
  572.6 1.8 gather_fusion.1
  574.9 1.9 copy.44
  576.8 1.1 copy.45
  (45 shorter events, 3.6 us)
Async XLA Ops:
  0.6 0.7 copy-start
  344.8 227.6 %copy-start.5 = (s32[32]{0:T(128)S(1)}, s32[32]{0:T(128)}, u32[]{:S(2)}) copy-start(s32[32]{0:T(128)} %param.16) | copy-start | bytes 388
  344.8 233.1 %copy-start.1 = (s32[32]{0:T(128)S(1)}, s32[32]{0:T(128)}, u32[]{:S(2)}) copy-start(s32[32]{0:T(128)} %param.15) | copy-start | bytes 388
  562.7 1.2 copy-start.2
  563.9 1.2 copy-start.3
  565.1 11.7 %copy-start.4 = (f32[160,2048]{1,0:T(8,128)S(1)}, f32[160,2048]{1,0:T(8,128)}, u32[]{:S(2)}) copy-start(f32[160,2048]{1,0:T(8,128)} %get-tuple-element.98) | copy-start | bytes 3932164

commit v8 on v7

--- a/solution.py
+++ b/solution.py
@@ -1328,7 +1328,9 @@
     return dot(mask.astype(jnp.bfloat16), rows).astype(jnp.bfloat16)
 
 
-def unpack_kernel(first_ref, second_ref, query_ref, key_ref, value_ref, gate_ref, up_ref):
+def unpack_kernel(first_ref, second_ref, out_ref, down_ref, query_ref, key_ref, value_ref, gate_ref, up_ref, *same_refs):
+    for ref, same_ref in zip((out_ref, down_ref), same_refs):
+        same_ref[...] = ref[...]
     count = first_ref.shape[0]
     head = query_ref.shape[1] // count
     units = gate_ref.shape[1] // count
@@ -1341,17 +1343,28 @@
         up_ref[:, j * units : (j + 1) * units] = second_ref[j, :, units - head :].astype(wide)
 
 
-def unpack(first, second, width, hidden):
-    rows = first.shape[1]
+def unpack(first, second, out_grad, down_grad, width, hidden):
+    count, rows, _ = first.shape
+    steps = 4
     widths = (width, width, width, hidden, hidden)
+
+    def slab(array):
+        return pl.BlockSpec((array.shape[0] // steps, array.shape[1]), lambda i: (i, 0))
+
+    def deep(array):
+        return pl.BlockSpec((count, rows // steps, array.shape[2]), lambda i: (0, i, 0))
+
+    shapes = [jax.ShapeDtypeStruct((rows, columns), jnp.float32) for columns in widths]
+    shapes += [jax.ShapeDtypeStruct(array.shape, jnp.float32) for array in (out_grad, down_grad)]
     return pl.pallas_call(
         unpack_kernel,
-        out_shape=[jax.ShapeDtypeStruct((rows, columns), jnp.float32) for columns in widths],
-        in_specs=[pl.BlockSpec(memory_space=pltpu.VMEM)] * 2,
-        out_specs=[pl.BlockSpec(memory_space=pltpu.VMEM)] * 5,
+        grid=(steps,),
+        out_shape=shapes,
+        in_specs=[deep(first), deep(second), slab(out_grad), slab(down_grad)],
+        out_specs=[slab(shape) for shape in shapes],
         name="unpack_columns",
-        compiler_params=pltpu.CompilerParams(vmem_limit_bytes=32 * 2**20),
-    )(first, second)
+        compiler_params=pltpu.CompilerParams(vmem_limit_bytes=63 * 2**20),
+    )(first, second, out_grad, down_grad)
 
 
 def body(
@@ -1448,8 +1461,8 @@
     ids = jnp.arange(count, dtype=jnp.int32)
     dealt_slot = jnp.sum(jnp.where(permutation[None, :] == ids[:, None], ids[None, :], 0), axis=1)
     tokens_grad = whole_rows(token_rows)[dealt_slot]
-    query_grad, key_grad, value_grad, gate_grad, up_grad = unpack(
-        first_grad, second_grad, width, hidden_width * count
+    query_grad, key_grad, value_grad, gate_grad, up_grad, out_grad, down_grad = unpack(
+        first_grad, second_grad, out_grad, down_grad, width, hidden_width * count
     )
     return (
         layer_output,

time: 585 us -> 582 us (level)
  no operation moved by 1% of the time
where the time goes in v8:
time: 582 us; the launch traced here: 575 us
  Pallas kernels  552 us (95%)
  other arithmetic  9.42 us (2%)
  local copies, waits for them, and re-layouts  9.27 us (2%)
    pallas_call x1, Pallas kernels, front(): pl.pallas_call(functools.partial(front_kernel, cuts), out_shape=[shape(lo...  331 us
    pallas_call x1, Pallas kernels, rear(): pl.pallas_call(functools.partial(rear_kernel, cuts), out_shape=[shape((he...  216 us

profile of v8, /device:TPU:29, one launch (start us, length us, event | category | flops | bytes accessed | tf_op | source)
XLA Modules:
  0.0 575.2 jit_solution(7879574497223707654)
XLA Ops:
  0.7 0.7 broadcast_multiply_fusion
  1.3 0.7 gather_fusion
  2.3 0.6 and_select_fusion.3
  2.9 0.6 fusion.28
  6.1 0.7 multiply_add_fusion
  6.9 0.6 pad_add_fusion.refs_2_
  7.7 0.7 copy.35
  8.4 0.6 broadcast_in_dim.39.refs_13_.refs_8_
  9.0 0.9 fusion.1.refs_11_.refs_18_
  9.9 2.0 reshape.387.refs_0_
  11.9 1.4 fusion.20.refs_3_
  13.2 331.0 %front.1 = (bf16[80,2048]{1,0:T(8,128)(2,1)}, f32[1,2048]{1,0:T(1,128)}, f32[128,384]{1,0:T(8,128)}, bf16[2048,256]{1,0:T(8,128)(2,1)}, bf16[2816,192]{1,0:T(8,1...) custom-call(bf16[128,2048]{1,0:T(8,128)(2,1)} %reshape.387.refs_0_, ...), custom_call_target="tpu_custom_call" | custom-call | tf_op jit(solution)/shard_map/front/pallas_call | solution.py:1082
  344.2 0.6 pad_add_fusion.1.refs_17_
  344.8 216.1 %rear.1 = (f32[64,2048]{1,0:T(8,128)}, bf16[2048,256]{1,0:T(8,128)(2,1)}, bf16[2048,256]{1,0:T(8,128)(2,1)}, bf16[512,512]{1,0:T(8,128)(2,1)}, bf16[512,128]{1,0...) custom-call(bf16[80,2048]{1,0:T(8,128)(2,1)} %get-tuple-element.40.refs_0_, ...), custom_call_target="tpu_custom_call" | custom-call | tf_op jit(solution)/shard_map/rear/pallas_call | solution.py:1291
  560.9 0.9 bitcast_convert_fusion
  562.1 0.5 add_bitcast_fusion
  562.7 5.3 unpack_columns.1
  567.9 1.2 reshape.389
  569.1 0.2 copy.36
  569.5 0.7 iota_compare_fusion.4
  570.1 1.1 fusion
  571.3 1.2 reshape.390
  572.6 1.8 gather_fusion.1
  574.4 0.6 fusion.32
  (37 shorter events, 1.6 us)
Async XLA Ops:
  0.6 0.7 copy-start
  344.8 227.7 %copy-start.2 = (s32[32]{0:T(128)S(1)}, s32[32]{0:T(128)}, u32[]{:S(2)}) copy-start(s32[32]{0:T(128)} %param.16) | copy-start | bytes 388
  344.8 230.2 %copy-start.1 = (s32[32]{0:T(128)S(1)}, s32[32]{0:T(128)}, u32[]{:S(2)}) copy-start(s32[32]{0:T(128)} %param.15) | copy-start | bytes 388
